TPU v7x, 256 devices: a whole 4x4x8 slice. The times are simulated.
256 devices in a mesh: row: 16 (over y, x_hi, core), col: 16 (over x_lo, z).
Axes of the slice: x: 4 (x_hi: 2, x_lo: 2; x = x_hi * 2 + x_lo), y: 4, z: 8, core: 2. Of those that a mesh axis runs over, the one named last changes fastest.
Arguments:
- object_field: float32 [2, 4096, 4096], P(None, 'row', 'col'), may hold values from -3 to 4
- probe_modes: float32 [2, 4, 128, 128], replicated, may hold values from -3 to 3
- scan_offsets: int32 [16, 16, 16, 2], P('row', 'col'), may hold values from 0 to 255
- measured: float32 [16, 16, 16, 128, 128], P('row', 'col'), may hold values from 0 to 24
Outputs:
- object_out: float32 [2, 4096, 4096], P(None, 'row', 'col')
- probe_out: float32 [2, 4, 128, 128], replicated
All inputs are finite; a program needn't handle non-finite values.
Results may differ from a plain program's by a relative error of at most 0.003.
The roundings to bfloat16 on the way count: a program that leaves them out, or rounds other values in their place, can miss the bound.
Values sent between devices are 32-bit elements; how exact they have to be, the bound alone decides.
No kernel may reach another device: no remote copies, remote signals or barrier semaphores. Data moves between devices by JAX's collectives and lax.ppermute only.
A program may use at most 64 MiB of HBM per device.

v0:
```python
import jax
import jax.numpy as jnp
from jax import lax
from jax.sharding import PartitionSpec as P

ITERS = 2


def padded_2(cells, sides, width):
    for axis, dim in sides:
        count = lax.axis_size(axis)
        ends = count - 1
        head = lax.slice_in_dim(cells, 0, width, axis=dim)
        tail = lax.slice_in_dim(cells, cells.shape[dim] - width, cells.shape[dim], axis=dim)
        cells = jnp.concatenate(
            [
                lax.ppermute(tail, axis, [(i, (i + 1) % count) for i in range(ends)]),
                cells,
                lax.ppermute(head, axis, [((i + 1) % count, i) for i in range(ends)]),
            ],
            axis=dim,
        )
    return cells


def dft_tables(patch_len, inverse):
    indices = jnp.arange(patch_len, dtype=jnp.int32)
    phases = indices[:, None] * indices[None, :] % patch_len
    radians = phases.astype(jnp.float32) * (2.0 * jnp.pi / patch_len)
    factor = 1.0 / jnp.sqrt(jnp.float32(patch_len))
    cosine = jnp.cos(radians) * factor
    sine_part = jnp.sin(radians) * factor
    imag_part = sine_part if inverse else -sine_part
    left_table = jnp.concatenate(
        [jnp.concatenate([cosine, -imag_part], 1), jnp.concatenate([imag_part, cosine], 1)], 0
    )
    right_table = jnp.concatenate([cosine, imag_part], 1)
    return (left_table.astype(jnp.bfloat16), right_table.astype(jnp.bfloat16))


def transform(field_low, tables, patch_len):
    stacked = field_low.reshape(field_low.shape[:-3] + (2 * patch_len, patch_len))
    sectioned = jnp.einsum(
        "ij,bmjk->bmik", tables[0], stacked, preferred_element_type=jnp.float32
    ).astype(jnp.bfloat16)
    product = jnp.einsum("bmij,jk->bmik", sectioned, tables[1], preferred_element_type=jnp.float32)
    upper_half = product[:, :, :patch_len, :]
    lower_half = product[:, :, patch_len:, :]
    real_out = upper_half[..., :patch_len] - lower_half[..., patch_len:]
    imag_out = upper_half[..., patch_len:] + lower_half[..., :patch_len]
    return (real_out, imag_out)


def wave_terms(windows, probes, amplitude, forward, backward, patch_len):
    probe_re = probes[0][None]
    probe_im = probes[1][None]
    window_re = windows[:, 0][:, None]
    window_im = windows[:, 1][:, None]
    exit_re = probe_re * window_re - probe_im * window_im
    exit_im = probe_re * window_im + probe_im * window_re
    exit_wave = jnp.stack([exit_re, exit_im], axis=2).astype(jnp.bfloat16)
    far_re, far_im = transform(exit_wave, forward, patch_len)
    intensity = jnp.sum(far_re * far_re + far_im * far_im, axis=1)
    scaling = (amplitude / jnp.sqrt(intensity + 1.0))[:, None]
    corrected = jnp.stack([far_re * scaling, far_im * scaling], axis=2).astype(jnp.bfloat16)
    back_re, back_im = transform(corrected, backward, patch_len)
    diff_re = back_re - exit_re
    diff_im = back_im - exit_im
    object_re = jnp.sum(probe_re * diff_re + probe_im * diff_im, axis=1)
    object_im = jnp.sum(probe_re * diff_im - probe_im * diff_re, axis=1)
    grad_re = jnp.sum(window_re * diff_re + window_im * diff_im, axis=0)
    grad_im = jnp.sum(window_re * diff_im - window_im * diff_re, axis=0)
    density = jnp.sum(windows[:, 0] * windows[:, 0] + windows[:, 1] * windows[:, 1], axis=0)
    return (object_re, object_im, jnp.stack([grad_re, grad_im]), density)


def local_terms(padded, probes, row_blocks, col_blocks, amplitudes, forward, backward, patch_len):
    lighting = jnp.sum(probes[0] * probes[0] + probes[1] * probes[1], axis=0)
    extent = padded.shape[1]
    zero_index = jnp.zeros((), jnp.int32)

    def cut_window(row_start, col_start):
        return lax.dynamic_slice(
            padded, (zero_index, row_start, col_start), (2, patch_len, patch_len)
        )

    def visit(running, element):
        placed, probe_grad, density = running
        row_group, col_group, amplitude = element
        windows = jax.vmap(cut_window)(row_group, col_group)
        object_re, object_im, grad_part, density_part = wave_terms(
            windows, probes, amplitude, forward, backward, patch_len
        )
        for slot in range(row_group.shape[0]):
            start = (zero_index, row_group[slot], col_group[slot])
            contrib = jnp.stack([object_re[slot], object_im[slot], lighting])
            region = lax.dynamic_slice(placed, start, (3, patch_len, patch_len))
            placed = lax.dynamic_update_slice(placed, region + contrib, start)
        return ((placed, probe_grad + grad_part, density + density_part), None)

    initial = (
        jnp.zeros((3, extent, extent), jnp.float32),
        jnp.zeros(probes.shape, jnp.float32),
        jnp.zeros((patch_len, patch_len), jnp.float32),
    )
    summed, _ = lax.scan(visit, initial, (row_blocks, col_blocks, amplitudes))
    return summed


def fold_rims(extended, length, band, offset, axis_dim):
    center = lax.slice_in_dim(extended, offset, offset + length, axis=axis_dim)
    lower_rim = lax.slice_in_dim(extended, 0, length, axis=axis_dim)
    upper_rim = lax.slice_in_dim(extended, 2 * offset, 2 * offset + length, axis=axis_dim)
    position = lax.broadcasted_iota(jnp.int32, center.shape, axis_dim)
    center = center + jnp.where(position < band, lower_rim, 0.0)
    return center + jnp.where(position >= length - band, upper_rim, 0.0)


def light_peak(value):
    return lax.pmax(value, ("row", "col"))


def body(object_field, probe_modes, scan_offsets, measured):
    patch_len = probe_modes.shape[-1]
    half_len = patch_len // 2
    tile_len = object_field.shape[1]
    positions = scan_offsets.shape[2]
    offsets = scan_offsets.reshape(positions, 2)
    row_blocks = offsets[:, 0].reshape(positions // 2, 2)
    col_blocks = offsets[:, 1].reshape(positions // 2, 2)
    amplitudes = measured.reshape(positions // 2, 2, patch_len, patch_len)
    forward = dft_tables(patch_len, False)
    backward = dft_tables(patch_len, True)
    probes = probe_modes
    current = object_field
    for sweep in range(ITERS):
        padded = padded_2(current, (("row", 1), ("col", 2)), half_len)
        placed, probe_grad, density = local_terms(
            padded, probes, row_blocks, col_blocks, amplitudes, forward, backward, patch_len
        )
        extended = padded_2(placed, (("row", 1), ("col", 2)), half_len)
        combined = fold_rims(
            fold_rims(extended, tile_len, half_len, patch_len, 1), tile_len, half_len, patch_len, 2
        )
        light_top = jnp.max(combined[2])
        light_max = light_peak(light_top)
        total_grad, total_density = lax.psum((probe_grad, density), ("row", "col"))
        probes = probes + total_grad / (total_density + 0.1 * jnp.max(total_density))
        current = current + combined[:2] / (combined[2] + 0.1 * light_max)
    return (current, probes)


def solution(mesh):
    return jax.shard_map(
        body,
        mesh=mesh,
        in_specs=(
            P(None, "row", "col"),
            P(),
            P("row", "col", None, None),
            P("row", "col", None, None, None),
        ),
        out_specs=(P(None, "row", "col"), P()),
        check_vma=False,
    )
```

profile of v0, /device:TPU:1, one launch (start us, length us, event | category | flops | bytes accessed | tf_op | source)
XLA Modules:
  0.0 1330.3 jit_solution(6883029534309862511)
XLA Ops:
  8.2 5.1 collective-permute-start.1
  20.3 3.6 collective-permute-start.2
  27.4 3.7 collective-permute-done.2
  31.1 4.1 collective-permute-done.3
  38.0 281.7 %while.37 = (s32[]{:T(128)}, f32[3,384,384]{2,1,0:T(8,128)}, f32[2,4,128,128]{3,2,1,0:T(8,128)}, f32[128,128]{1,0:T(8,128)S(1)}, s32[8,2]{1,0:T(8,128)S(1)}, /*i...) while((s32[]{:T(128)}, f32[3,384,384]{2,1,0:T(8,128)}, ...), condition=%wide.region_8.9_spmd.clone, body=%wide.region_1.8_spmd.clone.sunk | while | flops 545406976 | bytes 37880656 | solution.py:106
  47.5 6.2 while.40
  63.9 4.2 dynamic_update_slice.20
  69.3 3.8 dynamic_update_slice.21
  82.6 6.2 while.40
  99.0 4.2 dynamic_update_slice.20
  104.4 3.9 dynamic_update_slice.21
  117.8 6.2 while.40
  134.2 4.3 dynamic_update_slice.20
  139.6 4.0 dynamic_update_slice.21
  153.2 6.2 while.40
  169.6 4.2 dynamic_update_slice.20
  174.9 4.1 dynamic_update_slice.21
  188.5 6.2 while.40
  204.9 4.2 dynamic_update_slice.20
  210.3 3.9 dynamic_update_slice.21
  223.8 6.2 while.40
  240.2 4.2 dynamic_update_slice.20
  245.6 3.7 dynamic_update_slice.21
  258.8 6.2 while.40
  275.2 4.2 dynamic_update_slice.20
  280.6 3.9 dynamic_update_slice.21
  294.0 6.2 while.40
  310.4 4.3 dynamic_update_slice.20
  315.8 3.9 dynamic_update_slice.21
  320.9 7.5 collective-permute-start.4
  332.8 5.1 collective-permute-done.5
  345.9 251.0 %all-reduce.7.cloned.1.call-done = (f32[2,4,128,128]{3,2,1,0:T(8,128)}, f32[128,128]{1,0:T(8,128)}) async-done(((f32[2,4,128,128]{3,2,1,0:T(8,128)}, f32[128,128]{1,0:T(8,128)}), (f32[2,4,128,128]{3,2,1,0:T(8,128)}, f32[128,128]{1,0:T(8,128)})) %all-reduce.7.cloned.1.call-update) | async-done | bytes 589840 | tf_op jit(solution)/shard_map/psum | solution.py:147
  602.1 75.5 %pmax.14 = f32[]{:T(128)} all-reduce(f32[]{:T(128)} %slice_reduce_fusion.1), channel_id=1, replica_groups=mesh['row'=16,'col'=16] {'row','col'}, use_global_device_ids=true, to_apply=%region_10.11 | all-reduce | flops 1 | bytes 8 | tf_op jit(solution)/shard_map/pmax | solution.py:120
  678.5 3.8 collective-permute-start.8
  685.6 5.9 collective-permute-done.9
  697.0 3.8 collective-permute-done.11
  703.9 274.7 %while.39 = (s32[]{:T(128)}, f32[3,384,384]{2,1,0:T(8,128)}, f32[2,4,128,128]{3,2,1,0:T(8,128)}, f32[128,128]{1,0:T(8,128)S(1)}, s32[8,2]{1,0:T(8,128)S(1)}, /*i...) while((s32[]{:T(128)}, f32[3,384,384]{2,1,0:T(8,128)}, ...), condition=%wide.region_22.23_spmd.clone, body=%wide.region_15.22_spmd.clone.sunk | while | flops 545406976 | bytes 39977828 | solution.py:106
  712.4 5.8 while.41
  728.9 4.2 dynamic_update_slice.22
  734.3 3.8 dynamic_update_slice.23
  746.6 5.8 while.41
  763.1 4.2 dynamic_update_slice.22
  768.5 3.9 dynamic_update_slice.23
  780.9 5.8 while.41
  797.4 4.3 dynamic_update_slice.22
  802.9 4.0 dynamic_update_slice.23
  815.4 5.8 while.41
  831.9 4.2 dynamic_update_slice.22
  837.3 4.1 dynamic_update_slice.23
  849.8 5.8 while.41
  866.4 4.2 dynamic_update_slice.22
  871.8 3.9 dynamic_update_slice.23
  884.2 5.8 while.41
  900.8 4.2 dynamic_update_slice.22
  906.2 3.7 dynamic_update_slice.23
  918.4 5.8 while.41
  934.9 4.2 dynamic_update_slice.22
  940.3 3.9 dynamic_update_slice.23
  952.7 5.8 while.41
  969.3 4.3 dynamic_update_slice.22
  974.7 3.9 dynamic_update_slice.23
  988.6 6.4 collective-permute-done.13
  1001.8 237.3 %all-reduce.5.cloned.1.call-done = (f32[2,4,128,128]{3,2,1,0:T(8,128)}, f32[128,128]{1,0:T(8,128)}) async-done(((f32[2,4,128,128]{3,2,1,0:T(8,128)}, f32[128,128]{1,0:T(8,128)}), (f32[2,4,128,128]{3,2,1,0:T(8,128)}, f32[128,128]{1,0:T(8,128)})) %all-reduce.5.cloned.1.call-update) | async-done | bytes 589840 | tf_op jit(solution)/shard_map/psum | solution.py:147
  1246.2 75.4 %pmax.15 = f32[]{:T(128)} all-reduce(f32[]{:T(128)} %slice_reduce_fusion), channel_id=1, replica_groups=mesh['row'=16,'col'=16] {'row','col'}, use_global_device_ids=true, to_apply=%region_24.25 | all-reduce | flops 1 | bytes 8 | tf_op jit(solution)/shard_map/pmax | solution.py:120
  (904 shorter events, 368.2 us)
Async XLA Ops:
  7.2 589.8 %all-reduce.7.cloned.1.call-start = ((), (), s32[]{:S(2)}) async-start(), calls=%async_computation.1 | async-start | bytes 1179648 | tf_op jit(solution)/shard_map/psum | solution.py:147
  8.2 11.9 collective-permute-start.1
  13.4 5.5 collective-permute-start
  20.3 10.8 collective-permute-start.2
  23.8 11.3 collective-permute-start.3
  62.5 10.6 copy-start.3
  62.5 10.6 copy-start.15
  97.5 10.7 copy-start.3
  97.6 10.7 copy-start.15
  132.7 10.9 copy-start.3
  132.7 10.9 copy-start.15
  168.1 10.9 copy-start.3
  168.1 10.9 copy-start.15
  203.4 10.8 copy-start.3
  203.4 10.8 copy-start.15
  238.7 10.6 copy-start.3
  238.7 10.6 copy-start.15
  273.7 10.8 copy-start.3
  273.7 10.7 copy-start.15
  308.9 10.8 copy-start.3
  308.9 10.8 copy-start.15
  320.9 11.7 collective-permute-start.4
  328.4 9.5 collective-permute-start.5
  339.2 259.2 %collective-permute-start.6 = (f32[3,512,64]{1,2,0:T(8,128)}, f32[3,512,64]{1,2,0:T(8,128)}, u32[]{:S(2)}, u32[]{:S(2)}) collective-permute-start(f32[3,512,64]{1,2,0:T(8,128)} %get-tuple-element.468), channel_id=1, source_target_pairs={{0,1},{1,2},{2,3},{3,4},{4,5},{5,6},{6,7},{7,8},{8,9},{9,10},{10,1... | collective-permute-start | bytes 1179656 | tf_op jit(solution)/shard_map/ppermute | solution.py:17
  342.3 256.1 %collective-permute-start.7 = (f32[3,512,64]{1,2,0:T(8,128)S(1)}, f32[3,512,64]{1,2,0:T(8,128)}, u32[]{:S(2)}, u32[]{:S(2)}) collective-permute-start(f32[3,512,64]{1,2,0:T(8,128)S(1)} %get-tuple-element.469), channel_id=1, source_target_pairs={{1,0},{2,1},{3,2},{4,3},{5,4},{6,5},{7,6},{8,7},{9,8},{10,9},{11,1... | collective-permute-start | bytes 1179656 | tf_op jit(solution)/shard_map/ppermute | solution.py:19
  343.6 895.4 %all-reduce.5.cloned.1.call-start = ((), (), s32[]{:S(2)}) async-start(), calls=%async_computation | async-start | bytes 1179648 | tf_op jit(solution)/shard_map/psum | solution.py:147
  600.6 77.7 %copy-start.17 = (f32[2,256,256]{1,2,0:T(8,128)S(1)}, f32[2,256,256]{1,2,0:T(8,128)}, u32[]{:S(2)}) copy-start(f32[2,256,256]{1,2,0:T(8,128)} %copy.68) | copy-start | bytes 1572868
  601.5 82.7 %copy-start.20 = (f32[128,128]{1,0:T(8,128)S(1)}, f32[128,128]{1,0:T(8,128)}, u32[]{:S(2)}) copy-start(f32[128,128]{1,0:T(8,128)} %get-tuple-element.417) | copy-start | bytes 196612
  678.3 22.5 %copy-start.9 = (f32[2,256,256]{1,2,0:T(8,128)}, f32[2,256,256]{1,2,0:T(8,128)S(1)}, u32[]{:S(2)}) copy-start(f32[2,256,256]{1,2,0:T(8,128)S(1)} %fusion.41) | copy-start | bytes 1572868
  678.3 17.4 %copy-start.4 = (f32[2,4,128,128]{3,2,1,0:T(8,128)S(1)}, f32[2,4,128,128]{3,2,1,0:T(8,128)}, u32[]{:S(2)}) copy-start(f32[2,4,128,128]{3,2,1,0:T(8,128)} %param.9) | copy-start | bytes 1572868
  678.3 17.4 %copy-start.18 = (f32[2,4,128,128]{3,2,1,0:T(8,128)S(1)}, f32[2,4,128,128]{3,2,1,0:T(8,128)}, u32[]{:S(2)}) copy-start(f32[2,4,128,128]{3,2,1,0:T(8,128)} %get-tuple-element.416) | copy-start | bytes 1572868
  678.5 7.1 collective-permute-start.8
  682.3 9.2 collective-permute-start.9
  691.7 5.3 collective-permute-start.10
  694.4 6.4 collective-permute-start.11
  703.9 15.2 %copy-start = (f32[2,4,128,128]{3,2,1,0:T(8,128)}, f32[2,4,128,128]{3,2,1,0:T(8,128)S(1)}, u32[]{:S(2)}) copy-start(f32[2,4,128,128]{3,2,1,0:T(8,128)S(1)} %get-tuple-element.964) | copy-start | bytes 1572868 | tf_op jit(solution)/shard_map/while
  727.5 10.6 copy-start.1
  727.5 10.6 copy-start.12
  738.1 15.2 %copy-start = (f32[2,4,128,128]{3,2,1,0:T(8,128)}, f32[2,4,128,128]{3,2,1,0:T(8,128)S(1)}, u32[]{:S(2)}) copy-start(f32[2,4,128,128]{3,2,1,0:T(8,128)S(1)} %get-tuple-element.964) | copy-start | bytes 1572868 | tf_op jit(solution)/shard_map/while
  761.7 10.7 copy-start.1
  761.7 10.7 copy-start.12
  772.4 15.2 %copy-start = (f32[2,4,128,128]{3,2,1,0:T(8,128)}, f32[2,4,128,128]{3,2,1,0:T(8,128)S(1)}, u32[]{:S(2)}) copy-start(f32[2,4,128,128]{3,2,1,0:T(8,128)S(1)} %get-tuple-element.964) | copy-start | bytes 1572868 | tf_op jit(solution)/shard_map/while
  796.0 10.9 copy-start.1
  796.0 10.9 copy-start.12
  806.9 15.2 %copy-start = (f32[2,4,128,128]{3,2,1,0:T(8,128)}, f32[2,4,128,128]{3,2,1,0:T(8,128)S(1)}, u32[]{:S(2)}) copy-start(f32[2,4,128,128]{3,2,1,0:T(8,128)S(1)} %get-tuple-element.964) | copy-start | bytes 1572868 | tf_op jit(solution)/shard_map/while
  830.5 10.9 copy-start.1
  830.5 10.9 copy-start.12
  841.4 15.2 %copy-start = (f32[2,4,128,128]{3,2,1,0:T(8,128)}, f32[2,4,128,128]{3,2,1,0:T(8,128)S(1)}, u32[]{:S(2)}) copy-start(f32[2,4,128,128]{3,2,1,0:T(8,128)S(1)} %get-tuple-element.964) | copy-start | bytes 1572868 | tf_op jit(solution)/shard_map/while
  864.9 10.8 copy-start.1
  864.9 10.8 copy-start.12
  875.8 15.2 %copy-start = (f32[2,4,128,128]{3,2,1,0:T(8,128)}, f32[2,4,128,128]{3,2,1,0:T(8,128)S(1)}, u32[]{:S(2)}) copy-start(f32[2,4,128,128]{3,2,1,0:T(8,128)S(1)} %get-tuple-element.964) | copy-start | bytes 1572868 | tf_op jit(solution)/shard_map/while
  899.3 10.6 copy-start.1
  899.3 10.6 copy-start.12
  909.9 15.2 %copy-start = (f32[2,4,128,128]{3,2,1,0:T(8,128)}, f32[2,4,128,128]{3,2,1,0:T(8,128)S(1)}, u32[]{:S(2)}) copy-start(f32[2,4,128,128]{3,2,1,0:T(8,128)S(1)} %get-tuple-element.964) | copy-start | bytes 1572868 | tf_op jit(solution)/shard_map/while
  933.5 10.8 copy-start.1
  933.5 10.7 copy-start.12
  944.2 15.2 %copy-start = (f32[2,4,128,128]{3,2,1,0:T(8,128)}, f32[2,4,128,128]{3,2,1,0:T(8,128)S(1)}, u32[]{:S(2)}) copy-start(f32[2,4,128,128]{3,2,1,0:T(8,128)S(1)} %get-tuple-element.964) | copy-start | bytes 1572868 | tf_op jit(solution)/shard_map/while
  967.8 10.8 copy-start.1
  967.8 10.8 copy-start.12
  980.4 7.9 collective-permute-start.12
  983.9 11.1 collective-permute-start.13
  997.4 244.7 %collective-permute-start.14 = (f32[3,512,64]{1,2,0:T(8,128)}, f32[3,512,64]{1,2,0:T(8,128)}, u32[]{:S(2)}, u32[]{:S(2)}) collective-permute-start(f32[3,512,64]{1,2,0:T(8,128)} %get-tuple-element.466), channel_id=1, source_target_pairs={{0,1},{1,2},{2,3},{3,4},{4,5},{5,6},{6,7},{7,8},{8,9},{9,10},{10,1... | collective-permute-start | bytes 1179656 | tf_op jit(solution)/shard_map/ppermute | solution.py:17
  1000.5 241.6 %collective-permute-start.15 = (f32[3,512,64]{1,2,0:T(8,128)}, f32[3,512,64]{1,2,0:T(8,128)}, u32[]{:S(2)}, u32[]{:S(2)}) collective-permute-start(f32[3,512,64]{1,2,0:T(8,128)} %get-tuple-element.467), channel_id=1, source_target_pairs={{1,0},{2,1},{3,2},{4,3},{5,4},{6,5},{7,6},{8,7},{9,8},{10,9},{11,1... | collective-permute-start | bytes 1179656 | tf_op jit(solution)/shard_map/ppermute | solution.py:19
  1244.5 77.8 %copy-start.10 = (f32[2,256,256]{1,2,0:T(8,128)S(1)}, f32[2,256,256]{1,2,0:T(8,128)}, u32[]{:S(2)}) copy-start(f32[2,256,256]{1,2,0:T(8,128)} %copy-done.9) | copy-start | bytes 1572868
  (52 other events, 220.5 us)
Sparse Core Ops, SparseCore 0:
  343.8 253.1 all-reduce.6
  988.5 250.5 all-reduce.4
where the time goes:
time: 1340 us; the launch traced here: 1330 us
  waiting for transfers between devices  519 us (39%)
  local copies, waits for them, and re-layouts  286 us (21%)
  blocking collectives  151 us (11%)
  loops' own time  127 us (9%)
  other arithmetic  126 us (9%)
  matrix products  57.2 us (4%)
  starting transfers between devices  46.6 us (3%)
  between operations  17.1 us (1%)
    psum x2, waiting for transfers between devices, body(): total_grad, total_density = lax.psum((probe_grad, density), ('row', 'col'))  488 us
    pmax x2, blocking collectives, light_peak(): return lax.pmax(value, ('row', 'col'))  151 us
    dynamic_update_slice x32, local copies, waits for them, and re-layouts, visit(): placed = lax.dynamic_update_slice(placed, region + contrib, start)  130 us
    another operation x2, loops' own time, local_terms(): summed, _ = lax.scan(visit, initial, (row_blocks, col_blocks, amplitudes))  126 us
    gather x96, local copies, waits for them, and re-layouts  95.1 us
    dot_general x32, matrix products, transform(): jnp.einsum('bmij,jk->bmik', sectioned, tables[1], preferred_element_type=...  57.2 us
    add x32, other arithmetic, visit(): placed = lax.dynamic_update_slice(placed, region + contrib, start)  38.4 us
    ppermute x8, starting transfers between devices, padded_2(): lax.ppermute(tail, axis, [(i, (i + 1) % count) for i in range(ends)])  30.1 us
  transfers between devices with their start and end apart: 18, of which 10 were waited for; matrix products, arithmetic and copies ran while one was open for 2% of the time, Pallas kernels for 0%

commit v1 on v0

v1 whole, which is shorter than its diff:
```python
import functools

import jax
import jax.numpy as jnp
import numpy as np
from jax import lax
from jax.experimental import pallas as pl
from jax.experimental.pallas import tpu as pltpu
from jax.sharding import PartitionSpec as P

ITERS = 2
BATCH = 2


def dft_pair(n):
    index = np.arange(n)
    angle = (index[:, None] * index[None, :] % n) * (2.0 * np.pi / n)
    c = np.cos(angle) / np.sqrt(n)
    s = np.sin(angle) / np.sqrt(n)
    forward = np.block([[c, s], [-s, c]])
    backward = np.block([[c, -s], [s, c]])
    return jnp.asarray(forward, jnp.bfloat16), jnp.asarray(backward, jnp.bfloat16)


def spot(off_ref, q, n):
    u = off_ref[q, 0]
    v = off_ref[q, 1]
    return u, v // n, lax.rem(v, n)


def place(canvas, ch, where, lane, value):
    u, k, s = where
    n = value.shape[0]
    rolled = pltpu.roll(value, s, 1)
    canvas[ch, k, pl.ds(u, n), :] += jnp.where(lane >= s, rolled, 0.0)
    canvas[ch, k + 1, pl.ds(u, n), :] += jnp.where(lane >= s, 0.0, rolled)


def light_kernel(off_ref, probe_ref, placed_ref, canvas):
    n = probe_ref.shape[2]
    lane = lax.broadcasted_iota(jnp.int32, (n, n), 1)
    light = jnp.sum(probe_ref[0] * probe_ref[0] + probe_ref[1] * probe_ref[1], axis=0)
    canvas[...] = jnp.zeros_like(canvas)

    def step(q, carry):
        place(canvas, 0, spot(off_ref, q, n), lane, light)
        return carry

    lax.fori_loop(0, off_ref.shape[0], step, 0)
    for k in range(canvas.shape[1]):
        placed_ref[:, k * n : (k + 1) * n] = canvas[0, k]


def sweep_kernel(
    off_ref, obj_ref, probe_ref, meas_ref, fwd_ref, bwd_ref, placed_ref, grad_ref, cells, canvas
):
    modes = probe_ref.shape[1]
    n = probe_ref.shape[2]
    blocks = cells.shape[1]
    for k in range(blocks):
        cells[:, k] = obj_ref[:, :, k * n : (k + 1) * n]
    canvas[...] = jnp.zeros_like(canvas)
    grad_ref[...] = jnp.zeros_like(grad_ref)
    lane = lax.broadcasted_iota(jnp.int32, (n, n), 1)

    def window(ch, where):
        u, k, s = where
        left = cells[ch, k, pl.ds(u, n), :]
        right = cells[ch, k + 1, pl.ds(u, n), :]
        return pltpu.roll(jnp.where(lane >= s, left, right), n - s, 1)

    def transform(field, left, right):
        sec = jnp.dot(left, field, preferred_element_type=jnp.float32).astype(jnp.bfloat16)
        parts = [slice(m * n, (m + 1) * n) for m in range(modes)]
        rows = [jnp.concatenate([sec[:n, part], sec[n:, part]], 1) for part in parts]
        return jnp.dot(jnp.concatenate(rows, 0), right, preferred_element_type=jnp.float32)

    def paired(re_parts, im_parts):
        re_all = jnp.concatenate([x.astype(jnp.bfloat16) for x in re_parts], 1)
        im_all = jnp.concatenate([x.astype(jnp.bfloat16) for x in im_parts], 1)
        return jnp.concatenate([re_all, im_all], 0)

    def split(wave):
        return [(wave[m * n : (m + 1) * n, :n], wave[m * n : (m + 1) * n, n:]) for m in range(modes)]

    def step(i, carry):
        probes = [(probe_ref[0, m], probe_ref[1, m]) for m in range(modes)]
        spots = [spot(off_ref, i * BATCH + j, n) for j in range(BATCH)]
        wins = [(window(0, where), window(1, where)) for where in spots]
        exits = []
        for w_re, w_im in wins:
            re_parts = [p_re * w_re - p_im * w_im for p_re, p_im in probes]
            im_parts = [p_re * w_im + p_im * w_re for p_re, p_im in probes]
            exits.append(paired(re_parts, im_parts))
        fars = [split(transform(x, fwd_ref[...], bwd_ref[...])) for x in exits]
        corrected = []
        for j, far in enumerate(fars):
            power = functools.reduce(jnp.add, [re * re + im * im for re, im in far])
            scale = meas_ref[i * BATCH + j] / jnp.sqrt(power + 1.0)
            corrected.append(paired([re * scale for re, _ in far], [im * scale for _, im in far]))
        backs = [split(transform(x, bwd_ref[...], fwd_ref[...])) for x in corrected]
        for where, back in zip(spots, backs):
            terms_re = [p[0] * b[0] + p[1] * b[1] for p, b in zip(probes, back)]
            terms_im = [p[0] * b[1] - p[1] * b[0] for p, b in zip(probes, back)]
            place(canvas, 0, where, lane, functools.reduce(jnp.add, terms_re))
            place(canvas, 1, where, lane, functools.reduce(jnp.add, terms_im))
        for m in range(modes):
            pairs = [(w, back[m]) for w, back in zip(wins, backs)]
            grad_ref[m] += functools.reduce(jnp.add, [w[0] * b[0] + w[1] * b[1] for w, b in pairs])
            grad_ref[modes + m] += functools.reduce(
                jnp.add, [w[0] * b[1] - w[1] * b[0] for w, b in pairs]
            )
        grad_ref[2 * modes] += functools.reduce(jnp.add, [w[0] * w[0] + w[1] * w[1] for w in wins])
        return carry

    lax.fori_loop(0, meas_ref.shape[0] // BATCH, step, 0)
    for k in range(blocks):
        placed_ref[:, :, k * n : (k + 1) * n] = canvas[:, k]


VM = pl.BlockSpec(memory_space=pltpu.VMEM)
SM = pl.BlockSpec(memory_space=pltpu.SMEM)


def place_light(offsets, probes, extent):
    n = probes.shape[-1]
    return pl.pallas_call(
        light_kernel,
        out_shape=jax.ShapeDtypeStruct((extent, extent), jnp.float32),
        in_specs=[SM, VM],
        out_specs=VM,
        scratch_shapes=[pltpu.VMEM((1, extent // n, extent, n), jnp.float32)],
        compiler_params=pltpu.CompilerParams(vmem_limit_bytes=16 * 1024 * 1024),
        name="place_light",
    )(offsets, probes)


def sweep_tile(offsets, padded, probes, measured, tables):
    n = probes.shape[-1]
    extent = padded.shape[1]
    shape = (2, extent // n, extent, n)
    return pl.pallas_call(
        sweep_kernel,
        out_shape=(
            jax.ShapeDtypeStruct(padded.shape, jnp.float32),
            jax.ShapeDtypeStruct((2 * probes.shape[1] + 1, n, n), jnp.float32),
        ),
        in_specs=[SM] + [VM] * 5,
        out_specs=(VM, VM),
        scratch_shapes=[pltpu.VMEM(shape, jnp.float32)] * 2,
        compiler_params=pltpu.CompilerParams(vmem_limit_bytes=48 * 1024 * 1024),
        name="sweep_tile",
    )(offsets, padded, probes, measured, *tables)


def shift_up(axis):
    count = lax.axis_size(axis)
    return [(i, i + 1) for i in range(count - 1)]


def shift_down(axis):
    count = lax.axis_size(axis)
    return [(i + 1, i) for i in range(count - 1)]


def pad_tile(cells, width):
    for axis, dim in (("row", 1), ("col", 2)):
        size = cells.shape[dim]
        head = lax.slice_in_dim(cells, 0, width, axis=dim)
        tail = lax.slice_in_dim(cells, size - width, size, axis=dim)
        before = lax.ppermute(tail, axis, shift_up(axis))
        after = lax.ppermute(head, axis, shift_down(axis))
        cells = jnp.concatenate([before, cells, after], axis=dim)
    return cells


def sum_overlaps(cells, band):
    for axis, dim in (("row", 1), ("col", 2)):
        size = cells.shape[dim]
        head = lax.slice_in_dim(cells, 0, band, axis=dim)
        middle = lax.slice_in_dim(cells, band, size - band, axis=dim)
        tail = lax.slice_in_dim(cells, size - band, size, axis=dim)
        head = head + lax.ppermute(tail, axis, shift_up(axis))
        tail = tail + lax.ppermute(
            lax.slice_in_dim(cells, 0, band, axis=dim), axis, shift_down(axis)
        )
        cells = jnp.concatenate([head, middle, tail], axis=dim)
    return cells


def body(object_field, probe_modes, scan_offsets, measured):
    n = probe_modes.shape[-1]
    modes = probe_modes.shape[1]
    half = n // 2
    tile = object_field.shape[1]
    extent = tile + n
    positions = scan_offsets.shape[2]
    offsets = scan_offsets.reshape(positions, 2)
    amplitudes = measured.reshape(positions, n, n)
    tables = dft_pair(n)
    inside = np.ones((extent, extent), bool)
    for axis, dim in (("row", 0), ("col", 1)):
        at = lax.broadcasted_iota(jnp.int32, (extent, extent), dim)
        at = at + lax.axis_index(axis) * tile - half
        inside = inside & (at >= 0) & (at < tile * lax.axis_size(axis))
    probes = probe_modes
    padded = pad_tile(object_field, half)
    for sweep in range(ITERS):
        light = place_light(offsets, probes, extent)
        light = sum_overlaps(light[None], n)[0]
        light_max = lax.pmax(jnp.max(light[half : half + tile, half : half + tile]), ("row", "col"))
        placed, grads = sweep_tile(offsets, padded, probes, amplitudes, tables)
        placed = sum_overlaps(placed, n)
        step = (placed - padded * light) / (light + 0.1 * light_max)
        padded = jnp.where(inside, padded + step, 0.0)
        totals = lax.psum(grads, ("row", "col"))
        density = totals[2 * modes]
        sums = totals[: 2 * modes].reshape(probes.shape)
        probes = probes + (sums - probes * density) / (density + 0.1 * jnp.max(density))
    return padded[:, half : half + tile, half : half + tile], probes


def solution(mesh):
    return jax.shard_map(
        body,
        mesh=mesh,
        in_specs=(
            P(None, "row", "col"),
            P(),
            P("row", "col", None, None),
            P("row", "col", None, None, None),
        ),
        out_specs=(P(None, "row", "col"), P()),
        check_vma=False,
    )
```

time: 1340 us -> 723 us (0.54)
  local copies, waits for them, and re-layouts: 286 us -> 11.8 us
  loops' own time: 127 us -> 0 us
  other arithmetic: 126 us -> 18.4 us
  blocking collectives: 151 us -> 80 us
  matrix products: 57.2 us -> 0 us
  Pallas kernels: 0 us -> 29.1 us
  waiting for transfers between devices: 519 us -> 504 us
    dynamic_update_slice x32 -> x0, local copies, waits for them, and re-layouts: 130 us -> none  [visit(): placed = lax.dynamic_update_slice(placed, region + contrib, start)]
    another operation x18 -> x0, loops' own time: 127 us -> none  [the longest x2 126 us: local_terms(): summed, _ = lax.scan(visit, initial, (row_blocks, col_blocks, amplitudes))]
    gather x96 -> x0, local copies, waits for them, and re-layouts: 95.1 us -> none
    pmax x2 -> x1, blocking collectives: 151 us -> 80 us  [body(): lax.pmax(jnp.max(light[half:half + tile, half:half + tile]), ('row', 'col'))]
    dot_general x32 -> x0, matrix products: 57.2 us -> none  [transform(): jnp.einsum('bmij,jk->bmik', sectioned, tables[1], preferred_element_type=...]
    another operation x66 -> x0, other arithmetic: 40 us -> none  [the longest x16 19.1 us: wave_terms(): exit_wave = jnp.stack([exit_re, exit_im], axis=2).astype(jnp.bfloat16)]
    add x74 -> x12, other arithmetic: 44.2 us -> 8.16 us  [the longest x6 4.25 us: sum_overlaps(): head = head + lax.ppermute(tail, axis, shift_up(axis))]
    pallas_call x0 -> x4, Pallas kernels: none -> 29.1 us  [the longest x2 24.8 us: sweep_tile(): pl.pallas_call(sweep_kernel, out_shape=(jax.ShapeDtypeStruct(padded.shape...]
  transfers between devices with their start and end apart: 18 -> 22, of which waited for: 10 -> 6; matrix products, arithmetic and copies ran while one was open for 2% -> 3% of each run, Pallas kernels for 0% -> 2%
where the time goes in v1:
time: 723 us; the launch traced here: 719 us
  waiting for transfers between devices  504 us (70%)
  blocking collectives  80 us (11%)
  starting transfers between devices  58.7 us (8%)
  Pallas kernels  29.1 us (4%)
  other arithmetic  18.4 us (3%)
  between operations  17.4 us (2%)
  local copies, waits for them, and re-layouts  11.8 us (2%)
    psum x2, waiting for transfers between devices, body(): totals = lax.psum(grads, ('row', 'col'))  486 us
    pmax x1, blocking collectives, body(): lax.pmax(jnp.max(light[half:half + tile, half:half + tile]), ('row', 'col'))  80 us
    ppermute x8, starting transfers between devices, sum_overlaps(): head = head + lax.ppermute(tail, axis, shift_up(axis))  32.2 us
    pallas_call x2, Pallas kernels, sweep_tile(): pl.pallas_call(sweep_kernel, out_shape=(jax.ShapeDtypeStruct(padded.shape...  24.8 us
  transfers between devices with their start and end apart: 22, of which 6 were waited for; matrix products, arithmetic and copies ran while one was open for 3% of the time, Pallas kernels for 2%

profile of v1, /device:TPU:1, one launch (start us, length us, event | category | flops | bytes accessed | tf_op | source)
XLA Modules:
  0.0 719.4 jit_solution(11010397423959887551)
XLA Ops:
  7.2 1.0 fusion.23
  8.2 6.0 collective-permute-start
  14.3 1.9 collective-permute-start.1
  16.2 0.8 copy.9.off_ref
  16.9 1.0 copy-done
  18.0 2.2 place_light.2
  20.2 5.1 collective-permute-start.8
  25.3 1.9 collective-permute-start.9
  27.3 0.8 and_and_fusion
  28.2 0.2 fusion.16
  28.4 1.3 collective-permute-start.3
  29.7 4.2 collective-permute-start.2
  34.1 3.5 collective-permute-start.10
  37.6 1.4 collective-permute-start.11
  39.1 3.0 collective-permute-done.2
  42.1 0.5 pad_maximum_fusion.obj_ref
  42.6 0.3 copy-done.26
  42.9 12.4 %sweep_tile.2 = (f32[2,384,384]{2,1,0:T(8,128)S(1)}, f32[9,128,128]{2,1,0:T(8,128)}) custom-call(s32[16,2]{1,0:T(8,128)S(1)} %copy.9.off_ref, f32[2,384,384]{2,1,0:T(8,128)S(1)} %pad_maximum_fusion.obj_ref, f32[2,4,128,128]{3,2,1,0:T(8,128)S(1)} %copy-done.1, f32[16,128,128]{2,1,0:T(8,128)S(1)} %bitcast.26, bf16[256,256]{1,0:T(8,128)(2,1)S(1)} %copy-done.7, ...), custom_call_target="tpu_custom_call" | custom-call | tf_op jit(solution)/shard_map/sweep_tile/pallas_call | solution.py:142
  55.2 1.1 copy-done.3
  56.3 0.9 fusion.15
  57.2 6.8 collective-permute-start.4
  64.1 1.9 collective-permute-start.5
  66.1 0.7 fusion.20
  66.9 0.9 slice_reduce_fusion
  67.8 252.8 %all-reduce.4.cloned.1.call-done = f32[9,128,128]{2,1,0:T(8,128)} async-done(((f32[9,128,128]{2,1,0:T(8,128)}), f32[9,128,128]{2,1,0:T(8,128)}) %all-reduce.4.cloned.1.call-update) | async-done | bytes 589840 | tf_op jit(solution)/shard_map/psum | solution.py:216
  320.6 1.5 slice_bitcast_fusion.1
  322.7 0.8 broadcast_add_fusion.1
  323.7 2.2 place_light.3
  325.9 4.9 collective-permute-start.16
  330.7 1.9 collective-permute-start.17
  332.7 1.3 slice_add_fusion.15
  334.1 5.1 collective-permute-done.17
  339.4 2.1 collective-permute-start.18
  341.5 1.3 collective-permute-start.19
  342.8 0.9 fusion.14
  343.7 4.7 collective-permute-start.6
  348.4 1.3 collective-permute-start.7
  349.7 0.7 slice_bitcast_fusion.2
  350.5 0.7 copy-done.20
  351.2 1.4 fusion.17
  352.7 80.0 %all-reduce = (f32[]{:T(128)}, f32[]{:T(128)}) all-reduce(f32[]{:T(128)} %slice_reduce_fusion, f32[]{:T(128)} %get-tuple-element.37), channel_id=1, replica_groups=mesh['row'=16,'col'=16] {'row','col'}, use_global_device_ids=true, to_apply=%region_1.0 | all-reduce | flops 2 | bytes 16 | tf_op jit(solution)/shard_map/pmax | solution.py:211
  433.4 1.0 maximum_add_fusion
  434.5 1.4 slice_add_fusion.11
  435.9 0.1 copy-done.25
  436.0 0.1 copy-done.27
  436.2 0.5 fusion.2.obj_ref
  436.7 12.4 %sweep_tile.3 = (f32[2,384,384]{2,1,0:T(8,128)S(1)}, f32[9,128,128]{2,1,0:T(8,128)}) custom-call(s32[16,2]{1,0:T(8,128)S(1)} %copy.9.off_ref, f32[2,384,384]{2,1,0:T(8,128)S(1)} %fusion.2.obj_ref, f32[2,4,128,128]{3,2,1,0:T(8,128)S(1)} %divide_add_fusion.1.probe_ref, f32[16,128,128]{2,1,0:T(8,128)S(1)} %bitcast.27, bf16[256,256]{1,0:T(8,128)(2,1)S(1)} %copy-done.7, ...), custom_call_target="tpu_custom_call" | custom-call | tf_op jit(solution)/shard_map/sweep_tile/pallas_call | solution.py:142
  449.1 1.1 copy-done.5
  450.2 2.1 fusion.13
  452.3 3.6 collective-permute-start.12
  455.9 1.9 collective-permute-start.13
  457.8 1.0 slice.175
  459.6 1.1 maximum_add_fusion.1
  460.7 0.1 slice.174
  460.8 233.7 %all-reduce.6.cloned.1.call-done = f32[9,128,128]{2,1,0:T(8,128)} async-done(((f32[9,128,128]{2,1,0:T(8,128)}), f32[9,128,128]{2,1,0:T(8,128)}) %all-reduce.6.cloned.1.call-update) | async-done | bytes 589840 | tf_op jit(solution)/shard_map/psum | solution.py:216
  694.5 1.5 slice_bitcast_fusion
  696.8 1.3 slice_add_fusion.13
  698.2 1.4 collective-permute-start.14
  699.7 1.3 collective-permute-start.15
  701.0 0.9 divide_add_fusion
  701.9 5.1 collective-permute-done.14
  707.0 4.2 collective-permute-done.15
  711.2 0.1 slice_add_fusion.9
  711.3 1.3 fusion.6
  (99 shorter events, 1.2 us)
Async XLA Ops:
  7.2 313.4 %all-reduce.4.cloned.1.call-start = ((), (), s32[]{:S(2)}) async-start(), calls=%async_computation | async-start | bytes 1179648 | tf_op jit(solution)/shard_map/psum | solution.py:216
  8.2 19.9 %collective-permute-start = (f32[2,64,256]{2,1,0:T(8,128)S(1)}, f32[2,64,256]{2,1,0:T(8,128)S(1)}, u32[]{:S(2)}, u32[]{:S(2)}) collective-permute-start(f32[2,64,256]{2,1,0:T(8,128)S(1)} %get-tuple-element.63), channel_id=1, source_target_pairs={{0,16},{16,32},{32,48},{48,64},{64,80},{80,96},{96,112},{112,128},... | collective-permute-start | bytes 393224 | tf_op jit(solution)/shard_map/ppermute | solution.py:171
  14.3 13.9 %collective-permute-start.1 = (f32[2,64,256]{2,1,0:T(8,128)S(1)}, f32[2,64,256]{2,1,0:T(8,128)S(1)}, u32[]{:S(2)}, u32[]{:S(2)}) collective-permute-start(f32[2,64,256]{2,1,0:T(8,128)S(1)} %get-tuple-element.62), channel_id=1, source_target_pairs={{16,0},{32,16},{48,32},{64,48},{80,64},{96,80},{112,96},{128,112},... | collective-permute-start | bytes 393224 | tf_op jit(solution)/shard_map/ppermute | solution.py:172
  16.9 1.0 copy-start
  18.0 10.1 %copy-start.28 = (f32[2,256,256]{2,1,0:T(8,128)S(1)}, f32[2,256,256]{2,1,0:T(8,128)}, u32[]{:S(2)}) copy-start(f32[2,256,256]{2,1,0:T(8,128)} %param.7) | copy-start | bytes 1572868
  20.2 13.7 %collective-permute-start.8 = (f32[1,128,384]{2,1,0:T(8,128)S(1)}, f32[1,128,384]{2,1,0:T(8,128)S(1)}, u32[]{:S(2)}, u32[]{:S(2)}) collective-permute-start(f32[1,128,384]{2,1,0:T(8,128)S(1)} %get-tuple-element.60), channel_id=1, source_target_pairs={{0,16},{16,32},{32,48},{48,64},{64,80},{80,96},{96,112},{112,128},... | collective-permute-start | bytes 589832 | tf_op jit(solution)/shard_map/ppermute | solution.py:183
  25.3 8.6 %collective-permute-start.9 = (f32[1,128,384]{2,1,0:T(8,128)S(1)}, f32[1,128,384]{2,1,0:T(8,128)S(1)}, u32[]{:S(2)}, u32[]{:S(2)}) collective-permute-start(f32[1,128,384]{2,1,0:T(8,128)S(1)} %get-tuple-element.61), channel_id=1, source_target_pairs={{16,0},{32,16},{48,32},{64,48},{80,64},{96,80},{112,96},{128,112},... | collective-permute-start | bytes 589832 | tf_op jit(solution)/shard_map/ppermute | solution.py:184
  28.2 13.9 %copy-start.11 = (f32[2,384,256]{2,1,0:T(8,128)}, f32[2,384,256]{2,1,0:T(8,128)S(1)}, u32[]{:S(2)}) copy-start(f32[2,384,256]{2,1,0:T(8,128)S(1)} %constant_dynamic-update-slice_fusion) | copy-start | bytes 2359300
  28.4 10.7 %collective-permute-start.3 = (f32[2,384,64]{2,1,0:T(8,128)S(1)}, f32[2,384,64]{2,1,0:T(8,128)S(1)}, u32[]{:S(2)}, u32[]{:S(2)}) collective-permute-start(f32[2,384,64]{2,1,0:T(8,128)S(1)} %get-tuple-element.33), channel_id=1, source_target_pairs={{1,0},{2,1},{3,2},{4,3},{5,4},{6,5},{7,6},{8,7},{9,8},{10,9},{11,1... | collective-permute-start | bytes 589832 | tf_op jit(solution)/shard_map/ppermute | solution.py:172
  29.7 12.4 %collective-permute-start.2 = (f32[2,384,64]{2,1,0:T(8,128)S(1)}, f32[2,384,64]{2,1,0:T(8,128)S(1)}, u32[]{:S(2)}, u32[]{:S(2)}) collective-permute-start(f32[2,384,64]{2,1,0:T(8,128)S(1)} %get-tuple-element.32), channel_id=1, source_target_pairs={{0,1},{1,2},{2,3},{3,4},{4,5},{5,6},{6,7},{7,8},{8,9},{9,10},{10,1... | collective-permute-start | bytes 589832 | tf_op jit(solution)/shard_map/ppermute | solution.py:171
  34.1 32.0 %collective-permute-start.10 = (f32[1,384,128]{2,1,0:T(8,128)S(1)}, f32[1,384,128]{2,1,0:T(8,128)S(1)}, u32[]{:S(2)}, u32[]{:S(2)}) collective-permute-start(f32[1,384,128]{2,1,0:T(8,128)S(1)} %get-tuple-element.55), channel_id=1, source_target_pairs={{0,1},{1,2},{2,3},{3,4},{4,5},{5,6},{6,7},{7,8},{8,9},{9,10},{10,1... | collective-permute-start | bytes 589832 | tf_op jit(solution)/shard_map/ppermute | solution.py:183
  37.6 5.2 copy-start.1
  37.6 5.2 copy-start.2
  37.6 5.2 copy-start.7
  37.6 5.2 copy-start.8
  37.6 28.4 %collective-permute-start.11 = (f32[1,384,128]{2,1,0:T(8,128)S(1)}, f32[1,384,128]{2,1,0:T(8,128)S(1)}, u32[]{:S(2)}, u32[]{:S(2)}) collective-permute-start(f32[1,384,128]{2,1,0:T(8,128)S(1)} %get-tuple-element.56), channel_id=1, source_target_pairs={{1,0},{2,1},{3,2},{4,3},{5,4},{6,5},{7,6},{8,7},{9,8},{10,9},{11,1... | collective-permute-start | bytes 589832 | tf_op jit(solution)/shard_map/ppermute | solution.py:184
  39.1 3.5 copy-start.24
  42.1 0.7 copy-start.26
  55.2 1.1 copy-start.3
  57.2 275.4 %collective-permute-start.4 = (f32[2,128,384]{2,1,0:T(8,128)}, f32[2,128,384]{2,1,0:T(8,128)}, u32[]{:S(2)}, u32[]{:S(2)}) collective-permute-start(f32[2,128,384]{2,1,0:T(8,128)} %get-tuple-element.30), channel_id=1, source_target_pairs={{0,16},{16,32},{32,48},{48,64},{64,80},{80,96},{96,112},{112,128},... | collective-permute-start | bytes 1179656 | tf_op jit(solution)/shard_map/ppermute | solution.py:183
  64.1 268.6 %collective-permute-start.5 = (f32[2,128,384]{2,1,0:T(8,128)}, f32[2,128,384]{2,1,0:T(8,128)}, u32[]{:S(2)}, u32[]{:S(2)}) collective-permute-start(f32[2,128,384]{2,1,0:T(8,128)} %get-tuple-element.31), channel_id=1, source_target_pairs={{16,0},{32,16},{48,32},{64,48},{80,64},{96,80},{112,96},{128,112},... | collective-permute-start | bytes 1179656 | tf_op jit(solution)/shard_map/ppermute | solution.py:184
  66.0 628.5 %all-reduce.6.cloned.1.call-start = ((), (), s32[]{:S(2)}) async-start(), calls=%async_computation.1 | async-start | bytes 1179648 | tf_op jit(solution)/shard_map/psum | solution.py:216
  66.8 255.8 %copy-start.16 = (f32[1,384,128]{2,1,0:T(8,128)}, f32[1,384,128]{2,1,0:T(8,128)S(1)}, u32[]{:S(2)}) copy-start(f32[1,384,128]{2,1,0:T(8,128)S(1)} %get-tuple-element.52) | copy-start | bytes 589828
  66.8 255.9 %copy-start.18 = (f32[1,384,128]{2,1,0:T(8,128)}, f32[1,384,128]{2,1,0:T(8,128)S(1)}, u32[]{:S(2)}) copy-start(f32[1,384,128]{2,1,0:T(8,128)S(1)} %get-tuple-element.53) | copy-start | bytes 589828
  66.9 256.7 %copy-start.13 = (f32[384,384]{1,0:T(8,128)}, f32[384,384]{1,0:T(8,128)S(1)}, u32[]{:S(2)}) copy-start(f32[384,384]{1,0:T(8,128)S(1)} %maximum_bitcast_fusion) | copy-start | bytes 1769476
  320.6 3.0 slice-start.1
  323.6 9.0 %copy-start.4 = (f32[2,384,384]{2,1,0:T(8,128)S(1)}, f32[2,384,384]{2,1,0:T(8,128)}, u32[]{:S(2)}) copy-start(f32[2,384,384]{2,1,0:T(8,128)} %copy-done.3) | copy-start | bytes 3538948
  325.9 8.2 %collective-permute-start.16 = (f32[1,128,384]{2,1,0:T(8,128)S(1)}, f32[1,128,384]{2,1,0:T(8,128)S(1)}, u32[]{:S(2)}, u32[]{:S(2)}) collective-permute-start(f32[1,128,384]{2,1,0:T(8,128)S(1)} %get-tuple-element.47), channel_id=1, source_target_pairs={{0,16},{16,32},{32,48},{48,64},{64,80},{80,96},{96,112},{112,128},... | collective-permute-start | bytes 589832 | tf_op jit(solution)/shard_map/ppermute | solution.py:183
  330.7 8.5 %collective-permute-start.17 = (f32[1,128,384]{2,1,0:T(8,128)S(1)}, f32[1,128,384]{2,1,0:T(8,128)S(1)}, u32[]{:S(2)}, u32[]{:S(2)}) collective-permute-start(f32[1,128,384]{2,1,0:T(8,128)S(1)} %get-tuple-element.48), channel_id=1, source_target_pairs={{16,0},{32,16},{48,32},{64,48},{80,64},{96,80},{112,96},{128,112},... | collective-permute-start | bytes 589832 | tf_op jit(solution)/shard_map/ppermute | solution.py:184
  334.1 8.7 %copy-start.9 = (f32[2,384,384]{2,1,0:T(8,128)}, f32[2,384,384]{2,1,0:T(8,128)S(1)}, u32[]{:S(2)}) copy-start(f32[2,384,384]{2,1,0:T(8,128)S(1)} %pad_maximum_fusion.1) | copy-start | bytes 3538948
  339.4 10.3 %collective-permute-start.18 = (f32[1,384,128]{2,1,0:T(8,128)S(1)}, f32[1,384,128]{2,1,0:T(8,128)S(1)}, u32[]{:S(2)}, u32[]{:S(2)}) collective-permute-start(f32[1,384,128]{2,1,0:T(8,128)S(1)} %get-tuple-element.42), channel_id=1, source_target_pairs={{0,1},{1,2},{2,3},{3,4},{4,5},{5,6},{6,7},{7,8},{8,9},{9,10},{10,1... | collective-permute-start | bytes 589832 | tf_op jit(solution)/shard_map/ppermute | solution.py:183
  341.5 8.3 %collective-permute-start.19 = (f32[1,384,128]{2,1,0:T(8,128)S(1)}, f32[1,384,128]{2,1,0:T(8,128)S(1)}, u32[]{:S(2)}, u32[]{:S(2)}) collective-permute-start(f32[1,384,128]{2,1,0:T(8,128)S(1)} %get-tuple-element.43), channel_id=1, source_target_pairs={{1,0},{2,1},{3,2},{4,3},{5,4},{6,5},{7,6},{8,7},{9,8},{10,9},{11,1... | collective-permute-start | bytes 589832 | tf_op jit(solution)/shard_map/ppermute | solution.py:184
  343.7 90.8 %collective-permute-start.6 = (f32[2,384,128]{2,1,0:T(8,128)}, f32[2,384,128]{2,1,0:T(8,128)}, u32[]{:S(2)}, u32[]{:S(2)}) collective-permute-start(f32[2,384,128]{2,1,0:T(8,128)} %get-tuple-element.25), channel_id=1, source_target_pairs={{0,1},{1,2},{2,3},{3,4},{4,5},{5,6},{6,7},{7,8},{8,9},{9,10},{10,1... | collective-permute-start | bytes 1179656 | tf_op jit(solution)/shard_map/ppermute | solution.py:183
  348.4 86.0 %collective-permute-start.7 = (f32[2,384,128]{2,1,0:T(8,128)}, f32[2,384,128]{2,1,0:T(8,128)}, u32[]{:S(2)}, u32[]{:S(2)}) collective-permute-start(f32[2,384,128]{2,1,0:T(8,128)} %get-tuple-element.26), channel_id=1, source_target_pairs={{1,0},{2,1},{3,2},{4,3},{5,4},{6,5},{7,6},{8,7},{9,8},{10,9},{11,1... | collective-permute-start | bytes 1179656 | tf_op jit(solution)/shard_map/ppermute | solution.py:184
  350.5 0.7 copy-start.20
  350.5 0.8 copy-start.22
  350.5 82.9 %copy-start.17 = (f32[1,384,128]{2,1,0:T(8,128)S(1)}, f32[1,384,128]{2,1,0:T(8,128)}, u32[]{:S(2)}) copy-start(f32[1,384,128]{2,1,0:T(8,128)} %copy-done.16) | copy-start | bytes 589828
  350.5 82.9 %copy-start.19 = (f32[1,384,128]{2,1,0:T(8,128)S(1)}, f32[1,384,128]{2,1,0:T(8,128)}, u32[]{:S(2)}) copy-start(f32[1,384,128]{2,1,0:T(8,128)} %copy-done.18) | copy-start | bytes 589828
  351.1 83.3 %copy-start.10 = (f32[2,384,384]{2,1,0:T(8,128)S(1)}, f32[2,384,384]{2,1,0:T(8,128)}, u32[]{:S(2)}) copy-start(f32[2,384,384]{2,1,0:T(8,128)} %copy-done.9) | copy-start | bytes 3538948
  434.4 1.5 copy-start.12
  434.4 1.5 copy-start.14
  434.4 1.6 copy-start.25
  434.4 1.7 copy-start.27
  434.4 1.8 copy-start.30
  449.1 1.1 copy-start.5
  450.2 9.4 %copy-start.21 = (f32[1,384,128]{2,1,0:T(8,128)S(1)}, f32[1,384,128]{2,1,0:T(8,128)}, u32[]{:S(2)}) copy-start(f32[1,384,128]{2,1,0:T(8,128)} %copy-done.20) | copy-start | bytes 589828
  450.2 9.4 %copy-start.23 = (f32[1,384,128]{2,1,0:T(8,128)S(1)}, f32[1,384,128]{2,1,0:T(8,128)}, u32[]{:S(2)}) copy-start(f32[1,384,128]{2,1,0:T(8,128)} %copy-done.22) | copy-start | bytes 589828
  452.3 244.4 %collective-permute-start.12 = (f32[2,128,384]{2,1,0:T(8,128)}, f32[2,128,384]{2,1,0:T(8,128)}, u32[]{:S(2)}, u32[]{:S(2)}) collective-permute-start(f32[2,128,384]{2,1,0:T(8,128)} %get-tuple-element.20), channel_id=1, source_target_pairs={{0,16},{16,32},{32,48},{48,64},{64,80},{80,96},{96,112},{112,128},... | collective-permute-start | bytes 1179656 | tf_op jit(solution)/shard_map/ppermute | solution.py:183
  455.9 240.8 %collective-permute-start.13 = (f32[2,128,384]{2,1,0:T(8,128)}, f32[2,128,384]{2,1,0:T(8,128)}, u32[]{:S(2)}, u32[]{:S(2)}) collective-permute-start(f32[2,128,384]{2,1,0:T(8,128)} %get-tuple-element.21), channel_id=1, source_target_pairs={{16,0},{32,16},{48,32},{64,48},{80,64},{96,80},{112,96},{128,112},... | collective-permute-start | bytes 1179656 | tf_op jit(solution)/shard_map/ppermute | solution.py:184
  459.6 237.2 %copy-start.6 = (f32[2,384,384]{2,1,0:T(8,128)S(1)}, f32[2,384,384]{2,1,0:T(8,128)}, u32[]{:S(2)}) copy-start(f32[2,384,384]{2,1,0:T(8,128)} %copy-done.5) | copy-start | bytes 3538948
  698.2 2.8 copy-start.15
  698.2 2.9 slice-start
  698.2 8.7 %collective-permute-start.14 = (f32[2,384,128]{2,1,0:T(8,128)S(1)}, f32[2,384,128]{2,1,0:T(8,128)S(1)}, u32[]{:S(2)}, u32[]{:S(2)}) collective-permute-start(f32[2,384,128]{2,1,0:T(8,128)S(1)} %get-tuple-element.15), channel_id=1, source_target_pairs={{0,1},{1,2},{2,3},{3,4},{4,5},{5,6},{6,7},{7,8},{8,9},{9,10},{10,1... | collective-permute-start | bytes 1179656 | tf_op jit(solution)/shard_map/ppermute | solution.py:183
  699.7 11.5 %collective-permute-start.15 = (f32[2,384,128]{2,1,0:T(8,128)S(1)}, f32[2,384,128]{2,1,0:T(8,128)S(1)}, u32[]{:S(2)}, u32[]{:S(2)}) collective-permute-start(f32[2,384,128]{2,1,0:T(8,128)S(1)} %get-tuple-element.16), channel_id=1, source_target_pairs={{1,0},{2,1},{3,2},{4,3},{5,4},{6,5},{7,6},{8,7},{9,8},{10,9},{11,1... | collective-permute-start | bytes 1179656 | tf_op jit(solution)/shard_map/ppermute | solution.py:184
  701.9 9.4 %copy-start.29 = (f32[256,256]{1,0:T(8,128)S(1)}, f32[256,256]{1,0:T(8,128)}, u32[]{:S(2)}) copy-start(f32[256,256]{1,0:T(8,128)} %get-tuple-element.36) | copy-start | bytes 786436
Sparse Core Ops, SparseCore 0:
  66.1 254.3 all-reduce.3
  450.3 244.1 all-reduce.5

commit v2 on v1

v2 whole, which is shorter than its diff:
```python
import functools

import jax
import jax.numpy as jnp
import numpy as np
from jax import lax
from jax.experimental import pallas as pl
from jax.experimental.pallas import tpu as pltpu
from jax.sharding import Mesh, PartitionSpec as P

ITERS = 2
BATCH = 2
SPLIT = (("y", 4), ("xh", 2), ("core", 2), ("xl", 2), ("z", 8))
ROW = ("y", "xh", "core")
COL = ("xl", "z")
RING = ("y", "z")
PARTS = 32
CHUNK = 24
DATA = 18

VM = pl.BlockSpec(memory_space=pltpu.VMEM)
SM = pl.BlockSpec(memory_space=pltpu.SMEM)
F32 = jnp.float32
SPOTS = pltpu.SMEM((9 * 16 + 1, 2), jnp.int32)


def dft_pair(n):
    index = np.arange(n)
    angle = (index[:, None] * index[None, :] % n) * (2.0 * np.pi / n)
    c = np.cos(angle) / np.sqrt(n)
    s = np.sin(angle) / np.sqrt(n)
    forward = np.block([[c, s], [-s, c]])
    backward = np.block([[c, -s], [s, c]])
    return jnp.asarray(forward, jnp.bfloat16), jnp.asarray(backward, jnp.bfloat16)


def total(values):
    return functools.reduce(jnp.add, values)


def place(canvas, ch, where, lane, value):
    u, k, s = where
    n = value.shape[0]
    rolled = pltpu.roll(value, s, 1)
    canvas[ch, k, pl.ds(u, n), :] += jnp.where(lane >= s, rolled, 0.0)
    canvas[ch, k + 1, pl.ds(u, n), :] += jnp.where(lane >= s, 0.0, rolled)


def sweep_positions(off_ref, probe_ref, meas_ref, fwd_ref, bwd_ref, cells, canvas, grads):
    modes = probe_ref.shape[1]
    n = probe_ref.shape[2]
    canvas[...] = jnp.zeros_like(canvas)
    grads[...] = jnp.zeros_like(grads)
    lane = lax.broadcasted_iota(jnp.int32, (n, n), 1)

    def window(ch, where):
        u, k, s = where
        left = cells[ch, k, pl.ds(u, n), :]
        right = cells[ch, k + 1, pl.ds(u, n), :]
        return pltpu.roll(jnp.where(lane >= s, left, right), n - s, 1)

    def transform(field, left, right):
        sec = jnp.dot(left, field, preferred_element_type=F32).astype(jnp.bfloat16)
        parts = [slice(m * n, (m + 1) * n) for m in range(modes)]
        rows = [jnp.concatenate([sec[:n, part], sec[n:, part]], 1) for part in parts]
        return jnp.dot(jnp.concatenate(rows, 0), right, preferred_element_type=F32)

    def paired(re_parts, im_parts):
        re_all = jnp.concatenate([x.astype(jnp.bfloat16) for x in re_parts], 1)
        im_all = jnp.concatenate([x.astype(jnp.bfloat16) for x in im_parts], 1)
        return jnp.concatenate([re_all, im_all], 0)

    def split(wave):
        return [(wave[m * n : (m + 1) * n, :n], wave[m * n : (m + 1) * n, n:]) for m in range(modes)]

    def spot(q):
        u = off_ref[q, 0]
        v = off_ref[q, 1]
        return u, v // n, lax.rem(v, n)

    def step(i, carry):
        probes = [(probe_ref[0, m], probe_ref[1, m]) for m in range(modes)]
        spots = [spot(i * BATCH + j) for j in range(BATCH)]
        wins = [(window(0, where), window(1, where)) for where in spots]
        exits = []
        for w_re, w_im in wins:
            re_parts = [p_re * w_re - p_im * w_im for p_re, p_im in probes]
            im_parts = [p_re * w_im + p_im * w_re for p_re, p_im in probes]
            exits.append(paired(re_parts, im_parts))
        fars = [split(transform(x, fwd_ref[...], bwd_ref[...])) for x in exits]
        corrected = []
        for j, far in enumerate(fars):
            power = total([re * re + im * im for re, im in far])
            scale = meas_ref[i * BATCH + j] / jnp.sqrt(power + 1.0)
            corrected.append(paired([re * scale for re, _ in far], [im * scale for _, im in far]))
        backs = [split(transform(x, bwd_ref[...], fwd_ref[...])) for x in corrected]
        for where, back in zip(spots, backs):
            place(canvas, 0, where, lane, total([p[0] * b[0] + p[1] * b[1] for p, b in zip(probes, back)]))
            place(canvas, 1, where, lane, total([p[0] * b[1] - p[1] * b[0] for p, b in zip(probes, back)]))
        for m in range(modes):
            pairs = [(w, back[m]) for w, back in zip(wins, backs)]
            grads[m] += total([w[0] * b[0] + w[1] * b[1] for w, b in pairs])
            grads[modes + m] += total([w[0] * b[1] - w[1] * b[0] for w, b in pairs])
        grads[2 * modes] += total([w[0] * w[0] + w[1] * w[1] for w in wins])
        return carry

    lax.fori_loop(0, meas_ref.shape[0] // BATCH, step, 0)


def pack_half(grads, half, out_ref):
    planes = grads.shape[0]
    out_ref[...] = jnp.zeros_like(out_ref)
    for c in range(planes):
        for t in range(2):
            out_ref[pl.ds(2 * c + t, PARTS, stride=CHUNK), :] = grads[
                c, pl.ds(half * 2 * PARTS + t, PARTS, stride=2), :
            ]


def unpack_half(in_ref, half, grads):
    planes = grads.shape[0]
    for c in range(planes):
        for t in range(2):
            grads[c, pl.ds(half * 2 * PARTS + t, PARTS, stride=2), :] = in_ref[
                pl.ds(2 * c + t, PARTS, stride=CHUNK), :
            ]


def finish(copies, at_ref, canvas, grads, top_ref, mid_ref, low_ref, keep_ref, send_ref):
    n = grads.shape[1]
    starts = (0, top_ref.shape[1], top_ref.shape[1] + mid_ref.shape[1])
    for ref, start in zip((top_ref, mid_ref, low_ref), starts):
        for k in range(canvas.shape[1]):
            ref[:, :, k * n : (k + 1) * n] = canvas[:, k, start : start + ref.shape[1]]
        copies.ready(ref)
    for core in range(2):

        @pl.when(at_ref[0] == core)
        def _():
            pack_half(grads, core, keep_ref)
            pack_half(grads, 1 - core, send_ref)


def join_rows_kernel(copies, obj_ref, upper_ref, lower_ref, tag_ref, tall_ref, left_ref, right_ref):
    band = upper_ref.shape[1] - 8
    size = obj_ref.shape[1]
    n = left_ref.shape[1]
    extent = tall_ref.shape[1]
    tall_ref[:, :band] = upper_ref[:, :band]
    copies.need(obj_ref)
    tall_ref[:, band : band + size] = obj_ref[...]
    tall_ref[:, band + size :] = lower_ref[:, :band]
    lane = lax.broadcasted_iota(jnp.int32, (extent, n), 1)
    left_ref[:extent] = jnp.where(lane < band, tall_ref[0, :, :n], pltpu.roll(tall_ref[1, :, :n], band, 1))
    right_ref[:extent] = jnp.where(
        lane < band, pltpu.roll(tall_ref[0, :, size - n :], band, 1), tall_ref[1, :, size - n :]
    )
    for ref in (left_ref, right_ref):
        ref[extent : extent + 1] = upper_ref[0, band : band + 1, :n]
        ref[extent + 1 : extent + 2] = tag_ref[:1]
        ref[extent + 2 : extent + 3] = lower_ref[0, band : band + 1, :n]
        ref[extent + 3 :] = jnp.zeros((5, n), F32)


def first_kernel(
    copies, off_ref, at_ref, tall_ref, before_ref, after_ref, probe_ref, meas_ref, fwd_ref, bwd_ref,
    top_ref, mid_ref, low_ref, keep_ref, send_ref, cells, canvas, grads,
):
    n = probe_ref.shape[2]
    half = n // 2
    extent = tall_ref.shape[1]
    lane = lax.broadcasted_iota(jnp.int32, (extent, n), 1)
    before = before_ref[:extent]
    after = after_ref[:extent]
    strips = [
        (before, pltpu.roll(after, half, 1)),
        (pltpu.roll(before, half, 1), after),
    ]
    for ch in range(2):
        inner = [pltpu.roll(tall_ref[ch, :, k * n : (k + 1) * n], half, 1) for k in range(2)]
        row = [strips[ch][0], *inner, strips[ch][1]]
        for k in range(3):
            cells[ch, k] = jnp.where(lane < half, row[k], row[k + 1])
    copies.ready(cells)
    copies.need(meas_ref, fwd_ref, bwd_ref)
    sweep_positions(off_ref, probe_ref, meas_ref, fwd_ref, bwd_ref, cells, canvas, grads)
    finish(copies, at_ref, canvas, grads, top_ref, mid_ref, low_ref, keep_ref, send_ref)


def light_peak(mine_ref, other_ref):
    best = [jnp.max(ref[pl.ds(DATA, PARTS, stride=CHUNK), :]) for ref in (mine_ref, other_ref)]
    return jnp.maximum(best[0], best[1])


def update_probes(at_ref, mine_ref, other_ref, probe_ref, grads, new_probe_ref):
    modes = probe_ref.shape[1]
    for core in range(2):

        @pl.when(at_ref[0] == core)
        def _():
            unpack_half(mine_ref, core, grads)
            unpack_half(other_ref, 1 - core, grads)

    density = grads[2 * modes]
    scale = 1.0 / (density + 0.1 * jnp.max(density))
    for part in range(2):
        for m in range(modes):
            old = probe_ref[part, m]
            new_probe_ref[part, m] = old + (grads[part * modes + m] - old * density) * scale


def updated(old, sums, light, peak):
    scale = 1.0 / (light + 0.1 * peak)
    return [old[ch] + (sums[ch] - old[ch] * light) * scale for ch in range(2)]


def next_kernel(
    copies, off_ref, at_ref, obj_ref, top_ref, mid_ref, low_ref, left_ref, right_ref, light_ref,
    mine_ref, other_ref, probe_ref, meas_ref, fwd_ref, bwd_ref,
    new_top_ref, new_mid_ref, new_low_ref, keep_ref, send_ref, new_obj_ref, new_probe_ref,
    canvas, grads,
):
    n = probe_ref.shape[2]
    blocks = obj_ref.shape[1]
    copies.need(obj_ref, top_ref, mid_ref, low_ref, left_ref, right_ref, light_ref)
    peak = light_peak(mine_ref, other_ref)
    for j, ref in enumerate((top_ref, mid_ref, low_ref)):
        rows = slice(j * n, (j + 1) * n)
        row = lax.broadcasted_iota(jnp.int32, (n, n), 0) + j * n
        row_ok = (row >= at_ref[1]) & (row < at_ref[2])
        for k in range(blocks):
            col = lax.broadcasted_iota(jnp.int32, (n, n), 1) + k * n
            inside = row_ok & (col >= at_ref[3]) & (col < at_ref[4])
            sums = ref[:, :, k * n : (k + 1) * n]
            if k == 0:
                sums = sums + left_ref[:, rows]
            elif k == blocks - 1:
                sums = sums + right_ref[:, rows]
            new = updated(obj_ref[:, k, rows], sums, light_ref[0, k + 1, n + j * n : 2 * n + j * n], peak)
            for ch in range(2):
                new_obj_ref[ch, k, rows] = jnp.where(inside, new[ch], 0.0)
    copies.ready(new_obj_ref)
    copies.need(probe_ref)
    update_probes(at_ref, mine_ref, other_ref, probe_ref, grads, new_probe_ref)
    copies.ready(new_probe_ref)
    copies.need(meas_ref, fwd_ref, bwd_ref)
    sweep_positions(off_ref, new_probe_ref, meas_ref, fwd_ref, bwd_ref, new_obj_ref, canvas, grads)
    finish(copies, at_ref, canvas, grads, new_top_ref, new_mid_ref, new_low_ref, keep_ref, send_ref)


def last_kernel(
    copies, at_ref, obj_ref, sums_ref, left_ref, right_ref, light_ref, mine_ref, other_ref, probe_ref,
    out_ref, new_probe_ref, grads,
):
    n = probe_ref.shape[2]
    half = n // 2
    blocks = obj_ref.shape[1]
    tile = out_ref.shape[1]
    inner = slice(half, half + tile)
    copies.need(probe_ref)
    update_probes(at_ref, mine_ref, other_ref, probe_ref, grads, new_probe_ref)
    copies.need(obj_ref, sums_ref, left_ref, right_ref, light_ref)
    peak = light_peak(mine_ref, other_ref)
    lane = lax.broadcasted_iota(jnp.int32, (tile, n), 1)
    rolled = []
    for k in range(blocks):
        sums = [sums_ref[ch, :, k * n : (k + 1) * n] for ch in range(2)]
        if k == 0:
            sums[0] = sums[0] + jnp.where(lane < half, 0.0, left_ref[...])
            sums[1] = sums[1] + jnp.where(lane < half, 0.0, pltpu.roll(left_ref[...], half, 1))
        elif k == blocks - 1:
            sums[0] = sums[0] + jnp.where(lane < half, right_ref[...], 0.0)
            sums[1] = sums[1] + jnp.where(lane < half, pltpu.roll(right_ref[...], half, 1), 0.0)
        new = updated(obj_ref[:, k, inner], sums, light_ref[0, k + 1, n + half : n + half + tile], peak)
        rolled.append([pltpu.roll(x, half, 1) for x in new])
    for k in range(blocks - 1):
        for ch in range(2):
            out_ref[ch, :, k * n : (k + 1) * n] = jnp.where(lane < half, rolled[k][ch], rolled[k + 1][ch])


def fold_kernel(copies, top_ref, low_ref, mid_ref, upper_ref, lower_ref, new_top_ref, new_low_ref, left_ref, right_ref):
    n = left_ref.shape[2]
    extent = left_ref.shape[1]
    copies.need(top_ref, low_ref, upper_ref, lower_ref)
    new_top_ref[...] = top_ref[...] + upper_ref[...]
    copies.ready(new_top_ref)
    new_low_ref[...] = low_ref[...] + lower_ref[...]
    copies.ready(new_low_ref)
    copies.need(mid_ref)
    for j, ref in enumerate((new_top_ref, mid_ref, new_low_ref)):
        left_ref[:, j * n : (j + 1) * n] = ref[:, :, :n]
        right_ref[:, j * n : (j + 1) * n] = ref[:, :, extent - n :]
    copies.ready(left_ref, right_ref)


def fold_inner_kernel(copies, mid_ref, upper_ref, lower_ref, sums_ref, left_ref, right_ref):
    n = left_ref.shape[1]
    band = upper_ref.shape[1]
    tile = mid_ref.shape[1]
    extent = mid_ref.shape[2]
    copies.need(mid_ref, upper_ref, lower_ref)
    sums_ref[:, :band] = mid_ref[:, :band] + upper_ref[...]
    sums_ref[:, band : tile - band] = mid_ref[:, band : tile - band]
    sums_ref[:, tile - band :] = mid_ref[:, tile - band :] + lower_ref[...]
    lane = lax.broadcasted_iota(jnp.int32, (tile, n), 1)
    left_ref[...] = jnp.where(lane < band, sums_ref[0, :, :n], pltpu.roll(sums_ref[1, :, :n], band, 1))
    right_ref[...] = jnp.where(
        lane < band, pltpu.roll(sums_ref[1, :, extent - n :], band, 1), sums_ref[0, :, extent - n :]
    )
    copies.ready(sums_ref, left_ref, right_ref)


def place_lights(tag_ref, probe_ref, canvas, spots, rim, tile):
    n = probe_ref.shape[2]
    half = n // 2
    lane = lax.broadcasted_iota(jnp.int32, (n, n), 1)
    value = jnp.sum(probe_ref[0] * probe_ref[0] + probe_ref[1] * probe_ref[1], axis=0)
    count = jnp.int32(0)
    for t in range(9):
        if rim and t == 4:
            continue
        down, across = t % 3 - 1, t // 3 - 1

        def gather(p, count):
            u = tag_ref[t, 2 * p].astype(jnp.int32)
            v = tag_ref[t, 2 * p + 1].astype(jnp.int32)
            held = u > 0
            u = u + (n - 1 + down * tile)
            v = v + (n - 1 + across * tile)
            inner = (u > half) & (u < tile + n + half) & (v > half) & (v < tile + n + half)
            if rim:
                held = held & ~inner & (u > 0) & (u < tile + 2 * n) & (v > 0) & (v < tile + 2 * n)
            else:
                held = held & inner
            spots[count, 0] = u
            spots[count, 1] = v
            return count + held.astype(jnp.int32)

        count = lax.fori_loop(0, tag_ref.shape[1] // 2, gather, count, unroll=4)

    def step(q, carry):
        v = spots[q, 1]
        place(canvas, 0, (spots[q, 0], v // n, lax.rem(v, n)), lane, value)
        return carry

    lax.fori_loop(0, count, step, 0)


def light_kernel(copies, tag_ref, probe_ref, light_ref, peak_ref, spots):
    n = probe_ref.shape[2]
    tile = light_ref.shape[2] - 3 * n
    edge = 3 * n // 2
    blocks = light_ref.shape[1]
    light_ref[...] = jnp.zeros_like(light_ref)
    copies.need(probe_ref)
    place_lights(tag_ref, probe_ref, light_ref, spots, False, tile)
    copies.ready(light_ref)
    lane = lax.broadcasted_iota(jnp.int32, (tile, n), 1)
    best = None
    for k in range(1, blocks - 1):
        mine = light_ref[0, k, edge : edge + tile]
        if k == 1:
            mine = jnp.where(lane >= n // 2, mine, 0.0)
        elif k == blocks - 2:
            mine = jnp.where(lane < n // 2, mine, 0.0)
        best = mine if best is None else jnp.maximum(best, mine)
    peak_ref[...] = jnp.full(peak_ref.shape, jnp.max(best), F32)


def more_light_kernel(copies, tag_ref, probe_ref, light_ref, all_ref, spots):
    copies.need(light_ref, probe_ref)
    all_ref[...] = light_ref[...]
    place_lights(tag_ref, probe_ref, all_ref, spots, True, light_ref.shape[2] - 3 * probe_ref.shape[2])
    copies.ready(all_ref)


def share_kernel(copies, parts_ref, peak_ref, out_ref):
    share = parts_ref[:CHUNK]
    for s in range(1, PARTS):
        share = share + parts_ref[s * CHUNK : (s + 1) * CHUNK]
    row = lax.broadcasted_iota(jnp.int32, share.shape, 0)
    out_ref[...] = jnp.where(row < DATA, share, peak_ref[:1])


class Far:
    def __init__(self, value):
        self.value = value


class Copies:
    def __init__(self, ins, outs):
        self.ins = ins
        self.outs = outs
        for copy in ins.values():
            copy.start()

    def need(self, *refs):
        for ref in refs:
            copy = self.ins.pop(id(ref), None)
            if copy is not None:
                copy.wait()

    def ready(self, *refs):
        for ref in refs:
            copy = self.outs.get(id(ref))
            if copy is not None:
                copy.start()


def call(kernel, outs, scratch, args, scalars, name, limit=24):
    far_in = [isinstance(x, Far) for x in args]
    far_out = [isinstance(x, Far) for x in outs]
    args = [pltpu.with_memory_space_constraint(x.value, pltpu.HBM) if isinstance(x, Far) else x for x in args]
    shapes = [x.value if isinstance(x, Far) else x for x in outs]
    buffers = [pltpu.VMEM(x.shape, x.dtype) for x, far in zip(args, far_in) if far]
    buffers += [pltpu.VMEM(x, F32) for x, far in zip(shapes, far_out) if far]
    moved = len(buffers)
    total_in, total_out = len(args), len(shapes)

    def whole(*refs):
        sems = refs[-1]
        refs = list(refs[:-1])
        spare = refs[total_in + total_out :][:moved]
        rest = refs[total_in + total_out + moved :]
        ins, results, at = {}, {}, 0
        for i, far in enumerate(far_in + far_out):
            if not far:
                continue
            remote, local = refs[i], spare[at]
            if i < total_in:
                ins[id(local)] = pltpu.make_async_copy(remote, local, sems.at[at])
            else:
                results[id(local)] = pltpu.make_async_copy(local, remote, sems.at[at])
            refs[i] = local
            at += 1
        copies = Copies(ins, results)
        kernel(copies, *refs[: total_in + total_out], *rest)
        for copy in results.values():
            copy.wait()

    far_spec = pl.BlockSpec(memory_space=pltpu.HBM)
    in_specs = [SM if i < scalars else (far_spec if far else VM) for i, far in enumerate(far_in)]
    return pl.pallas_call(
        whole,
        out_shape=tuple(
            pltpu.HBM(shape, F32) if far else jax.ShapeDtypeStruct(shape, F32) for shape, far in zip(shapes, far_out)
        ),
        in_specs=in_specs,
        out_specs=tuple(far_spec if far else VM for far in far_out),
        scratch_shapes=buffers + [x if x is SPOTS else pltpu.VMEM(x, F32) for x in scratch] + [pltpu.SemaphoreType.DMA((max(moved, 1),))],
        compiler_params=pltpu.CompilerParams(vmem_limit_bytes=limit * 1024 * 1024),
        name=name,
    )(*args)


def length(axes):
    return functools.reduce(lambda a, b: a * b, [lax.axis_size(axis) for axis in axes])


def from_before(value, axes):
    return lax.ppermute(value, axes, [(i, i + 1) for i in range(length(axes) - 1)])


def from_after(value, axes):
    return lax.ppermute(value, axes, [(i + 1, i) for i in range(length(axes) - 1)])


def swap(value, axes):
    count = length(axes)
    return lax.ppermute(value, axes, [(i, count - 1 - i) for i in range(count)])


def share_over_x(share):
    near = swap(share, ("xl",))
    far = swap(share, ("xh",))
    cross = swap(share, ("xh", "xl"))
    at = lax.broadcasted_iota(jnp.int32, share.shape, 0)
    added = (share + near) + (far + cross)
    largest = jnp.maximum(jnp.maximum(share, near), jnp.maximum(far, cross))
    return jnp.where(at < DATA, added, largest)


def body(object_field, probe_modes, scan_offsets, measured):
    n = probe_modes.shape[-1]
    modes = probe_modes.shape[1]
    half = n // 2
    tile = object_field.shape[1]
    extent = tile + n
    blocks = extent // n
    positions = scan_offsets.shape[2]
    offsets = scan_offsets.reshape(positions, 2)
    amplitudes = measured.reshape(positions, n, n)
    tables = dft_pair(n)
    row = lax.axis_index(ROW)
    col = lax.axis_index(COL)
    info = jnp.stack(
        [
            lax.axis_index("core"),
            jnp.where(row == 0, half, 0),
            jnp.where(row == length(ROW) - 1, extent - half, extent),
            jnp.where(col == 0, half, 0),
            jnp.where(col == length(COL) - 1, extent - half, extent),
        ]
    ).astype(jnp.int32)

    tag = (offsets + 1).astype(F32).reshape(1, 2 * positions)
    tag_rows = jnp.pad(tag, ((0, 7), (0, n - 2 * positions)))
    tag_block = jnp.pad(tag[None], ((0, 1), (0, 7), (0, tile - 2 * positions)))
    upper = from_before(jnp.concatenate([object_field[:, tile - half :], tag_block], 1), ROW)
    lower = from_after(jnp.concatenate([object_field[:, :half], tag_block], 1), ROW)
    strip = (extent + 8, n)
    tall, left, right = call(
        join_rows_kernel, [(2, extent, tile), strip, strip], [], [Far(object_field), upper, lower, tag_rows], 0, "join_rows"
    )
    before = from_before(right, COL)
    after = from_after(left, COL)
    own = jnp.concatenate([upper[0, half : half + 1, :32], tag, lower[0, half : half + 1, :32]], 0)
    tags = jnp.concatenate([before[extent : extent + 3, :32], own, after[extent : extent + 3, :32]], 0)

    cells = (2, blocks, extent, n)
    canvas = (1, blocks + 2, extent + 2 * n, n)
    grads = (2 * modes + 1, n, n)
    packed = (PARTS * CHUNK, n)
    band = (2, n, extent)
    probes = probe_modes
    tables = [Far(x) for x in tables]
    amplitudes = Far(amplitudes)
    for sweep in range(ITERS):
        last = sweep == ITERS - 1
        bands = [(2, half, extent), (2, tile, extent), (2, half, extent)] if last else [band] * 3
        outs = [Far(x) for x in bands] + [packed, packed, Far(cells)]
        if sweep == 0:
            args = [offsets, info, tall, before, after, probes, amplitudes, *tables]
            top, mid, low, keep, send, cells_now = call(first_kernel, outs, [cells, grads], args, 2, "first_sweep")
        else:
            held = [Far(x) for x in (cells_now, *sums, light)]
            args = [offsets, info, *held, mine, other, Far(probes), amplitudes, *tables]
            top, mid, low, keep, send, cells_now, probes = call(
                next_kernel, outs + [Far(probes.shape)], [cells, grads], args, 2, "next_sweep"
            )
        received = swap(send, ("core",))
        received, top, low, probes = lax.optimization_barrier((received, top, low, probes))
        parts = lax.all_to_all(keep + received, RING, 0, 0, tiled=True)
        light, peak = call(light_kernel, [Far(canvas), (8, n)], [SPOTS], [tags, Far(probes)], 1, "light")
        upper = from_before(low, ROW)
        lower = from_after(top, ROW)
        parts, upper, lower = lax.optimization_barrier((parts, upper, lower))
        share = call(share_kernel, [(CHUNK, n)], [], [parts, peak], 0, "share")[0]
        share = share_over_x(share)
        copies = jnp.broadcast_to(share[None], (PARTS,) + share.shape).reshape(packed)
        light, copies = lax.optimization_barrier((light, copies))
        mine = lax.all_to_all(copies, RING, 0, 0, tiled=True)
        if last:
            outs = [Far((2, tile, extent)), Far((tile, n)), Far((tile, n))]
            args = [Far(x) for x in (mid, upper, lower)]
            sums, left, right = call(fold_inner_kernel, outs, [], args, 0, "fold_inner")
            sums = [sums]
        else:
            side = (2, extent, n)
            outs = [Far(x) for x in (band, band, side, side)]
            args = [Far(x) for x in (top, low, mid, upper, lower)]
            top, low, left, right = call(fold_kernel, outs, [], args, 0, "fold_rows")
            sums = [top, mid, low]
            args = [tags, Far(probes), Far(light)]
            light = call(more_light_kernel, [Far(canvas)], [SPOTS], args, 1, "more_light")[0]
        left, right = from_before(right, COL), from_after(left, COL)
        mine, left, right, light = lax.optimization_barrier((mine, left, right, light))
        sums += [left, right]
        other = swap(mine, ("core",))
    held = [Far(x) for x in (cells_now, *sums, light)]
    args = [info, *held, mine, other, Far(probes)]
    return call(last_kernel, [object_field.shape, probes.shape], [grads], args, 1, "last_update")


def solution(mesh):
    names = tuple(name for name, _ in SPLIT)
    sizes = tuple(size for _, size in SPLIT)
    fine = Mesh(mesh.devices.reshape(sizes), names)
    return jax.shard_map(
        body,
        mesh=fine,
        in_specs=(
            P(None, ROW, COL),
            P(),
            P(ROW, COL, None, None),
            P(ROW, COL, None, None, None),
        ),
        out_specs=(P(None, ROW, COL), P()),
        check_vma=False,
    )
```

time: 723 us -> 193 us (0.27)
  waiting for transfers between devices: 504 us -> 27.5 us
  blocking collectives: 80 us -> 0 us
  starting transfers between devices: 58.7 us -> 95.2 us
  Pallas kernels: 29.1 us -> 61.9 us
  between operations: 17.4 us -> 1.32 us
  other arithmetic: 18.4 us -> 2.5 us
  local copies, waits for them, and re-layouts: 11.8 us -> 3.15 us
    psum x2 -> x0, waiting for transfers between devices: 486 us -> none  [body(): totals = lax.psum(grads, ('row', 'col'))]
    pmax x1 -> x0, blocking collectives: 80 us -> none  [body(): lax.pmax(jnp.max(light[half:half + tile, half:half + tile]), ('row', 'col'))]
    all_to_all x0 -> x4, starting transfers between devices: none -> 44.3 us  [the longest x2 26.3 us: body(): parts = lax.all_to_all(keep + received, RING, 0, 0, tiled=True)]
    pallas_call x4 -> x11, Pallas kernels: 29.1 us -> 61.9 us  [call(): pl.pallas_call(whole, out_shape=tuple((pltpu.HBM(shape, F32) if far else...]
    ppermute x20 -> x22, waiting for transfers between devices: 17.4 us -> 27.5 us  [the longest x10 11.5 us: swap(): return lax.ppermute(value, axes, [(i, count - 1 - i) for i in range(count)])]
    ppermute x20 -> x22, starting transfers between devices: 58.6 us -> 50.9 us  [the longest x6 21 us: from_before(): lax.ppermute(value, axes, [(i, i + 1) for i in range(length(axes) - 1)])]
  transfers between devices with their start and end apart: 22 -> 26, of which waited for: 6 -> 17; matrix products, arithmetic and copies ran while one was open for 3% -> 0% of each run, Pallas kernels for 2% -> 14%
where the time goes in v2:
time: 193 us; the launch traced here: 192 us
  starting transfers between devices  95.2 us (49%)
  Pallas kernels  61.9 us (32%)
  waiting for transfers between devices  27.5 us (14%)
  local copies, waits for them, and re-layouts  3.15 us (2%)
  other arithmetic  2.5 us (1%)
    pallas_call x11, Pallas kernels, call(): pl.pallas_call(whole, out_shape=tuple((pltpu.HBM(shape, F32) if far else...  61.9 us
    all_to_all x2, starting transfers between devices, body(): parts = lax.all_to_all(keep + received, RING, 0, 0, tiled=True)  26.3 us
    ppermute x6, starting transfers between devices, from_before(): lax.ppermute(value, axes, [(i, i + 1) for i in range(length(axes) - 1)])  21 us
    all_to_all x2, starting transfers between devices, body(): mine = lax.all_to_all(copies, RING, 0, 0, tiled=True)  18 us
    ppermute x10, starting transfers between devices, swap(): return lax.ppermute(value, axes, [(i, count - 1 - i) for i in range(count)])  16.3 us
    ppermute x6, starting transfers between devices, from_after(): lax.ppermute(value, axes, [(i + 1, i) for i in range(length(axes) - 1)])  13.5 us
    ppermute x10, waiting for transfers between devices, swap(): return lax.ppermute(value, axes, [(i, count - 1 - i) for i in range(count)])  11.5 us
    ppermute x6, waiting for transfers between devices, from_after(): lax.ppermute(value, axes, [(i + 1, i) for i in range(length(axes) - 1)])  8.99 us
  transfers between devices with their start and end apart: 26, of which 17 were waited for; matrix products, arithmetic and copies ran while one was open for 0% of the time, Pallas kernels for 14%

profile of v2, /device:TPU:1, one launch (start us, length us, event | category | flops | bytes accessed | tf_op | source)
XLA Modules:
  0.0 191.6 jit_solution(10633170653214919914)
XLA Ops:
  0.7 0.7 add_convert_fusion
  1.4 0.1 copy.12
  1.5 0.1 convert_element_type.28
  1.6 1.0 fusion.2
  2.6 5.1 %collective-permute-start.1 = (f32[2,72,256]{2,1,0:T(8,128)S(1)}, f32[2,72,256]{2,1,0:T(8,128)S(1)}, u32[]{:S(2)}, u32[]{:S(2)}) collective-permute-start(f32[2,72,256]{2,1,0:T(8,128)S(1)} %get-tuple-element.110), channel_id=1, source_target_pairs={{16,0},{32,16},{48,32},{64,48},{80,64},{96,80},{112,96},{128,112},... | collective-permute-start | bytes 442376 | tf_op jit(solution)/shard_map/ppermute | solution.py:465
  7.8 2.8 %collective-permute-start = (f32[2,72,256]{2,1,0:T(8,128)S(1)}, f32[2,72,256]{2,1,0:T(8,128)S(1)}, u32[]{:S(2)}, u32[]{:S(2)}) collective-permute-start(f32[2,72,256]{2,1,0:T(8,128)S(1)} %get-tuple-element.111), channel_id=1, source_target_pairs={{0,16},{16,32},{32,48},{48,64},{64,80},{80,96},{96,112},{112,128},... | collective-permute-start | bytes 442376 | tf_op jit(solution)/shard_map/ppermute | solution.py:461
  10.6 0.1 convert_element_type.29
  10.7 0.8 collective-permute-done.1.refs_2_
  11.5 1.2 collective-permute-done.refs_1_
  12.7 1.2 join_rows.1
  13.9 3.6 %collective-permute-start.2 = (f32[392,128]{1,0:T(8,128)S(1)}, f32[392,128]{1,0:T(8,128)S(1)}, u32[]{:S(2)}, u32[]{:S(2)}) collective-permute-start(f32[392,128]{1,0:T(8,128)S(1)} %get-tuple-element.56), channel_id=1, source_target_pairs={{0,1},{1,2},{2,3},{3,4},{4,5},{5,6},{6,7},{7,8},{8,9},{9,10},{10,1... | collective-permute-start | bytes 602120 | tf_op jit(solution)/shard_map/ppermute | solution.py:461
  17.4 1.3 collective-permute-start.3
  18.8 0.1 copy.15.refs_0_
  18.9 0.1 stack.23.refs_1_.refs_0_
  18.9 1.1 collective-permute-done.2.refs_3_
  20.1 4.0 %collective-permute-done.3.refs_4_ = f32[392,128]{1,0:T(8,128)S(1)} collective-permute-done((f32[392,128]{1,0:T(8,128)S(1)}, f32[392,128]{1,0:T(8,128)S(1)}, u32[]{:S(2)}, u32[]{:S(2)}) %collective-permute-start.3) | collective-permute-done | bytes 200736 | tf_op jit(solution)/shard_map/ppermute | solution.py:465
  24.1 13.5 %first_sweep.1 = (f32[2,128,384]{2,1,0:T(8,128)}, f32[2,128,384]{2,1,0:T(8,128)}, f32[2,128,384]{2,1,0:T(8,128)}, f32[768,128]{1,0:T(8,128)S(1)}, f32[768,128]{1,0:T(8,128)S(1)}, /*index=5*/f32[2,3,384,128]{3,2,1,0:T(8,128)}) custom-call(s32[16,2]{1,0:T(8,128)S(1)} %copy.15.refs_0_, s32[5]{0:T(128)S(1)} %stack.23.refs_1_.refs_0_, ...), custom_call_target="tpu_custom_call" | custom-call | tf_op jit(solution)/shard_map/first_sweep/pallas_call | solution.py:443
  37.6 0.1 collective-permute-start.4
  37.7 1.7 collective-permute-done.4
  39.4 0.8 add.64
  40.2 16.6 %all-to-all-start = ((f32[32,24,128]{2,1,0:T(8,128)}), f32[32,24,128]{2,1,0:T(8,128)S(1)}, u32[]{:S(2)}, u32[]{:S(2)}) async-start(f32[32,24,128]{2,1,0:T(8,128)} %bitcast.7), calls=%async_computation | async-start | bytes 786432 | tf_op jit(solution)/shard_map/all_to_all | solution.py:543
  56.8 2.6 %collective-permute-start.6 = (f32[2,128,384]{2,1,0:T(8,128)S(1)}, f32[2,128,384]{2,1,0:T(8,128)S(1)}, u32[]{:S(2)}, u32[]{:S(2)}) collective-permute-start(f32[2,128,384]{2,1,0:T(8,128)S(1)} %copy-done.3), channel_id=1, source_target_pairs={{16,0},{32,16},{48,32},{64,48},{80,64},{96,80},{112,96},{128,112},... | collective-permute-start | bytes 1179656 | tf_op jit(solution)/shard_map/ppermute | solution.py:465
  59.4 4.5 %collective-permute-start.5 = (f32[2,128,384]{2,1,0:T(8,128)S(1)}, f32[2,128,384]{2,1,0:T(8,128)S(1)}, u32[]{:S(2)}, u32[]{:S(2)}) collective-permute-start(f32[2,128,384]{2,1,0:T(8,128)S(1)} %copy-done.4), channel_id=1, source_target_pairs={{0,16},{16,32},{32,48},{48,64},{64,80},{80,96},{96,112},{112,128},... | collective-permute-start | bytes 1179656 | tf_op jit(solution)/shard_map/ppermute | solution.py:461
  64.0 0.1 concatenate.11.refs_0_
  64.1 7.4 %light.2 = (f32[1,5,640,128]{3,2,1,0:T(8,128)}, f32[8,128]{1,0:T(8,128)S(1)}) custom-call(f32[9,32]{1,0:T(8,128)S(1)} %concatenate.11.refs_0_, f32[2,4,128,128]{3,2,1,0:T(8,128)} %refs_11_), custom_call_target="tpu_custom_call" | custom-call | tf_op jit(solution)/shard_map/light/pallas_call | solution.py:443
  71.6 1.5 collective-permute-start.9
  73.1 1.4 collective-permute-start.8
  74.5 0.4 collective-permute-start.7
  74.9 0.5 collective-permute-done.9
  75.4 1.7 collective-permute-done.8
  77.1 0.2 collective-permute-done.7
  77.4 0.8 broadcast_in_dim.4
  78.2 9.4 %all-to-all-start.1 = ((f32[32,24,128]{2,1,0:T(8,128)}), f32[32,24,128]{2,1,0:T(8,128)S(1)}, u32[]{:S(2)}, u32[]{:S(2)}) async-start(f32[32,24,128]{2,1,0:T(8,128)} %bitcast.12), calls=%async_computation.1 | async-start | bytes 786432 | tf_op jit(solution)/shard_map/all_to_all | solution.py:552
  87.6 2.8 %fold_rows.1 = (f32[2,128,384]{2,1,0:T(8,128)}, f32[2,128,384]{2,1,0:T(8,128)}, f32[2,384,128]{2,1,0:T(8,128)}, f32[2,384,128]{2,1,0:T(8,128)}) custom-call(f32[2,128,384]{2,1,0:T(8,128)} %get-tuple-element.62.refs_0_, f32[2,128,384]{2,1,0:T(8,128)} %get-tuple-element.63.refs_1_, f32[2,128,384]{2,1,0:T(8,128)} %get-tuple-element.64.refs_2_.refs_4_, ...), custom_call_target="tpu_custom_call" | custom-call | tf_op jit(solution)/shard_map/fold_rows/pallas_call | solution.py:443
  90.4 3.2 %collective-permute-start.10 = (f32[2,384,128]{2,1,0:T(8,128)}, f32[2,384,128]{2,1,0:T(8,128)S(1)}, u32[]{:S(2)}, u32[]{:S(2)}) collective-permute-start(f32[2,384,128]{2,1,0:T(8,128)} %get-tuple-element.76), channel_id=1, source_target_pairs={{0,1},{1,2},{2,3},{3,4},{4,5},{5,6},{6,7},{7,8},{8,9},{9,10},{10,1... | collective-permute-start | bytes 1179656 | tf_op jit(solution)/shard_map/ppermute | solution.py:461
  93.5 1.3 collective-permute-start.11
  94.8 7.3 %more_light.1.refs_8_ = f32[1,5,640,128]{3,2,1,0:T(8,128)} custom-call(f32[9,32]{1,0:T(8,128)S(1)} %concatenate.11.refs_0_, f32[2,4,128,128]{3,2,1,0:T(8,128)} %refs_11_, f32[1,5,640,128]{3,2,1,0:T(8,128)} %get-tuple-element.78.refs_2_), custom_call_target="tpu_custom_call" | custom-call | tf_op jit(solution)/shard_map/more_light/pallas_call | solution.py:443
  102.2 1.6 collective-permute-done.10.refs_6_
  103.8 0.7 collective-permute-done.11.refs_7_
  104.5 2.9 %collective-permute-start.12 = (f32[768,128]{1,0:T(8,128)S(1)}, f32[768,128]{1,0:T(8,128)S(1)}, u32[]{:S(2)}, u32[]{:S(2)}) collective-permute-start(f32[768,128]{1,0:T(8,128)S(1)} %bitcast.25), channel_id=1, source_target_pairs={{0,16},{16,0},{1,17},{17,1},{2,18},{18,2},{3,19},{19,3},{4,20},{20... | collective-permute-start | bytes 1179656 | tf_op jit(solution)/shard_map/ppermute | solution.py:470
  107.4 1.3 collective-permute-done.12.refs_10_
  108.8 15.5 %next_sweep.1 = (f32[2,64,384]{2,1,0:T(8,128)}, f32[2,256,384]{2,1,0:T(8,128)}, f32[2,64,384]{2,1,0:T(8,128)}, f32[768,128]{1,0:T(8,128)S(1)}, f32[768,128]{1,0:...) custom-call(s32[16,2]{1,0:T(8,128)S(1)} %copy.15.refs_0_, s32[5]{0:T(128)S(1)} %stack.23.refs_1_.refs_0_, ...), custom_call_target="tpu_custom_call" | custom-call | tf_op jit(solution)/shard_map/next_sweep/pallas_call | solution.py:443
  124.3 0.7 collective-permute-start.13
  124.9 1.3 collective-permute-done.13
  126.3 0.8 add.68
  127.1 9.7 %all-to-all-start.2 = ((f32[32,24,128]{2,1,0:T(8,128)}), f32[32,24,128]{2,1,0:T(8,128)S(1)}, u32[]{:S(2)}, u32[]{:S(2)}) async-start(f32[32,24,128]{2,1,0:T(8,128)} %bitcast.14), calls=%async_computation.2 | async-start | bytes 786432 | tf_op jit(solution)/shard_map/all_to_all | solution.py:543
  136.8 3.9 %collective-permute-start.14 = (f32[2,64,384]{2,1,0:T(8,128)S(1)}, f32[2,64,384]{2,1,0:T(8,128)S(1)}, u32[]{:S(2)}, u32[]{:S(2)}) collective-permute-start(f32[2,64,384]{2,1,0:T(8,128)S(1)} %copy-done.13), channel_id=1, source_target_pairs={{0,16},{16,32},{32,48},{48,64},{64,80},{80,96},{96,112},{112,128},... | collective-permute-start | bytes 589832 | tf_op jit(solution)/shard_map/ppermute | solution.py:461
  140.7 1.9 %collective-permute-start.15 = (f32[2,64,384]{2,1,0:T(8,128)S(1)}, f32[2,64,384]{2,1,0:T(8,128)S(1)}, u32[]{:S(2)}, u32[]{:S(2)}) collective-permute-start(f32[2,64,384]{2,1,0:T(8,128)S(1)} %copy-done.12), channel_id=1, source_target_pairs={{16,0},{32,16},{48,32},{64,48},{80,64},{96,80},{112,96},{128,112},... | collective-permute-start | bytes 589832 | tf_op jit(solution)/shard_map/ppermute | solution.py:465
  142.6 7.5 %light.3 = (f32[1,5,640,128]{3,2,1,0:T(8,128)}, f32[8,128]{1,0:T(8,128)S(1)}) custom-call(f32[9,32]{1,0:T(8,128)S(1)} %concatenate.11.refs_0_, f32[2,4,128,128]{3,2,1,0:T(8,128)} %get-tuple-element.96.refs_1_.refs_8_), custom_call_target="tpu_custom_call" | custom-call | tf_op jit(solution)/shard_map/light/pallas_call | solution.py:443
  150.2 4.1 %collective-permute-start.18 = (f32[24,128]{1,0:T(8,128)S(1)}, f32[24,128]{1,0:T(8,128)S(1)}, u32[]{:S(2)}, u32[]{:S(2)}) collective-permute-start(f32[24,128]{1,0:T(8,128)S(1)} %share.3), channel_id=1, source_target_pairs={{0,40},{8,32},{32,8},{40,0},{1,41},{9,33},{33,9},{41,1},{2,42},{10... | collective-permute-start | bytes 36872 | tf_op jit(solution)/shard_map/ppermute | solution.py:470
  154.2 0.7 collective-permute-start.16
  154.9 0.4 collective-permute-done.18
  155.3 3.0 %collective-permute-done.17 = f32[24,128]{1,0:T(8,128)S(1)} collective-permute-done((f32[24,128]{1,0:T(8,128)S(1)}, f32[24,128]{1,0:T(8,128)S(1)}, u32[]{:S(2)}, u32[]{:S(2)}) %collective-permute-start.17) | collective-permute-done | bytes 12320 | tf_op jit(solution)/shard_map/ppermute | solution.py:470
  158.3 0.1 maximum_select_fusion
  158.4 0.8 broadcast_in_dim.5
  159.2 8.6 %all-to-all-start.3 = ((f32[32,24,128]{2,1,0:T(8,128)}), f32[32,24,128]{2,1,0:T(8,128)S(1)}, u32[]{:S(2)}, u32[]{:S(2)}) async-start(f32[32,24,128]{2,1,0:T(8,128)} %bitcast.17), calls=%async_computation.3 | async-start | bytes 786432 | tf_op jit(solution)/shard_map/all_to_all | solution.py:552
  167.8 2.3 %fold_inner.1 = (f32[2,256,384]{2,1,0:T(8,128)}, f32[256,128]{1,0:T(8,128)}, f32[256,128]{1,0:T(8,128)}) custom-call(f32[2,256,384]{2,1,0:T(8,128)} %get-tuple-element.84.refs_0_, f32[2,64,384]{2,1,0:T(8,128)} %copy-done.7, f32[2,64,384]{2,1,0:T(8,128)} %copy-done.8), custom_call_target="tpu_custom_call" | custom-call | tf_op jit(solution)/shard_map/fold_inner/pallas_call | solution.py:443
  170.1 3.1 %collective-permute-start.19 = (f32[256,128]{1,0:T(8,128)}, f32[256,128]{1,0:T(8,128)S(1)}, u32[]{:S(2)}, u32[]{:S(2)}) collective-permute-start(f32[256,128]{1,0:T(8,128)} %get-tuple-element.101), channel_id=1, source_target_pairs={{0,1},{1,2},{2,3},{3,4},{4,5},{5,6},{6,7},{7,8},{8,9},{9,10},{10,1... | collective-permute-start | bytes 393224 | tf_op jit(solution)/shard_map/ppermute | solution.py:461
  173.3 1.3 collective-permute-start.20
  174.6 3.1 %collective-permute-done.19.refs_3_ = f32[256,128]{1,0:T(8,128)S(1)} collective-permute-done((f32[256,128]{1,0:T(8,128)}, f32[256,128]{1,0:T(8,128)S(1)}, u32[]{:S(2)}, u32[]{:S(2)}) %collective-permute-start.19) | collective-permute-done | bytes 131104 | tf_op jit(solution)/shard_map/ppermute | solution.py:461
  177.7 3.5 %collective-permute-done.20.refs_4_ = f32[256,128]{1,0:T(8,128)S(1)} collective-permute-done((f32[256,128]{1,0:T(8,128)}, f32[256,128]{1,0:T(8,128)S(1)}, u32[]{:S(2)}, u32[]{:S(2)}) %collective-permute-start.20) | collective-permute-done | bytes 131104 | tf_op jit(solution)/shard_map/ppermute | solution.py:465
  181.2 4.5 %collective-permute-start.21 = (f32[768,128]{1,0:T(8,128)S(1)}, f32[768,128]{1,0:T(8,128)S(1)}, u32[]{:S(2)}, u32[]{:S(2)}) collective-permute-start(f32[768,128]{1,0:T(8,128)S(1)} %bitcast.29), channel_id=1, source_target_pairs={{0,16},{16,0},{1,17},{17,1},{2,18},{18,2},{3,19},{19,3},{4,20},{20... | collective-permute-start | bytes 1179656 | tf_op jit(solution)/shard_map/ppermute | solution.py:470
  185.7 1.3 collective-permute-done.21.refs_7_
  187.1 4.4 %last_update.1 = (f32[2,256,256]{2,1,0:T(8,128)}, f32[2,4,128,128]{3,2,1,0:T(8,128)}) custom-call(s32[5]{0:T(128)S(1)} %stack.23.refs_1_.refs_0_, f32[2,3,384,128]{3,2,1,0:T(8,128)} %get-tuple-element.83.refs_1_, f32[2,256,384]{2,1,0:T(8,128)} %get-tuple-element.95.refs_2_, f32[256,128]{1,0:T(8,128)} %copy-done.9, f32[256,128]{1,0:T(8,128)} %copy-done.10, ...), custom_call_target="tpu_custom_call" | custom-call | tf_op jit(solution)/shard_map/last_update/pallas_call | solution.py:443
  (48 shorter events, 0.3 us)
Async XLA Ops:
  0.6 18.1 %copy-start.11 = (s32[1,1,16,2]{2,3,1,0:T(2,128)S(1)}, s32[1,1,16,2]{2,3,1,0:T(2,128)}, u32[]{:S(2)}) copy-start(s32[1,1,16,2]{2,3,1,0:T(2,128)} %param.8) | copy-start | bytes 388
  0.6 23.4 %copy-start = (f32[2,4,128,128]{3,2,1,0:T(8,128)S(1)}, f32[2,4,128,128]{3,2,1,0:T(8,128)}, u32[]{:S(2)}) copy-start(f32[2,4,128,128]{3,2,1,0:T(8,128)} %refs_11_) | copy-start | bytes 1572868
  2.6 8.9 %collective-permute-start.1 = (f32[2,72,256]{2,1,0:T(8,128)S(1)}, f32[2,72,256]{2,1,0:T(8,128)S(1)}, u32[]{:S(2)}, u32[]{:S(2)}) collective-permute-start(f32[2,72,256]{2,1,0:T(8,128)S(1)} %get-tuple-element.110), channel_id=1, source_target_pairs={{16,0},{32,16},{48,32},{64,48},{80,64},{96,80},{112,96},{128,112},... | collective-permute-start | bytes 442376 | tf_op jit(solution)/shard_map/ppermute | solution.py:465
  7.8 4.9 %collective-permute-start = (f32[2,72,256]{2,1,0:T(8,128)S(1)}, f32[2,72,256]{2,1,0:T(8,128)S(1)}, u32[]{:S(2)}, u32[]{:S(2)}) collective-permute-start(f32[2,72,256]{2,1,0:T(8,128)S(1)} %get-tuple-element.111), channel_id=1, source_target_pairs={{0,16},{16,32},{32,48},{48,64},{64,80},{80,96},{96,112},{112,128},... | collective-permute-start | bytes 442376 | tf_op jit(solution)/shard_map/ppermute | solution.py:461
  13.9 6.2 %collective-permute-start.2 = (f32[392,128]{1,0:T(8,128)S(1)}, f32[392,128]{1,0:T(8,128)S(1)}, u32[]{:S(2)}, u32[]{:S(2)}) collective-permute-start(f32[392,128]{1,0:T(8,128)S(1)} %get-tuple-element.56), channel_id=1, source_target_pairs={{0,1},{1,2},{2,3},{3,4},{4,5},{5,6},{6,7},{7,8},{8,9},{9,10},{10,1... | collective-permute-start | bytes 602120 | tf_op jit(solution)/shard_map/ppermute | solution.py:461
  17.4 6.6 %collective-permute-start.3 = (f32[392,128]{1,0:T(8,128)S(1)}, f32[392,128]{1,0:T(8,128)S(1)}, u32[]{:S(2)}, u32[]{:S(2)}) collective-permute-start(f32[392,128]{1,0:T(8,128)S(1)} %get-tuple-element.57), channel_id=1, source_target_pairs={{1,0},{2,1},{3,2},{4,3},{5,4},{6,5},{7,6},{8,7},{9,8},{10,9},{11,1... | collective-permute-start | bytes 602120 | tf_op jit(solution)/shard_map/ppermute | solution.py:465
  37.6 19.3 %copy-start.3 = (f32[2,128,384]{2,1,0:T(8,128)S(1)}, f32[2,128,384]{2,1,0:T(8,128)}, u32[]{:S(2)}) copy-start(f32[2,128,384]{2,1,0:T(8,128)} %get-tuple-element.62.refs_0_) | copy-start | bytes 1179652
  37.6 21.8 %copy-start.4 = (f32[2,128,384]{2,1,0:T(8,128)S(1)}, f32[2,128,384]{2,1,0:T(8,128)}, u32[]{:S(2)}) copy-start(f32[2,128,384]{2,1,0:T(8,128)} %get-tuple-element.63.refs_1_) | copy-start | bytes 1179652
  37.6 1.8 collective-permute-start.4
  40.2 31.3 %all-to-all-start = ((f32[32,24,128]{2,1,0:T(8,128)}), f32[32,24,128]{2,1,0:T(8,128)S(1)}, u32[]{:S(2)}, u32[]{:S(2)}) async-start(f32[32,24,128]{2,1,0:T(8,128)} %bitcast.7), calls=%async_computation | async-start | bytes 786432 | tf_op jit(solution)/shard_map/all_to_all | solution.py:543
  56.8 14.6 %collective-permute-start.6 = (f32[2,128,384]{2,1,0:T(8,128)S(1)}, f32[2,128,384]{2,1,0:T(8,128)S(1)}, u32[]{:S(2)}, u32[]{:S(2)}) collective-permute-start(f32[2,128,384]{2,1,0:T(8,128)S(1)} %copy-done.3), channel_id=1, source_target_pairs={{16,0},{32,16},{48,32},{64,48},{80,64},{96,80},{112,96},{128,112},... | collective-permute-start | bytes 1179656 | tf_op jit(solution)/shard_map/ppermute | solution.py:465
  59.4 12.1 %collective-permute-start.5 = (f32[2,128,384]{2,1,0:T(8,128)S(1)}, f32[2,128,384]{2,1,0:T(8,128)S(1)}, u32[]{:S(2)}, u32[]{:S(2)}) collective-permute-start(f32[2,128,384]{2,1,0:T(8,128)S(1)} %copy-done.4), channel_id=1, source_target_pairs={{0,16},{16,32},{32,48},{48,64},{64,80},{80,96},{96,112},{112,128},... | collective-permute-start | bytes 1179656 | tf_op jit(solution)/shard_map/ppermute | solution.py:461
  71.5 16.1 %copy-start.5 = (f32[2,128,384]{2,1,0:T(8,128)}, f32[2,128,384]{2,1,0:T(8,128)S(1)}, u32[]{:S(2)}) copy-start(f32[2,128,384]{2,1,0:T(8,128)S(1)} %collective-permute-done.6.refs_4_) | copy-start | bytes 1179652
  71.5 16.1 %copy-start.6 = (f32[2,128,384]{2,1,0:T(8,128)}, f32[2,128,384]{2,1,0:T(8,128)S(1)}, u32[]{:S(2)}) copy-start(f32[2,128,384]{2,1,0:T(8,128)S(1)} %collective-permute-done.5.refs_3_) | copy-start | bytes 1179652
  71.6 3.8 %collective-permute-start.9 = (f32[24,128]{1,0:T(8,128)S(1)}, f32[24,128]{1,0:T(8,128)S(1)}, u32[]{:S(2)}, u32[]{:S(2)}) collective-permute-start(f32[24,128]{1,0:T(8,128)S(1)} %share.2), channel_id=1, source_target_pairs={{0,40},{8,32},{32,8},{40,0},{1,41},{9,33},{33,9},{41,1},{2,42},{10... | collective-permute-start | bytes 36872 | tf_op jit(solution)/shard_map/ppermute | solution.py:470
  73.1 4.0 %collective-permute-start.8 = (f32[24,128]{1,0:T(8,128)S(1)}, f32[24,128]{1,0:T(8,128)S(1)}, u32[]{:S(2)}, u32[]{:S(2)}) collective-permute-start(f32[24,128]{1,0:T(8,128)S(1)} %share.2), channel_id=1, source_target_pairs={{0,32},{32,0},{1,33},{33,1},{2,34},{34,2},{3,35},{35,3},{4,36},{36... | collective-permute-start | bytes 36872 | tf_op jit(solution)/shard_map/ppermute | solution.py:470
  74.5 2.8 %collective-permute-start.7 = (f32[24,128]{1,0:T(8,128)S(1)}, f32[24,128]{1,0:T(8,128)S(1)}, u32[]{:S(2)}, u32[]{:S(2)}) collective-permute-start(f32[24,128]{1,0:T(8,128)S(1)} %share.2), channel_id=1, source_target_pairs={{0,8},{8,0},{1,9},{9,1},{2,10},{10,2},{3,11},{11,3},{4,12},{12,4},... | collective-permute-start | bytes 36872 | tf_op jit(solution)/shard_map/ppermute | solution.py:470
  78.2 26.3 %all-to-all-start.1 = ((f32[32,24,128]{2,1,0:T(8,128)}), f32[32,24,128]{2,1,0:T(8,128)S(1)}, u32[]{:S(2)}, u32[]{:S(2)}) async-start(f32[32,24,128]{2,1,0:T(8,128)} %bitcast.12), calls=%async_computation.1 | async-start | bytes 786432 | tf_op jit(solution)/shard_map/all_to_all | solution.py:552
  90.4 13.4 %collective-permute-start.10 = (f32[2,384,128]{2,1,0:T(8,128)}, f32[2,384,128]{2,1,0:T(8,128)S(1)}, u32[]{:S(2)}, u32[]{:S(2)}) collective-permute-start(f32[2,384,128]{2,1,0:T(8,128)} %get-tuple-element.76), channel_id=1, source_target_pairs={{0,1},{1,2},{2,3},{3,4},{4,5},{5,6},{6,7},{7,8},{8,9},{9,10},{10,1... | collective-permute-start | bytes 1179656 | tf_op jit(solution)/shard_map/ppermute | solution.py:461
  93.5 10.9 %collective-permute-start.11 = (f32[2,384,128]{2,1,0:T(8,128)}, f32[2,384,128]{2,1,0:T(8,128)S(1)}, u32[]{:S(2)}, u32[]{:S(2)}) collective-permute-start(f32[2,384,128]{2,1,0:T(8,128)} %get-tuple-element.77), channel_id=1, source_target_pairs={{1,0},{2,1},{3,2},{4,3},{5,4},{6,5},{7,6},{8,7},{9,8},{10,9},{11,1... | collective-permute-start | bytes 1179656 | tf_op jit(solution)/shard_map/ppermute | solution.py:465
  103.8 5.0 %copy-start.1 = (f32[2,384,128]{2,1,0:T(8,128)}, f32[2,384,128]{2,1,0:T(8,128)S(1)}, u32[]{:S(2)}) copy-start(f32[2,384,128]{2,1,0:T(8,128)S(1)} %collective-permute-done.10.refs_6_) | copy-start | bytes 1179652
  104.5 4.3 %copy-start.2 = (f32[2,384,128]{2,1,0:T(8,128)}, f32[2,384,128]{2,1,0:T(8,128)S(1)}, u32[]{:S(2)}) copy-start(f32[2,384,128]{2,1,0:T(8,128)S(1)} %collective-permute-done.11.refs_7_) | copy-start | bytes 1179652
  104.5 4.3 %collective-permute-start.12 = (f32[768,128]{1,0:T(8,128)S(1)}, f32[768,128]{1,0:T(8,128)S(1)}, u32[]{:S(2)}, u32[]{:S(2)}) collective-permute-start(f32[768,128]{1,0:T(8,128)S(1)} %bitcast.25), channel_id=1, source_target_pairs={{0,16},{16,0},{1,17},{17,1},{2,18},{18,2},{3,19},{19,3},{4,20},{20... | collective-permute-start | bytes 1179656 | tf_op jit(solution)/shard_map/ppermute | solution.py:470
  124.2 12.5 %copy-start.13 = (f32[2,64,384]{2,1,0:T(8,128)S(1)}, f32[2,64,384]{2,1,0:T(8,128)}, u32[]{:S(2)}) copy-start(f32[2,64,384]{2,1,0:T(8,128)} %get-tuple-element.91) | copy-start | bytes 589828
  124.3 16.4 %copy-start.12 = (f32[2,64,384]{2,1,0:T(8,128)S(1)}, f32[2,64,384]{2,1,0:T(8,128)}, u32[]{:S(2)}) copy-start(f32[2,64,384]{2,1,0:T(8,128)} %get-tuple-element.92) | copy-start | bytes 589828
  124.3 2.0 %collective-permute-start.13 = (f32[768,128]{1,0:T(8,128)S(1)}, f32[768,128]{1,0:T(8,128)S(1)}, u32[]{:S(2)}, u32[]{:S(2)}) collective-permute-start(f32[768,128]{1,0:T(8,128)S(1)} %get-tuple-element.86), channel_id=1, source_target_pairs={{0,16},{16,0},{1,17},{17,1},{2,18},{18,2},{3,19},{19,3},{4,20},{20... | collective-permute-start | bytes 1179656 | tf_op jit(solution)/shard_map/ppermute | solution.py:470
  127.1 23.0 %all-to-all-start.2 = ((f32[32,24,128]{2,1,0:T(8,128)}), f32[32,24,128]{2,1,0:T(8,128)S(1)}, u32[]{:S(2)}, u32[]{:S(2)}) async-start(f32[32,24,128]{2,1,0:T(8,128)} %bitcast.14), calls=%async_computation.2 | async-start | bytes 786432 | tf_op jit(solution)/shard_map/all_to_all | solution.py:543
  136.8 13.3 %collective-permute-start.14 = (f32[2,64,384]{2,1,0:T(8,128)S(1)}, f32[2,64,384]{2,1,0:T(8,128)S(1)}, u32[]{:S(2)}, u32[]{:S(2)}) collective-permute-start(f32[2,64,384]{2,1,0:T(8,128)S(1)} %copy-done.13), channel_id=1, source_target_pairs={{0,16},{16,32},{32,48},{48,64},{64,80},{80,96},{96,112},{112,128},... | collective-permute-start | bytes 589832 | tf_op jit(solution)/shard_map/ppermute | solution.py:461
  140.7 9.4 %collective-permute-start.15 = (f32[2,64,384]{2,1,0:T(8,128)S(1)}, f32[2,64,384]{2,1,0:T(8,128)S(1)}, u32[]{:S(2)}, u32[]{:S(2)}) collective-permute-start(f32[2,64,384]{2,1,0:T(8,128)S(1)} %copy-done.12), channel_id=1, source_target_pairs={{16,0},{32,16},{48,32},{64,48},{80,64},{96,80},{112,96},{128,112},... | collective-permute-start | bytes 589832 | tf_op jit(solution)/shard_map/ppermute | solution.py:465
  150.1 17.7 %copy-start.7 = (f32[2,64,384]{2,1,0:T(8,128)}, f32[2,64,384]{2,1,0:T(8,128)S(1)}, u32[]{:S(2)}) copy-start(f32[2,64,384]{2,1,0:T(8,128)S(1)} %collective-permute-done.14.refs_1_) | copy-start | bytes 589828
  150.1 17.7 %copy-start.8 = (f32[2,64,384]{2,1,0:T(8,128)}, f32[2,64,384]{2,1,0:T(8,128)S(1)}, u32[]{:S(2)}) copy-start(f32[2,64,384]{2,1,0:T(8,128)S(1)} %collective-permute-done.15.refs_2_) | copy-start | bytes 589828
  150.2 5.2 %collective-permute-start.18 = (f32[24,128]{1,0:T(8,128)S(1)}, f32[24,128]{1,0:T(8,128)S(1)}, u32[]{:S(2)}, u32[]{:S(2)}) collective-permute-start(f32[24,128]{1,0:T(8,128)S(1)} %share.3), channel_id=1, source_target_pairs={{0,40},{8,32},{32,8},{40,0},{1,41},{9,33},{33,9},{41,1},{2,42},{10... | collective-permute-start | bytes 36872 | tf_op jit(solution)/shard_map/ppermute | solution.py:470
  154.2 4.0 %collective-permute-start.17 = (f32[24,128]{1,0:T(8,128)S(1)}, f32[24,128]{1,0:T(8,128)S(1)}, u32[]{:S(2)}, u32[]{:S(2)}) collective-permute-start(f32[24,128]{1,0:T(8,128)S(1)} %share.3), channel_id=1, source_target_pairs={{0,32},{32,0},{1,33},{33,1},{2,34},{34,2},{3,35},{35,3},{4,36},{36... | collective-permute-start | bytes 36872 | tf_op jit(solution)/shard_map/ppermute | solution.py:470
  154.2 4.0 %collective-permute-start.16 = (f32[24,128]{1,0:T(8,128)S(1)}, f32[24,128]{1,0:T(8,128)S(1)}, u32[]{:S(2)}, u32[]{:S(2)}) collective-permute-start(f32[24,128]{1,0:T(8,128)S(1)} %share.3), channel_id=1, source_target_pairs={{0,8},{8,0},{1,9},{9,1},{2,10},{10,2},{3,11},{11,3},{4,12},{12,4},... | collective-permute-start | bytes 36872 | tf_op jit(solution)/shard_map/ppermute | solution.py:470
  159.2 22.0 %all-to-all-start.3 = ((f32[32,24,128]{2,1,0:T(8,128)}), f32[32,24,128]{2,1,0:T(8,128)S(1)}, u32[]{:S(2)}, u32[]{:S(2)}) async-start(f32[32,24,128]{2,1,0:T(8,128)} %bitcast.17), calls=%async_computation.3 | async-start | bytes 786432 | tf_op jit(solution)/shard_map/all_to_all | solution.py:552
  170.1 7.5 %collective-permute-start.19 = (f32[256,128]{1,0:T(8,128)}, f32[256,128]{1,0:T(8,128)S(1)}, u32[]{:S(2)}, u32[]{:S(2)}) collective-permute-start(f32[256,128]{1,0:T(8,128)} %get-tuple-element.101), channel_id=1, source_target_pairs={{0,1},{1,2},{2,3},{3,4},{4,5},{5,6},{6,7},{7,8},{8,9},{9,10},{10,1... | collective-permute-start | bytes 393224 | tf_op jit(solution)/shard_map/ppermute | solution.py:461
  173.3 7.9 %collective-permute-start.20 = (f32[256,128]{1,0:T(8,128)}, f32[256,128]{1,0:T(8,128)S(1)}, u32[]{:S(2)}, u32[]{:S(2)}) collective-permute-start(f32[256,128]{1,0:T(8,128)} %get-tuple-element.102), channel_id=1, source_target_pairs={{1,0},{2,1},{3,2},{4,3},{5,4},{6,5},{7,6},{8,7},{9,8},{10,9},{11,1... | collective-permute-start | bytes 393224 | tf_op jit(solution)/shard_map/ppermute | solution.py:465
  177.7 9.4 %copy-start.9 = (f32[256,128]{1,0:T(8,128)}, f32[256,128]{1,0:T(8,128)S(1)}, u32[]{:S(2)}) copy-start(f32[256,128]{1,0:T(8,128)S(1)} %collective-permute-done.19.refs_3_) | copy-start | bytes 393220
  181.2 5.9 %copy-start.10 = (f32[256,128]{1,0:T(8,128)}, f32[256,128]{1,0:T(8,128)S(1)}, u32[]{:S(2)}) copy-start(f32[256,128]{1,0:T(8,128)S(1)} %collective-permute-done.20.refs_4_) | copy-start | bytes 393220
  181.2 5.9 %collective-permute-start.21 = (f32[768,128]{1,0:T(8,128)S(1)}, f32[768,128]{1,0:T(8,128)S(1)}, u32[]{:S(2)}, u32[]{:S(2)}) collective-permute-start(f32[768,128]{1,0:T(8,128)S(1)} %bitcast.29), channel_id=1, source_target_pairs={{0,16},{16,0},{1,17},{17,1},{2,18},{18,2},{3,19},{19,3},{4,20},{20... | collective-permute-start | bytes 1179656 | tf_op jit(solution)/shard_map/ppermute | solution.py:470

commit v3 on v2

v3 whole, which is shorter than its diff:
```python
import functools

import jax
import jax.numpy as jnp
import numpy as np
from jax import lax
from jax.experimental import pallas as pl
from jax.experimental.pallas import tpu as pltpu
from jax.sharding import Mesh, PartitionSpec as P

ITERS = 2
BATCH = 4
SPLIT = (("y", 4), ("xh", 2), ("core", 2), ("xl", 2), ("z", 8))
ROW = ("y", "xh", "core")
COL = ("xl", "z")
RING = ("y", "z")
PARTS = 32
CHUNK = 24
DATA = 18

VM = pl.BlockSpec(memory_space=pltpu.VMEM)
SM = pl.BlockSpec(memory_space=pltpu.SMEM)
F32 = jnp.float32
SPOTS = pltpu.SMEM((9 * 16 + 4, 2), jnp.int32)


def dft_pair(n):
    index = np.arange(n)
    angle = (index[:, None] * index[None, :] % n) * (2.0 * np.pi / n)
    c = np.cos(angle) / np.sqrt(n)
    s = np.sin(angle) / np.sqrt(n)
    forward = np.block([[c, s], [-s, c]])
    backward = np.block([[c, -s], [s, c]])
    return jnp.asarray(forward, jnp.bfloat16), jnp.asarray(backward, jnp.bfloat16)


def ordered(odd, first, second):
    return jnp.where(odd, first, second), jnp.where(odd, second, first)


def total(values):
    return functools.reduce(jnp.add, values)


def place(canvas, ch, where, lane, value):
    u, k, s = where
    n = value.shape[0]
    rolled = pltpu.roll(value, s, 1)
    canvas[ch, k, pl.ds(u, n), :] += jnp.where(lane >= s, rolled, 0.0)
    canvas[ch, k + 1, pl.ds(u, n), :] += jnp.where(lane >= s, 0.0, rolled)


def sweep_positions(copies, off_ref, probe_ref, meas_ref, fwd_ref, bwd_ref, cells, canvas, grads):
    modes = probe_ref.shape[1]
    n = probe_ref.shape[2]
    grads[...] = jnp.zeros_like(grads)
    lane = lax.broadcasted_iota(jnp.int32, (n, n), 1)

    def window(ch, where):
        u, k, s = where
        left = cells[ch, k, pl.ds(u, n), :]
        right = cells[ch, k + 1, pl.ds(u, n), :]
        return pltpu.roll(jnp.where(lane >= s, left, right), n - s, 1)

    def transform(field, left, right):
        sec = jnp.dot(left, field, preferred_element_type=F32).astype(jnp.bfloat16)
        parts = [slice(m * n, (m + 1) * n) for m in range(modes)]
        rows = [jnp.concatenate([sec[:n, part], sec[n:, part]], 1) for part in parts]
        return jnp.dot(jnp.concatenate(rows, 0), right, preferred_element_type=F32)

    def paired(re_parts, im_parts):
        re_all = jnp.concatenate([x.astype(jnp.bfloat16) for x in re_parts], 1)
        im_all = jnp.concatenate([x.astype(jnp.bfloat16) for x in im_parts], 1)
        return jnp.concatenate([re_all, im_all], 0)

    def split(wave):
        return [(wave[m * n : (m + 1) * n, :n], wave[m * n : (m + 1) * n, n:]) for m in range(modes)]

    def spot(q):
        u = off_ref[q, 0]
        v = off_ref[q, 1]
        return u, v // n, lax.rem(v, n)

    def step(i, carry):
        copies.need_part(meas_ref, i)
        probes = [(probe_ref[0, m], probe_ref[1, m]) for m in range(modes)]
        spots = [spot(i * BATCH + j) for j in range(BATCH)]
        wins = [(window(0, where), window(1, where)) for where in spots]
        exits = []
        for w_re, w_im in wins:
            re_parts = [p_re * w_re - p_im * w_im for p_re, p_im in probes]
            im_parts = [p_re * w_im + p_im * w_re for p_re, p_im in probes]
            exits.append(paired(re_parts, im_parts))
        fars = [split(transform(x, fwd_ref[...], bwd_ref[...])) for x in exits]
        corrected = []
        for j, far in enumerate(fars):
            power = total([re * re + im * im for re, im in far])
            raised = power + 1.0
            root = lax.rsqrt(raised)
            root = root * (1.5 - 0.5 * raised * root * root)
            scale = meas_ref[i * BATCH + j] * root
            corrected.append(paired([re * scale for re, _ in far], [im * scale for _, im in far]))
        backs = [split(transform(x, bwd_ref[...], fwd_ref[...])) for x in corrected]
        for where, back in zip(spots, backs):
            place(canvas, 0, where, lane, total([p[0] * b[0] + p[1] * b[1] for p, b in zip(probes, back)]))
            place(canvas, 1, where, lane, total([p[0] * b[1] - p[1] * b[0] for p, b in zip(probes, back)]))
        for m in range(modes):
            pairs = [(w, back[m]) for w, back in zip(wins, backs)]
            grads[m] += total([w[0] * b[0] + w[1] * b[1] for w, b in pairs])
            grads[modes + m] += total([w[0] * b[1] - w[1] * b[0] for w, b in pairs])
        grads[2 * modes] += total([w[0] * w[0] + w[1] * w[1] for w in wins])
        return carry

    lax.fori_loop(0, meas_ref.shape[0] // BATCH, step, 0)


def pack_half(grads, half, out_ref):
    planes = grads.shape[0]
    out_ref[...] = jnp.zeros_like(out_ref)
    for c in range(planes):
        for t in range(2):
            out_ref[pl.ds(2 * c + t, PARTS, stride=CHUNK), :] = grads[
                c, pl.ds(half * 2 * PARTS + t, PARTS, stride=2), :
            ]


def unpack_half(in_ref, half, grads):
    planes = grads.shape[0]
    for c in range(planes):
        for t in range(2):
            grads[c, pl.ds(half * 2 * PARTS + t, PARTS, stride=2), :] = in_ref[
                pl.ds(2 * c + t, PARTS, stride=CHUNK), :
            ]


def finish(copies, at_ref, canvas, grads, first_ref, second_ref, mid_ref, keep_ref, send_ref):
    band = first_ref.shape[2]
    far = canvas.shape[2] - band
    low = (1 - at_ref[5]) * far
    copies.send(canvas.at[:, :, pl.ds(pl.multiple_of(low, 8), band)], first_ref)
    copies.send(canvas.at[:, :, pl.ds(pl.multiple_of(far - low, 8), band)], second_ref)
    copies.send(canvas.at[:, :, band : band + mid_ref.shape[2]], mid_ref)
    for core in range(2):

        @pl.when(at_ref[0] == core)
        def _():
            pack_half(grads, core, keep_ref)
            pack_half(grads, 1 - core, send_ref)


def brightness(probe_ref):
    return jnp.sum(probe_ref[0] * probe_ref[0] + probe_ref[1] * probe_ref[1], axis=0)


def join_rows_kernel(
    copies, at_ref, obj_ref, row_a_ref, row_b_ref, tag_ref, tall_ref, col_a_ref, col_b_ref, tags_ref
):
    band = row_a_ref.shape[1] - 8
    size = obj_ref.shape[1]
    n = col_a_ref.shape[1]
    extent = tall_ref.shape[1]
    upper, lower = ordered(at_ref[5] == 1, row_a_ref[...], row_b_ref[...])
    tall_ref[:, :band] = upper[:, :band]
    tall_ref[:, band + size :] = lower[:, :band]
    tags_ref[...] = jnp.zeros_like(tags_ref)
    tags_ref[:1] = upper[0, band : band + 1, :n]
    tags_ref[1:2] = tag_ref[:1]
    tags_ref[2:3] = lower[0, band : band + 1, :n]
    copies.need(obj_ref)
    tall_ref[:, band : band + size] = obj_ref[...]
    lane = lax.broadcasted_iota(jnp.int32, (extent, n), 1)
    left = jnp.where(lane < band, tall_ref[0, :, :n], pltpu.roll(tall_ref[1, :, :n], band, 1))
    right = jnp.where(lane < band, pltpu.roll(tall_ref[0, :, size - n :], band, 1), tall_ref[1, :, size - n :])
    col_a_ref[:extent], col_b_ref[:extent] = ordered(at_ref[6] == 1, left, right)
    col_a_ref[extent:] = tags_ref[...]
    col_b_ref[extent:] = tags_ref[...]


def first_kernel(
    copies, off_ref, at_ref, tall_ref, col_a_ref, col_b_ref, probe_ref, meas_ref, fwd_ref, bwd_ref,
    first_ref, second_ref, mid_ref, keep_ref, send_ref, cells, bright_ref, canvas, grads,
):
    n = probe_ref.shape[2]
    half = n // 2
    extent = tall_ref.shape[1]
    lane = lax.broadcasted_iota(jnp.int32, (extent, n), 1)
    canvas[...] = jnp.zeros_like(canvas)
    bright_ref[...] = brightness(probe_ref)
    copies.ready(bright_ref)
    before, after = ordered(at_ref[6] == 1, col_a_ref[:extent], col_b_ref[:extent])
    strips = [
        (before, pltpu.roll(after, half, 1)),
        (pltpu.roll(before, half, 1), after),
    ]
    for ch in range(2):
        inner = [pltpu.roll(tall_ref[ch, :, k * n : (k + 1) * n], half, 1) for k in range(2)]
        row = [strips[ch][0], *inner, strips[ch][1]]
        for k in range(3):
            cells[ch, k] = jnp.where(lane < half, row[k], row[k + 1])
    copies.ready(cells)
    copies.need(fwd_ref, bwd_ref)
    sweep_positions(copies, off_ref, probe_ref, meas_ref, fwd_ref, bwd_ref, cells, canvas, grads)
    finish(copies, at_ref, canvas, grads, first_ref, second_ref, mid_ref, keep_ref, send_ref)


def light_peak(mine_ref, other_ref):
    best = [jnp.max(ref[pl.ds(DATA, PARTS, stride=CHUNK), :]) for ref in (mine_ref, other_ref)]
    return jnp.maximum(best[0], best[1])


def update_probes(at_ref, mine_ref, other_ref, probe_ref, grads, new_probe_ref):
    modes = probe_ref.shape[1]
    for core in range(2):

        @pl.when(at_ref[0] == core)
        def _():
            unpack_half(mine_ref, core, grads)
            unpack_half(other_ref, 1 - core, grads)

    density = grads[2 * modes]
    scale = 1.0 / (density + 0.1 * jnp.max(density))
    for part in range(2):
        for m in range(modes):
            old = probe_ref[part, m]
            new_probe_ref[part, m] = old + (grads[part * modes + m] - old * density) * scale


def updated(old, sums, light, peak):
    scale = 1.0 / (light + 0.1 * peak)
    return [old[ch] + (sums[ch] - old[ch] * light) * scale for ch in range(2)]


def next_kernel(
    copies, off_ref, at_ref, obj_ref, top_ref, mid_ref, low_ref, col_a_ref, col_b_ref, light_ref,
    mine_ref, other_ref, probe_ref, meas_ref, fwd_ref, bwd_ref,
    first_ref, second_ref, new_mid_ref, keep_ref, send_ref, new_obj_ref, bright_ref, new_probe_ref,
    canvas, grads,
):
    n = probe_ref.shape[2]
    blocks = obj_ref.shape[1]
    canvas[...] = jnp.zeros_like(canvas)
    peak = light_peak(mine_ref, other_ref)
    copies.need(probe_ref)
    update_probes(at_ref, mine_ref, other_ref, probe_ref, grads, new_probe_ref)
    copies.ready(new_probe_ref)
    bright_ref[...] = brightness(new_probe_ref)
    copies.ready(bright_ref)
    copies.need(obj_ref, top_ref, mid_ref, low_ref, col_a_ref, col_b_ref, light_ref)
    for j, ref in enumerate((top_ref, mid_ref, low_ref)):
        rows = slice(j * n, (j + 1) * n)
        row = lax.broadcasted_iota(jnp.int32, (n, n), 0) + j * n
        row_ok = (row >= at_ref[1]) & (row < at_ref[2])
        for k in range(blocks):
            col = lax.broadcasted_iota(jnp.int32, (n, n), 1) + k * n
            inside = row_ok & (col >= at_ref[3]) & (col < at_ref[4])
            sums = ref[:, k]
            if k in (0, blocks - 1):
                sides = ordered(at_ref[6] == 1, col_a_ref[:, rows], col_b_ref[:, rows])
                sums = sums + sides[k > 0]
            new = updated(obj_ref[:, k, rows], sums, light_ref[k, rows], peak)
            for ch in range(2):
                new_obj_ref[ch, k, rows] = jnp.where(inside, new[ch], 0.0)
    copies.ready(new_obj_ref)
    copies.need(fwd_ref, bwd_ref)
    sweep_positions(copies, off_ref, new_probe_ref, meas_ref, fwd_ref, bwd_ref, new_obj_ref, canvas, grads)
    finish(copies, at_ref, canvas, grads, first_ref, second_ref, new_mid_ref, keep_ref, send_ref)


def last_kernel(
    copies, at_ref, obj_ref, sums_ref, col_a_ref, col_b_ref, light_ref, mine_ref, other_ref, probe_ref,
    out_ref, new_probe_ref, grads,
):
    n = probe_ref.shape[2]
    half = n // 2
    blocks = obj_ref.shape[1]
    tile = out_ref.shape[1]
    inner = slice(half, half + tile)
    copies.need(probe_ref)
    update_probes(at_ref, mine_ref, other_ref, probe_ref, grads, new_probe_ref)
    copies.ready(new_probe_ref)
    copies.need(obj_ref, sums_ref, col_a_ref, col_b_ref, light_ref)
    left, right = ordered(at_ref[6] == 1, col_a_ref[...], col_b_ref[...])
    peak = light_peak(mine_ref, other_ref)
    lane = lax.broadcasted_iota(jnp.int32, (tile, n), 1)
    rolled = []
    for k in range(blocks):
        sums = [sums_ref[ch, k] for ch in range(2)]
        if k == 0:
            sums[0] = sums[0] + jnp.where(lane < half, 0.0, left)
            sums[1] = sums[1] + jnp.where(lane < half, 0.0, pltpu.roll(left, half, 1))
        elif k == blocks - 1:
            sums[0] = sums[0] + jnp.where(lane < half, right, 0.0)
            sums[1] = sums[1] + jnp.where(lane < half, pltpu.roll(right, half, 1), 0.0)
        new = updated(obj_ref[:, k, inner], sums, light_ref[k, inner], peak)
        rolled.append([pltpu.roll(x, half, 1) for x in new])
    for k in range(blocks - 1):
        for ch in range(2):
            out_ref[ch, :, k * n : (k + 1) * n] = jnp.where(lane < half, rolled[k][ch], rolled[k + 1][ch])
    copies.ready(out_ref)


def fold_kernel(
    copies, at_ref, first_ref, second_ref, mid_ref, row_a_ref, row_b_ref, top_ref, low_ref, col_a_ref, col_b_ref
):
    n = col_a_ref.shape[2]
    last = top_ref.shape[1] - 1
    copies.need(first_ref, second_ref, mid_ref, row_a_ref, row_b_ref)
    top_ref[...], low_ref[...] = ordered(
        at_ref[5] == 1, first_ref[...] + row_a_ref[...], second_ref[...] + row_b_ref[...]
    )
    for j, ref in enumerate((top_ref, mid_ref, low_ref)):
        rows = slice(j * n, (j + 1) * n)
        col_a_ref[:, rows], col_b_ref[:, rows] = ordered(at_ref[6] == 1, ref[:, 0], ref[:, last])
    copies.ready(col_a_ref, col_b_ref, top_ref, low_ref)


def fold_inner_kernel(copies, at_ref, mid_ref, row_a_ref, row_b_ref, sums_ref, col_a_ref, col_b_ref):
    n = col_a_ref.shape[1]
    band = row_a_ref.shape[2]
    tile = mid_ref.shape[2]
    last = mid_ref.shape[1] - 1
    copies.need(mid_ref, row_a_ref, row_b_ref)
    upper, lower = ordered(at_ref[5] == 1, row_a_ref[...], row_b_ref[...])
    sums_ref[:, :, :band] = mid_ref[:, :, :band] + upper
    sums_ref[:, :, band : tile - band] = mid_ref[:, :, band : tile - band]
    sums_ref[:, :, tile - band :] = mid_ref[:, :, tile - band :] + lower
    lane = lax.broadcasted_iota(jnp.int32, (tile, n), 1)
    left = jnp.where(lane < band, sums_ref[0, 0], pltpu.roll(sums_ref[1, 0], band, 1))
    right = jnp.where(lane < band, pltpu.roll(sums_ref[1, last], band, 1), sums_ref[0, last])
    col_a_ref[...], col_b_ref[...] = ordered(at_ref[6] == 1, left, right)
    copies.ready(col_a_ref, col_b_ref, sums_ref)


def place_lights(tag_ref, bright_ref, canvas, spots, rim, tile):
    n = bright_ref.shape[1]
    half = n // 2
    group = 4
    lane = lax.broadcasted_iota(jnp.int32, (n, n), 1)
    count = jnp.int32(0)
    for t in range(9):
        if rim and t == 4:
            continue
        down, across = t % 3 - 1, t // 3 - 1

        def gather(p, count):
            u = tag_ref[t, 2 * p]
            v = tag_ref[t, 2 * p + 1]
            held = u > 0
            u = u + (n - 1 + down * tile)
            v = v + (n - 1 + across * tile)
            inner = (u > half) & (u < tile + n + half) & (v > half) & (v < tile + n + half)
            if rim:
                held = held & ~inner & (u > 0) & (u < tile + 2 * n) & (v > 0) & (v < tile + 2 * n)
            else:
                held = held & inner
            spots[count, 0] = u
            spots[count, 1] = v
            return count + held.astype(jnp.int32)

        count = lax.fori_loop(0, tag_ref.shape[1] // 2, gather, count, unroll=16)
    for j in range(group):
        spots[count + j, 0] = 0
        spots[count + j, 1] = 0
    canvas[...] = jnp.zeros_like(canvas)
    value = bright_ref[...]

    def step(i, carry):
        held = []
        for j in range(group):
            u = spots[i * group + j, 0]
            v = spots[i * group + j, 1]
            s = lax.rem(v, n)
            held.append((u, v // n, s, pltpu.roll(value, s, 1)))
        for u, k, s, rolled in held:
            canvas[k, pl.ds(u, n), :] += jnp.where(lane >= s, rolled, 0.0)
            canvas[k + 1, pl.ds(u, n), :] += jnp.where(lane >= s, 0.0, rolled)
        return carry

    lax.fori_loop(0, (count + group - 1) // group, step, 0)


def light_kernel(copies, tag_ref, bright_ref, light_ref, peak_ref, canvas, spots):
    n = bright_ref.shape[1]
    half = n // 2
    blocks, extent = light_ref.shape[:2]
    copies.need(bright_ref)
    place_lights(tag_ref, bright_ref, canvas, spots, False, extent - n)
    light_ref[...] = canvas[1 : 1 + blocks, n : n + extent]
    copies.ready(light_ref)
    lane = lax.broadcasted_iota(jnp.int32, (extent - n, n), 1)
    best = None
    for k in range(blocks):
        mine = light_ref[k, half : extent - half]
        if k == 0:
            mine = jnp.where(lane >= half, mine, 0.0)
        elif k == blocks - 1:
            mine = jnp.where(lane < half, mine, 0.0)
        best = mine if best is None else jnp.maximum(best, mine)
    peak_ref[...] = jnp.full(peak_ref.shape, jnp.max(best), F32)


def more_light_kernel(copies, tag_ref, bright_ref, light_ref, all_ref, canvas, spots):
    n = bright_ref.shape[1]
    blocks, extent = light_ref.shape[:2]
    copies.need(bright_ref)
    place_lights(tag_ref, bright_ref, canvas, spots, True, extent - n)
    copies.need(light_ref)
    all_ref[...] = light_ref[...] + canvas[1 : 1 + blocks, n : n + extent]
    copies.ready(all_ref)


def share_kernel(copies, parts_ref, peak_ref, out_ref):
    share = parts_ref[:CHUNK]
    for s in range(1, PARTS):
        share = share + parts_ref[s * CHUNK : (s + 1) * CHUNK]
    row = lax.broadcasted_iota(jnp.int32, share.shape, 0)
    out_ref[...] = jnp.where(row < DATA, share, peak_ref[:1])


class Far:
    def __init__(self, value, parts=1):
        self.value = value
        self.parts = parts


class Raw(Far):
    pass


class Copies:
    def __init__(self):
        self.ins = {}
        self.outs = {}
        self.sems = {}
        self.sent = []

    def need(self, *refs):
        for ref in refs:
            copy = self.ins.pop(id(ref), None)
            if copy is not None:
                copy(0).wait()

    def need_part(self, ref, i):
        if id(ref) in self.ins:
            self.ins[id(ref)](i).wait()

    def ready(self, *refs):
        for ref in refs:
            copy = self.outs.get(id(ref))
            if copy is not None:
                copy.start()
                self.sent.append(copy)

    def send(self, local, remote):
        copy = pltpu.make_async_copy(local, remote, self.sems[id(remote)])
        copy.start()
        self.sent.append(copy)


def part_copy(remote, local, sems, first, parts):
    size = local.shape[0] // parts

    def copy(i):
        rows = pl.ds(i * size, size)
        return pltpu.make_async_copy(remote.at[rows], local.at[rows], sems.at[first + i])

    return copy


def call(kernel, outs, scratch, args, scalars, name, limit=24):
    info = list(args) + list(outs)
    split = len(args)
    values = [x.value if isinstance(x, Far) else x for x in info]
    far = [isinstance(x, Far) for x in info]
    raw = [isinstance(x, Raw) for x in info]
    buffers, sem_at, count = [], {}, 0
    for i, value in enumerate(values):
        if far[i]:
            sem_at[i] = count
            count += info[i].parts
            if not raw[i]:
                buffers.append(pltpu.VMEM(value.shape, value.dtype) if i < split else pltpu.VMEM(value, F32))

    def whole(*refs):
        sems = refs[-1]
        refs = list(refs[:-1])
        spare = iter(refs[len(info) : len(info) + len(buffers)])
        rest = refs[len(info) + len(buffers) :]
        copies = Copies()
        for i in sem_at:
            first = sem_at[i]
            if raw[i]:
                copies.sems[id(refs[i])] = sems.at[first]
                continue
            remote, local = refs[i], next(spare)
            refs[i] = local
            if i < split:
                copies.ins[id(local)] = part_copy(remote, local, sems, first, info[i].parts)
                for j in range(info[i].parts):
                    copies.ins[id(local)](j).start()
            else:
                copies.outs[id(local)] = pltpu.make_async_copy(local, remote, sems.at[first])
        kernel(copies, *refs[: len(info)], *rest)
        for copy in copies.sent:
            copy.wait()

    far_spec = pl.BlockSpec(memory_space=pltpu.HBM)
    specs = [SM if i < scalars else (far_spec if far[i] else VM) for i in range(len(info))]
    operands = [
        pltpu.with_memory_space_constraint(x, pltpu.HBM) if is_far else x for x, is_far in zip(values[:split], far)
    ]
    return pl.pallas_call(
        whole,
        out_shape=tuple(
            pltpu.HBM(x, F32) if is_far else jax.ShapeDtypeStruct(x, F32) for x, is_far in zip(values[split:], far[split:])
        ),
        in_specs=specs[:split],
        out_specs=tuple(specs[split:]),
        scratch_shapes=buffers
        + [x if x is SPOTS else pltpu.VMEM(x, F32) for x in scratch]
        + [pltpu.SemaphoreType.DMA((max(count, 1),))],
        compiler_params=pltpu.CompilerParams(vmem_limit_bytes=limit * 1024 * 1024),
        name=name,
    )(*operands)


def length(axes):
    return functools.reduce(lambda a, b: a * b, [lax.axis_size(axis) for axis in axes])


def exchange(first, second, axes):
    count = length(axes)
    first = lax.ppermute(first, axes, [(i, i ^ 1) for i in range(count)])
    pairs = [(i, i + 1) for i in range(1, count - 1, 2)]
    second = lax.ppermute(second, axes, pairs + [(j, i) for i, j in pairs])
    return first, second


def swap(value, axes):
    count = length(axes)
    return lax.ppermute(value, axes, [(i, count - 1 - i) for i in range(count)])


def share_over_x(share):
    near = swap(share, ("xl",))
    far = swap(share, ("xh",))
    cross = swap(share, ("xh", "xl"))
    at = lax.broadcasted_iota(jnp.int32, share.shape, 0)
    added = (share + near) + (far + cross)
    largest = jnp.maximum(jnp.maximum(share, near), jnp.maximum(far, cross))
    return jnp.where(at < DATA, added, largest)


def body(object_field, probe_modes, scan_offsets, measured):
    n = probe_modes.shape[-1]
    modes = probe_modes.shape[1]
    half = n // 2
    tile = object_field.shape[1]
    extent = tile + n
    blocks = extent // n
    positions = scan_offsets.shape[2]
    offsets = scan_offsets.reshape(positions, 2)
    amplitudes = measured.reshape(positions, n, n)
    tables = dft_pair(n)
    row = lax.axis_index(ROW)
    col = lax.axis_index(COL)
    info = jnp.stack(
        [
            lax.axis_index("core"),
            jnp.where(row == 0, half, 0),
            jnp.where(row == length(ROW) - 1, extent - half, extent),
            jnp.where(col == 0, half, 0),
            jnp.where(col == length(COL) - 1, extent - half, extent),
            row % 2,
            col % 2,
        ]
    ).astype(jnp.int32)

    tag = (offsets + 1).astype(F32).reshape(1, 2 * positions)
    tag_rows = jnp.pad(tag, ((0, 7), (0, n - 2 * positions)))
    tag_block = jnp.pad(tag[None], ((0, 1), (0, 7), (0, tile - 2 * positions)))
    low = (1 - row % 2) * (tile - half)
    first = lax.dynamic_slice_in_dim(object_field, low, half, 1)
    second = lax.dynamic_slice_in_dim(object_field, tile - half - low, half, 1)
    row_a, row_b = exchange(*(jnp.concatenate([x, tag_block], 1) for x in (first, second)), ROW)
    strip = (extent + 8, n)
    tall, col_a, col_b, own = call(
        join_rows_kernel,
        [(2, extent, tile), strip, strip, (8, n)],
        [],
        [info, Far(object_field), row_a, row_b, tag_rows],
        1,
        "join_rows",
    )
    col_a, col_b = exchange(col_a, col_b, COL)
    odd = col % 2 == 1
    before, after = ordered(odd, col_a[extent : extent + 3, :32], col_b[extent : extent + 3, :32])
    tags = jnp.concatenate([before, own[:3, :32], after], 0)
    tags = tags.astype(jnp.int32)

    cells = (2, blocks, extent, n)
    canvas = (blocks + 2, extent + 2 * n, n)
    lights = (blocks, extent, n)
    grads = (2 * modes + 1, n, n)
    packed = (PARTS * CHUNK, n)
    band = (2, blocks, n, n)
    probes = probe_modes
    tables = [Far(x) for x in tables]
    amplitudes = Far(amplitudes, positions // BATCH)
    for sweep in range(ITERS):
        last = sweep == ITERS - 1
        bands = [(2, blocks, x, n) for x in ((half, half, tile) if last else (n, n, n))]
        outs = [Raw(x) for x in bands] + [packed, packed, Far(cells), Far((n, n))]
        if sweep == 0:
            args = [offsets, info, tall, col_a, col_b, probes, amplitudes, *tables]
            first, second, mid, keep, send, cells_now, bright = call(first_kernel, outs, [cells, grads], args, 2, "first_sweep")
        else:
            held = [Far(x) for x in (cells_now, *sums, light)]
            args = [offsets, info, *held, mine, other, Far(probes), amplitudes, *tables]
            first, second, mid, keep, send, cells_now, bright, probes = call(
                next_kernel, outs + [Far(probes.shape)], [cells, grads], args, 2, "next_sweep"
            )
        received = swap(send, ("core",))
        received, first, second, bright = lax.optimization_barrier((received, first, second, bright))
        parts = lax.all_to_all(keep + received, RING, 0, 0, tiled=True)
        light, peak = call(light_kernel, [Far(lights), (8, n)], [canvas, SPOTS], [tags, Far(bright)], 1, "light")
        row_a, row_b = exchange(first, second, ROW)
        parts, row_a, row_b = lax.optimization_barrier((parts, row_a, row_b))
        share = call(share_kernel, [(CHUNK, n)], [], [parts, peak], 0, "share")[0]
        share = share_over_x(share)
        copies = jnp.broadcast_to(share[None], (PARTS,) + share.shape).reshape(packed)
        light, copies = lax.optimization_barrier((light, copies))
        mine = lax.all_to_all(copies, RING, 0, 0, tiled=True)
        if last:
            outs = [Far((2, blocks, tile, n)), Far((tile, n)), Far((tile, n))]
            args = [info] + [Far(x) for x in (mid, row_a, row_b)]
            sums, col_a, col_b = call(fold_inner_kernel, outs, [], args, 1, "fold_inner")
            sums = [sums]
        else:
            side = (2, extent, n)
            outs = [Far(x) for x in (band, band, side, side)]
            args = [info] + [Far(x) for x in (first, second, mid, row_a, row_b)]
            top, low, col_a, col_b = call(fold_kernel, outs, [], args, 1, "fold_rows")
            sums = [top, mid, low]
            args = [tags, Far(bright), Far(light)]
            light = call(more_light_kernel, [Far(lights)], [canvas, SPOTS], args, 1, "more_light")[0]
        col_a, col_b = exchange(col_a, col_b, COL)
        mine, col_a, col_b, light = lax.optimization_barrier((mine, col_a, col_b, light))
        sums += [col_a, col_b]
        other = swap(mine, ("core",))
    held = [Far(x) for x in (cells_now, *sums, light)]
    args = [info, *held, mine, other, Far(probes)]
    return call(last_kernel, [Far(object_field.shape), Far(probes.shape)], [grads], args, 1, "last_update")


def solution(mesh):
    names = tuple(name for name, _ in SPLIT)
    sizes = tuple(size for _, size in SPLIT)
    fine = Mesh(mesh.devices.reshape(sizes), names)
    return jax.shard_map(
        body,
        mesh=fine,
        in_specs=(
            P(None, ROW, COL),
            P(),
            P(ROW, COL, None, None),
            P(ROW, COL, None, None, None),
        ),
        out_specs=(P(None, ROW, COL), P()),
        check_vma=False,
    )
```

time: 193 us -> 179 us (0.927)
  starting transfers between devices: 95.2 us -> 81.1 us
  waiting for transfers between devices: 27.5 us -> 40.9 us
  Pallas kernels: 61.9 us -> 49.1 us
    ppermute x12, waiting for transfers between devices: 16 us -> 28.8 us  [the longest x6 18 us: exchange(): first = lax.ppermute(first, axes, [(i, i ^ 1) for i in range(count)])]
    pallas_call x11, Pallas kernels: 61.9 us -> 49.1 us  [call(): pl.pallas_call(whole, out_shape=tuple((pltpu.HBM(x, F32) if is_far else j...]
    ppermute x12, starting transfers between devices: 34.6 us -> 22.9 us  [the longest x6 16.9 us: exchange(): second = lax.ppermute(second, axes, pairs + [(j, i) for i, j in pairs])]
  transfers between devices with their start and end apart: 26 -> 26, of which waited for: 17 -> 15; matrix products, arithmetic and copies ran while one was open for 0% -> 0% of each run, Pallas kernels for 14% -> 11%
where the time goes in v3:
time: 179 us; the launch traced here: 178 us
  starting transfers between devices  81.1 us (45%)
  Pallas kernels  49.1 us (27%)
  waiting for transfers between devices  40.9 us (23%)
  local copies, waits for them, and re-layouts  3.06 us (2%)
  other arithmetic  2.51 us (1%)
    pallas_call x11, Pallas kernels, call(): pl.pallas_call(whole, out_shape=tuple((pltpu.HBM(x, F32) if is_far else j...  49.1 us
    all_to_all x2, starting transfers between devices, body(): parts = lax.all_to_all(keep + received, RING, 0, 0, tiled=True)  25.6 us
    ppermute x6, waiting for transfers between devices, exchange(): first = lax.ppermute(first, axes, [(i, i ^ 1) for i in range(count)])  18 us
    all_to_all x2, starting transfers between devices, body(): mine = lax.all_to_all(copies, RING, 0, 0, tiled=True)  17.7 us
    ppermute x6, starting transfers between devices, exchange(): second = lax.ppermute(second, axes, pairs + [(j, i) for i, j in pairs])  16.9 us
    ppermute x10, starting transfers between devices, swap(): return lax.ppermute(value, axes, [(i, count - 1 - i) for i in range(count)])  14.9 us
    ppermute x10, waiting for transfers between devices, swap(): return lax.ppermute(value, axes, [(i, count - 1 - i) for i in range(count)])  11.2 us
    ppermute x6, waiting for transfers between devices, exchange(): second = lax.ppermute(second, axes, pairs + [(j, i) for i, j in pairs])  10.8 us
  transfers between devices with their start and end apart: 26, of which 15 were waited for; matrix products, arithmetic and copies ran while one was open for 0% of the time, Pallas kernels for 11%

profile of v3, /device:TPU:1, one launch (start us, length us, event | category | flops | bytes accessed | tf_op | source)
XLA Modules:
  0.0 177.9 jit_solution(15399102016146653092)
XLA Ops:
  0.6 0.0 copy-start
  0.7 0.7 add_convert_fusion
  1.4 0.1 copy.12
  1.5 0.1 convert_element_type.31
  1.6 1.0 constant_dynamic-slice_fusion
  2.6 6.0 %collective-permute-start.1 = (f32[2,72,256]{2,1,0:T(8,128)S(1)}, f32[2,72,256]{2,1,0:T(8,128)S(1)}, u32[]{:S(2)}, u32[]{:S(2)}) collective-permute-start(f32[2,72,256]{2,1,0:T(8,128)S(1)} %get-tuple-element.118), channel_id=1, source_target_pairs={{16,32},{48,64},{80,96},{112,128},{144,160},{176,192},{208,224},{3... | collective-permute-start | bytes 442376 | tf_op jit(solution)/shard_map/ppermute | solution.py:535
  8.7 0.1 collective-permute-start
  8.8 0.1 convert_element_type.32
  8.9 0.1 stack.31.refs_0_.refs_1_
  9.0 3.1 %collective-permute-done.1.refs_3_ = f32[2,72,256]{2,1,0:T(8,128)S(1)} collective-permute-done((f32[2,72,256]{2,1,0:T(8,128)S(1)}, f32[2,72,256]{2,1,0:T(8,128)S(1)}, u32[]{:S(2)}, u32[]{:S(2)}) %collective-permute-start.1) | collective-permute-done | bytes 147488 | tf_op jit(solution)/shard_map/ppermute | solution.py:535
  12.2 1.8 join_rows.1
  13.9 1.7 collective-permute-start.2
  15.6 0.7 collective-permute-start.3
  16.3 0.1 copy.15.refs_0_
  16.4 2.9 %collective-permute-done.2.refs_3_ = f32[392,128]{1,0:T(8,128)S(1)} collective-permute-done((f32[392,128]{1,0:T(8,128)S(1)}, f32[392,128]{1,0:T(8,128)S(1)}, u32[]{:S(2)}, u32[]{:S(2)}) %collective-permute-start.2) | collective-permute-done | bytes 200736 | tf_op jit(solution)/shard_map/ppermute | solution.py:533
  19.3 11.0 %first_sweep.1 = (f32[2,3,128,128]{3,2,1,0:T(8,128)}, f32[2,3,128,128]{3,2,1,0:T(8,128)}, f32[2,3,128,128]{3,2,1,0:T(8,128)}, f32[768,128]{1,0:T(8,128)S(1)}, f3...) custom-call(s32[16,2]{1,0:T(8,128)S(1)} %copy.15.refs_0_, s32[7]{0:T(128)S(1)} %stack.31.refs_0_.refs_1_, ...), custom_call_target="tpu_custom_call" | custom-call | tf_op jit(solution)/shard_map/first_sweep/pallas_call | solution.py:512
  30.4 0.1 collective-permute-start.4
  30.5 1.7 collective-permute-done.4
  32.2 0.8 add.84
  33.0 17.4 %all-to-all-start = ((f32[32,24,128]{2,1,0:T(8,128)}), f32[32,24,128]{2,1,0:T(8,128)S(1)}, u32[]{:S(2)}, u32[]{:S(2)}) async-start(f32[32,24,128]{2,1,0:T(8,128)} %bitcast.9), calls=%async_computation | async-start | bytes 786432 | tf_op jit(solution)/shard_map/all_to_all | solution.py:625
  50.4 0.7 collective-permute-start.5
  51.1 5.5 %collective-permute-start.6 = (f32[2,3,128,128]{3,2,1,0:T(8,128)S(1)}, f32[2,3,128,128]{3,2,1,0:T(8,128)S(1)}, u32[]{:S(2)}, u32[]{:S(2)}) collective-permute-start(f32[2,3,128,128]{3,2,1,0:T(8,128)S(1)} %copy-done.4), channel_id=1, source_target_pairs={{16,32},{48,64},{80,96},{112,128},{144,160},{176,192},{208,224},{3... | collective-permute-start | bytes 1179656 | tf_op jit(solution)/shard_map/ppermute | solution.py:535
  56.7 4.3 %light.2 = (f32[3,384,128]{2,1,0:T(8,128)}, f32[8,128]{1,0:T(8,128)S(1)}) custom-call(s32[9,32]{1,0:T(8,128)S(1)} %maximum_convert_fusion.refs_0_, f32[128,128]{1,0:T(8,128)} %get-tuple-element.76.refs_1_), custom_call_target="tpu_custom_call" | custom-call | tf_op jit(solution)/shard_map/light/pallas_call | solution.py:512
  61.0 5.0 %collective-permute-done.6.refs_5_ = f32[2,3,128,128]{3,2,1,0:T(8,128)S(1)} collective-permute-done((f32[2,3,128,128]{3,2,1,0:T(8,128)S(1)}, f32[2,3,128,128]{3,2,1,0:T(8,128)S(1)}, u32[]{:S(2)}, u32[]{:S(2)}) %collective-permute-start.6) | collective-permute-done | bytes 393248 | tf_op jit(solution)/shard_map/ppermute | solution.py:535
  66.1 4.0 %collective-permute-start.9 = (f32[24,128]{1,0:T(8,128)S(1)}, f32[24,128]{1,0:T(8,128)S(1)}, u32[]{:S(2)}, u32[]{:S(2)}) collective-permute-start(f32[24,128]{1,0:T(8,128)S(1)} %share.2), channel_id=1, source_target_pairs={{0,40},{8,32},{32,8},{40,0},{1,41},{9,33},{33,9},{41,1},{2,42},{10... | collective-permute-start | bytes 36872 | tf_op jit(solution)/shard_map/ppermute | solution.py:541
  70.1 0.3 collective-permute-start.8
  70.4 0.3 collective-permute-start.7
  70.8 0.4 collective-permute-done.9
  71.2 3.0 %collective-permute-done.8 = f32[24,128]{1,0:T(8,128)S(1)} collective-permute-done((f32[24,128]{1,0:T(8,128)S(1)}, f32[24,128]{1,0:T(8,128)S(1)}, u32[]{:S(2)}, u32[]{:S(2)}) %collective-permute-start.8) | collective-permute-done | bytes 12320 | tf_op jit(solution)/shard_map/ppermute | solution.py:541
  74.1 0.1 maximum_select_fusion.1
  74.2 0.8 broadcast_in_dim.4
  75.0 9.0 %all-to-all-start.1 = ((f32[32,24,128]{2,1,0:T(8,128)}), f32[32,24,128]{2,1,0:T(8,128)S(1)}, u32[]{:S(2)}, u32[]{:S(2)}) async-start(f32[32,24,128]{2,1,0:T(8,128)} %bitcast.12), calls=%async_computation.1 | async-start | bytes 786432 | tf_op jit(solution)/shard_map/all_to_all | solution.py:633
  84.0 3.5 %fold_rows.1 = (f32[2,3,128,128]{3,2,1,0:T(8,128)}, f32[2,3,128,128]{3,2,1,0:T(8,128)}, f32[2,384,128]{2,1,0:T(8,128)}, f32[2,384,128]{2,1,0:T(8,128)}) custom-call(s32[7]{0:T(128)S(1)} %stack.31.refs_0_.refs_1_, f32[2,3,128,128]{3,2,1,0:T(8,128)} %get-tuple-element.66.refs_1_, f32[2,3,128,128]{3,2,1,0:T(8,128)} %get-tuple-element.67.refs_2_, ...), custom_call_target="tpu_custom_call" | custom-call | tf_op jit(solution)/shard_map/fold_rows/pallas_call | solution.py:512
  87.5 1.3 collective-permute-start.10
  88.8 0.7 collective-permute-start.11
  89.5 4.5 %more_light.1.refs_8_ = f32[3,384,128]{2,1,0:T(8,128)} custom-call(s32[9,32]{1,0:T(8,128)S(1)} %maximum_convert_fusion.refs_0_, f32[128,128]{1,0:T(8,128)} %get-tuple-element.76.refs_1_, f32[3,384,128]{2,1,0:T(8,128)} %get-tuple-element.83.refs_2_), custom_call_target="tpu_custom_call" | custom-call | tf_op jit(solution)/shard_map/more_light/pallas_call | solution.py:512
  94.0 8.3 %collective-permute-done.10.refs_6_ = f32[2,384,128]{2,1,0:T(8,128)S(1)} collective-permute-done((f32[2,384,128]{2,1,0:T(8,128)}, f32[2,384,128]{2,1,0:T(8,128)S(1)}, u32[]{:S(2)}, u32[]{:S(2)}) %collective-permute-start.10) | collective-permute-done | bytes 393248 | tf_op jit(solution)/shard_map/ppermute | solution.py:533
  102.3 1.5 collective-permute-start.12
  103.9 1.3 collective-permute-done.12.refs_10_
  105.2 12.6 %next_sweep.1 = (f32[2,3,64,128]{3,2,1,0:T(8,128)}, f32[2,3,64,128]{3,2,1,0:T(8,128)}, f32[2,3,256,128]{3,2,1,0:T(8,128)}, f32[768,128]{1,0:T(8,128)S(1)}, f32[7...) custom-call(s32[16,2]{1,0:T(8,128)S(1)} %copy.15.refs_0_, ...), custom_call_target="tpu_custom_call" | custom-call | tf_op jit(solution)/shard_map/next_sweep/pallas_call | solution.py:512
  117.8 0.5 collective-permute-start.13
  118.3 1.3 collective-permute-done.13
  119.7 0.8 add.88
  120.5 8.3 %all-to-all-start.2 = ((f32[32,24,128]{2,1,0:T(8,128)}), f32[32,24,128]{2,1,0:T(8,128)S(1)}, u32[]{:S(2)}, u32[]{:S(2)}) async-start(f32[32,24,128]{2,1,0:T(8,128)} %bitcast.14), calls=%async_computation.2 | async-start | bytes 786432 | tf_op jit(solution)/shard_map/all_to_all | solution.py:625
  128.7 0.7 collective-permute-start.14
  129.5 3.4 %collective-permute-start.15 = (f32[2,3,64,128]{3,2,1,0:T(8,128)S(1)}, f32[2,3,64,128]{3,2,1,0:T(8,128)S(1)}, u32[]{:S(2)}, u32[]{:S(2)}) collective-permute-start(f32[2,3,64,128]{3,2,1,0:T(8,128)S(1)} %copy-done.12), channel_id=1, source_target_pairs={{16,32},{48,64},{80,96},{112,128},{144,160},{176,192},{208,224},{3... | collective-permute-start | bytes 589832 | tf_op jit(solution)/shard_map/ppermute | solution.py:535
  132.9 4.3 %light.3 = (f32[3,384,128]{2,1,0:T(8,128)}, f32[8,128]{1,0:T(8,128)S(1)}) custom-call(s32[9,32]{1,0:T(8,128)S(1)} %maximum_convert_fusion.refs_0_, f32[128,128]{1,0:T(8,128)} %get-tuple-element.101.refs_1_), custom_call_target="tpu_custom_call" | custom-call | tf_op jit(solution)/shard_map/light/pallas_call | solution.py:512
  137.2 2.6 %collective-permute-done.15.refs_3_ = f32[2,3,64,128]{3,2,1,0:T(8,128)S(1)} collective-permute-done((f32[2,3,64,128]{3,2,1,0:T(8,128)S(1)}, f32[2,3,64,128]{3,2,1,0:T(8,128)S(1)}, u32[]{:S(2)}, u32[]{:S(2)}) %collective-permute-start.15) | collective-permute-done | bytes 196640 | tf_op jit(solution)/shard_map/ppermute | solution.py:535
  139.9 0.8 all-to-all-done.2
  140.8 1.4 collective-permute-start.18
  142.2 0.8 collective-permute-start.17
  143.0 1.1 collective-permute-start.16
  144.1 0.5 collective-permute-done.18
  144.6 1.6 collective-permute-done.17
  146.2 0.1 maximum_select_fusion
  146.3 0.8 broadcast_in_dim.5
  147.1 8.8 %all-to-all-start.3 = ((f32[32,24,128]{2,1,0:T(8,128)}), f32[32,24,128]{2,1,0:T(8,128)S(1)}, u32[]{:S(2)}, u32[]{:S(2)}) async-start(f32[32,24,128]{2,1,0:T(8,128)} %bitcast.17), calls=%async_computation.3 | async-start | bytes 786432 | tf_op jit(solution)/shard_map/all_to_all | solution.py:633
  155.9 2.9 %fold_inner.1 = (f32[2,3,256,128]{3,2,1,0:T(8,128)}, f32[256,128]{1,0:T(8,128)}, f32[256,128]{1,0:T(8,128)}) custom-call(s32[7]{0:T(128)S(1)} %stack.31.refs_0_.refs_1_, f32[2,3,256,128]{3,2,1,0:T(8,128)} %get-tuple-element.89.refs_1_, f32[2,3,64,128]{3,2,1,0:T(8,128)} %copy-done.7, f32[2,3,64,128]{3,2,1,0:T(8,128)} %copy-done.8), custom_call_target="tpu_custom_call" | custom-call | tf_op jit(solution)/shard_map/fold_inner/pallas_call | solution.py:512
  158.8 1.3 collective-permute-start.19
  160.1 0.7 collective-permute-start.20
  160.8 6.8 %collective-permute-done.19.refs_3_ = f32[256,128]{1,0:T(8,128)S(1)} collective-permute-done((f32[256,128]{1,0:T(8,128)}, f32[256,128]{1,0:T(8,128)S(1)}, u32[]{:S(2)}, u32[]{:S(2)}) %collective-permute-start.19) | collective-permute-done | bytes 131104 | tf_op jit(solution)/shard_map/ppermute | solution.py:533
  167.6 4.8 %collective-permute-start.21 = (f32[768,128]{1,0:T(8,128)S(1)}, f32[768,128]{1,0:T(8,128)S(1)}, u32[]{:S(2)}, u32[]{:S(2)}) collective-permute-start(f32[768,128]{1,0:T(8,128)S(1)} %bitcast.25), channel_id=1, source_target_pairs={{0,16},{16,0},{1,17},{17,1},{2,18},{18,2},{3,19},{19,3},{4,20},{20... | collective-permute-start | bytes 1179656 | tf_op jit(solution)/shard_map/ppermute | solution.py:541
  172.3 1.3 collective-permute-done.21.refs_7_
  173.7 4.1 %last_update.1 = (f32[2,256,256]{2,1,0:T(8,128)}, f32[2,4,128,128]{3,2,1,0:T(8,128)}) custom-call(s32[7]{0:T(128)S(1)} %stack.31.refs_0_.refs_1_, f32[2,3,384,128]{3,2,1,0:T(8,128)} %get-tuple-element.88.refs_1_, f32[2,3,256,128]{3,2,1,0:T(8,128)} %get-tuple-element.100.refs_2_, f32[256,128]{1,0:T(8,128)} %copy-done.9, f32[256,128]{1,0:T(8,128)} %copy-done.10, ...), custom_call_target="tpu_custom_call" | custom-call | tf_op jit(solution)/shard_map/last_update/pallas_call | solution.py:512
  (46 shorter events, 0.2 us)
Async XLA Ops:
  0.6 15.7 %copy-start.11 = (s32[1,1,16,2]{2,3,1,0:T(2,128)S(1)}, s32[1,1,16,2]{2,3,1,0:T(2,128)}, u32[]{:S(2)}) copy-start(s32[1,1,16,2]{2,3,1,0:T(2,128)} %param.8) | copy-start | bytes 388
  0.6 18.7 %copy-start = (f32[2,4,128,128]{3,2,1,0:T(8,128)S(1)}, f32[2,4,128,128]{3,2,1,0:T(8,128)}, u32[]{:S(2)}) copy-start(f32[2,4,128,128]{3,2,1,0:T(8,128)} %refs_11_.1) | copy-start | bytes 1572868
  2.6 9.5 %collective-permute-start.1 = (f32[2,72,256]{2,1,0:T(8,128)S(1)}, f32[2,72,256]{2,1,0:T(8,128)S(1)}, u32[]{:S(2)}, u32[]{:S(2)}) collective-permute-start(f32[2,72,256]{2,1,0:T(8,128)S(1)} %get-tuple-element.118), channel_id=1, source_target_pairs={{16,32},{48,64},{80,96},{112,128},{144,160},{176,192},{208,224},{3... | collective-permute-start | bytes 442376 | tf_op jit(solution)/shard_map/ppermute | solution.py:535
  8.7 3.5 %collective-permute-start = (f32[2,72,256]{2,1,0:T(8,128)S(1)}, f32[2,72,256]{2,1,0:T(8,128)S(1)}, u32[]{:S(2)}, u32[]{:S(2)}) collective-permute-start(f32[2,72,256]{2,1,0:T(8,128)S(1)} %get-tuple-element.119), channel_id=1, source_target_pairs={{0,16},{16,0},{32,48},{48,32},{64,80},{80,64},{96,112},{112,96},{1... | collective-permute-start | bytes 442376 | tf_op jit(solution)/shard_map/ppermute | solution.py:533
  13.9 5.4 %collective-permute-start.2 = (f32[392,128]{1,0:T(8,128)S(1)}, f32[392,128]{1,0:T(8,128)S(1)}, u32[]{:S(2)}, u32[]{:S(2)}) collective-permute-start(f32[392,128]{1,0:T(8,128)S(1)} %get-tuple-element.59), channel_id=1, source_target_pairs={{0,1},{1,0},{2,3},{3,2},{4,5},{5,4},{6,7},{7,6},{8,9},{9,8},{10,11... | collective-permute-start | bytes 602120 | tf_op jit(solution)/shard_map/ppermute | solution.py:533
  15.6 3.7 %collective-permute-start.3 = (f32[392,128]{1,0:T(8,128)S(1)}, f32[392,128]{1,0:T(8,128)S(1)}, u32[]{:S(2)}, u32[]{:S(2)}) collective-permute-start(f32[392,128]{1,0:T(8,128)S(1)} %get-tuple-element.60), channel_id=1, source_target_pairs={{1,2},{3,4},{5,6},{7,8},{9,10},{11,12},{13,14},{2,1},{4,3},{6,5},{... | collective-permute-start | bytes 602120 | tf_op jit(solution)/shard_map/ppermute | solution.py:535
  30.3 20.0 %copy-start.3 = (f32[2,3,128,128]{3,2,1,0:T(8,128)S(1)}, f32[2,3,128,128]{3,2,1,0:T(8,128)}, u32[]{:S(2)}) copy-start(f32[2,3,128,128]{3,2,1,0:T(8,128)} %get-tuple-element.66.refs_1_) | copy-start | bytes 1179652
  30.4 20.7 %copy-start.4 = (f32[2,3,128,128]{3,2,1,0:T(8,128)S(1)}, f32[2,3,128,128]{3,2,1,0:T(8,128)}, u32[]{:S(2)}) copy-start(f32[2,3,128,128]{3,2,1,0:T(8,128)} %get-tuple-element.67.refs_2_) | copy-start | bytes 1179652
  30.4 1.8 %collective-permute-start.4 = (f32[768,128]{1,0:T(8,128)S(1)}, f32[768,128]{1,0:T(8,128)S(1)}, u32[]{:S(2)}, u32[]{:S(2)}) collective-permute-start(f32[768,128]{1,0:T(8,128)S(1)} %get-tuple-element.62), channel_id=1, source_target_pairs={{0,16},{16,0},{1,17},{17,1},{2,18},{18,2},{3,19},{19,3},{4,20},{20... | collective-permute-start | bytes 1179656 | tf_op jit(solution)/shard_map/ppermute | solution.py:541
  33.0 33.1 %all-to-all-start = ((f32[32,24,128]{2,1,0:T(8,128)}), f32[32,24,128]{2,1,0:T(8,128)S(1)}, u32[]{:S(2)}, u32[]{:S(2)}) async-start(f32[32,24,128]{2,1,0:T(8,128)} %bitcast.9), calls=%async_computation | async-start | bytes 786432 | tf_op jit(solution)/shard_map/all_to_all | solution.py:625
  50.4 10.7 %collective-permute-start.5 = (f32[2,3,128,128]{3,2,1,0:T(8,128)S(1)}, f32[2,3,128,128]{3,2,1,0:T(8,128)S(1)}, u32[]{:S(2)}, u32[]{:S(2)}) collective-permute-start(f32[2,3,128,128]{3,2,1,0:T(8,128)S(1)} %copy-done.3), channel_id=1, source_target_pairs={{0,16},{16,0},{32,48},{48,32},{64,80},{80,64},{96,112},{112,96},{1... | collective-permute-start | bytes 1179656 | tf_op jit(solution)/shard_map/ppermute | solution.py:533
  51.1 15.0 %collective-permute-start.6 = (f32[2,3,128,128]{3,2,1,0:T(8,128)S(1)}, f32[2,3,128,128]{3,2,1,0:T(8,128)S(1)}, u32[]{:S(2)}, u32[]{:S(2)}) collective-permute-start(f32[2,3,128,128]{3,2,1,0:T(8,128)S(1)} %copy-done.4), channel_id=1, source_target_pairs={{16,32},{48,64},{80,96},{112,128},{144,160},{176,192},{208,224},{3... | collective-permute-start | bytes 1179656 | tf_op jit(solution)/shard_map/ppermute | solution.py:535
  61.0 22.9 %copy-start.5 = (f32[2,3,128,128]{3,2,1,0:T(8,128)}, f32[2,3,128,128]{3,2,1,0:T(8,128)S(1)}, u32[]{:S(2)}) copy-start(f32[2,3,128,128]{3,2,1,0:T(8,128)S(1)} %collective-permute-done.5.refs_4_) | copy-start | bytes 1179652
  66.1 17.9 %copy-start.6 = (f32[2,3,128,128]{3,2,1,0:T(8,128)}, f32[2,3,128,128]{3,2,1,0:T(8,128)S(1)}, u32[]{:S(2)}) copy-start(f32[2,3,128,128]{3,2,1,0:T(8,128)S(1)} %collective-permute-done.6.refs_5_) | copy-start | bytes 1179652
  66.1 5.0 %collective-permute-start.9 = (f32[24,128]{1,0:T(8,128)S(1)}, f32[24,128]{1,0:T(8,128)S(1)}, u32[]{:S(2)}, u32[]{:S(2)}) collective-permute-start(f32[24,128]{1,0:T(8,128)S(1)} %share.2), channel_id=1, source_target_pairs={{0,40},{8,32},{32,8},{40,0},{1,41},{9,33},{33,9},{41,1},{2,42},{10... | collective-permute-start | bytes 36872 | tf_op jit(solution)/shard_map/ppermute | solution.py:541
  70.1 4.0 %collective-permute-start.8 = (f32[24,128]{1,0:T(8,128)S(1)}, f32[24,128]{1,0:T(8,128)S(1)}, u32[]{:S(2)}, u32[]{:S(2)}) collective-permute-start(f32[24,128]{1,0:T(8,128)S(1)} %share.2), channel_id=1, source_target_pairs={{0,32},{32,0},{1,33},{33,1},{2,34},{34,2},{3,35},{35,3},{4,36},{36... | collective-permute-start | bytes 36872 | tf_op jit(solution)/shard_map/ppermute | solution.py:541
  70.4 3.7 %collective-permute-start.7 = (f32[24,128]{1,0:T(8,128)S(1)}, f32[24,128]{1,0:T(8,128)S(1)}, u32[]{:S(2)}, u32[]{:S(2)}) collective-permute-start(f32[24,128]{1,0:T(8,128)S(1)} %share.2), channel_id=1, source_target_pairs={{0,8},{8,0},{1,9},{9,1},{2,10},{10,2},{3,11},{11,3},{4,12},{12,4},... | collective-permute-start | bytes 36872 | tf_op jit(solution)/shard_map/ppermute | solution.py:541
  75.0 27.3 %all-to-all-start.1 = ((f32[32,24,128]{2,1,0:T(8,128)}), f32[32,24,128]{2,1,0:T(8,128)S(1)}, u32[]{:S(2)}, u32[]{:S(2)}) async-start(f32[32,24,128]{2,1,0:T(8,128)} %bitcast.12), calls=%async_computation.1 | async-start | bytes 786432 | tf_op jit(solution)/shard_map/all_to_all | solution.py:633
  87.5 14.8 %collective-permute-start.10 = (f32[2,384,128]{2,1,0:T(8,128)}, f32[2,384,128]{2,1,0:T(8,128)S(1)}, u32[]{:S(2)}, u32[]{:S(2)}) collective-permute-start(f32[2,384,128]{2,1,0:T(8,128)} %get-tuple-element.81), channel_id=1, source_target_pairs={{0,1},{1,0},{2,3},{3,2},{4,5},{5,4},{6,7},{7,6},{8,9},{9,8},{10,11... | collective-permute-start | bytes 1179656 | tf_op jit(solution)/shard_map/ppermute | solution.py:533
  88.8 13.5 %collective-permute-start.11 = (f32[2,384,128]{2,1,0:T(8,128)}, f32[2,384,128]{2,1,0:T(8,128)S(1)}, u32[]{:S(2)}, u32[]{:S(2)}) collective-permute-start(f32[2,384,128]{2,1,0:T(8,128)} %get-tuple-element.82), channel_id=1, source_target_pairs={{1,2},{3,4},{5,6},{7,8},{9,10},{11,12},{13,14},{2,1},{4,3},{6,5},{... | collective-permute-start | bytes 1179656 | tf_op jit(solution)/shard_map/ppermute | solution.py:535
  102.3 2.9 %copy-start.1 = (f32[2,384,128]{2,1,0:T(8,128)}, f32[2,384,128]{2,1,0:T(8,128)S(1)}, u32[]{:S(2)}) copy-start(f32[2,384,128]{2,1,0:T(8,128)S(1)} %collective-permute-done.10.refs_6_) | copy-start | bytes 1179652
  102.3 2.9 %copy-start.2 = (f32[2,384,128]{2,1,0:T(8,128)}, f32[2,384,128]{2,1,0:T(8,128)S(1)}, u32[]{:S(2)}) copy-start(f32[2,384,128]{2,1,0:T(8,128)S(1)} %collective-permute-done.11.refs_7_) | copy-start | bytes 1179652
  102.3 2.9 %collective-permute-start.12 = (f32[768,128]{1,0:T(8,128)S(1)}, f32[768,128]{1,0:T(8,128)S(1)}, u32[]{:S(2)}, u32[]{:S(2)}) collective-permute-start(f32[768,128]{1,0:T(8,128)S(1)} %bitcast.23), channel_id=1, source_target_pairs={{0,16},{16,0},{1,17},{17,1},{2,18},{18,2},{3,19},{19,3},{4,20},{20... | collective-permute-start | bytes 1179656 | tf_op jit(solution)/shard_map/ppermute | solution.py:541
  117.8 10.9 %copy-start.13 = (f32[2,3,64,128]{3,2,1,0:T(8,128)S(1)}, f32[2,3,64,128]{3,2,1,0:T(8,128)}, u32[]{:S(2)}) copy-start(f32[2,3,64,128]{3,2,1,0:T(8,128)} %get-tuple-element.96) | copy-start | bytes 589828
  117.8 11.7 %copy-start.12 = (f32[2,3,64,128]{3,2,1,0:T(8,128)S(1)}, f32[2,3,64,128]{3,2,1,0:T(8,128)}, u32[]{:S(2)}) copy-start(f32[2,3,64,128]{3,2,1,0:T(8,128)} %get-tuple-element.97) | copy-start | bytes 589828
  117.8 1.8 %collective-permute-start.13 = (f32[768,128]{1,0:T(8,128)S(1)}, f32[768,128]{1,0:T(8,128)S(1)}, u32[]{:S(2)}, u32[]{:S(2)}) collective-permute-start(f32[768,128]{1,0:T(8,128)S(1)} %get-tuple-element.91), channel_id=1, source_target_pairs={{0,16},{16,0},{1,17},{17,1},{2,18},{18,2},{3,19},{19,3},{4,20},{20... | collective-permute-start | bytes 1179656 | tf_op jit(solution)/shard_map/ppermute | solution.py:541
  120.5 20.3 %all-to-all-start.2 = ((f32[32,24,128]{2,1,0:T(8,128)}), f32[32,24,128]{2,1,0:T(8,128)S(1)}, u32[]{:S(2)}, u32[]{:S(2)}) async-start(f32[32,24,128]{2,1,0:T(8,128)} %bitcast.14), calls=%async_computation.2 | async-start | bytes 786432 | tf_op jit(solution)/shard_map/all_to_all | solution.py:625
  128.7 8.5 %collective-permute-start.14 = (f32[2,3,64,128]{3,2,1,0:T(8,128)S(1)}, f32[2,3,64,128]{3,2,1,0:T(8,128)S(1)}, u32[]{:S(2)}, u32[]{:S(2)}) collective-permute-start(f32[2,3,64,128]{3,2,1,0:T(8,128)S(1)} %copy-done.13), channel_id=1, source_target_pairs={{0,16},{16,0},{32,48},{48,32},{64,80},{80,64},{96,112},{112,96},{1... | collective-permute-start | bytes 589832 | tf_op jit(solution)/shard_map/ppermute | solution.py:533
  129.5 10.4 %collective-permute-start.15 = (f32[2,3,64,128]{3,2,1,0:T(8,128)S(1)}, f32[2,3,64,128]{3,2,1,0:T(8,128)S(1)}, u32[]{:S(2)}, u32[]{:S(2)}) collective-permute-start(f32[2,3,64,128]{3,2,1,0:T(8,128)S(1)} %copy-done.12), channel_id=1, source_target_pairs={{16,32},{48,64},{80,96},{112,128},{144,160},{176,192},{208,224},{3... | collective-permute-start | bytes 589832 | tf_op jit(solution)/shard_map/ppermute | solution.py:535
  137.2 18.6 %copy-start.7 = (f32[2,3,64,128]{3,2,1,0:T(8,128)}, f32[2,3,64,128]{3,2,1,0:T(8,128)S(1)}, u32[]{:S(2)}) copy-start(f32[2,3,64,128]{3,2,1,0:T(8,128)S(1)} %collective-permute-done.14.refs_2_) | copy-start | bytes 589828
  139.9 16.0 %copy-start.8 = (f32[2,3,64,128]{3,2,1,0:T(8,128)}, f32[2,3,64,128]{3,2,1,0:T(8,128)S(1)}, u32[]{:S(2)}) copy-start(f32[2,3,64,128]{3,2,1,0:T(8,128)S(1)} %collective-permute-done.15.refs_3_) | copy-start | bytes 589828
  140.8 3.8 %collective-permute-start.18 = (f32[24,128]{1,0:T(8,128)S(1)}, f32[24,128]{1,0:T(8,128)S(1)}, u32[]{:S(2)}, u32[]{:S(2)}) collective-permute-start(f32[24,128]{1,0:T(8,128)S(1)} %share.3), channel_id=1, source_target_pairs={{0,40},{8,32},{32,8},{40,0},{1,41},{9,33},{33,9},{41,1},{2,42},{10... | collective-permute-start | bytes 36872 | tf_op jit(solution)/shard_map/ppermute | solution.py:541
  142.2 4.0 %collective-permute-start.17 = (f32[24,128]{1,0:T(8,128)S(1)}, f32[24,128]{1,0:T(8,128)S(1)}, u32[]{:S(2)}, u32[]{:S(2)}) collective-permute-start(f32[24,128]{1,0:T(8,128)S(1)} %share.3), channel_id=1, source_target_pairs={{0,32},{32,0},{1,33},{33,1},{2,34},{34,2},{3,35},{35,3},{4,36},{36... | collective-permute-start | bytes 36872 | tf_op jit(solution)/shard_map/ppermute | solution.py:541
  143.0 3.2 %collective-permute-start.16 = (f32[24,128]{1,0:T(8,128)S(1)}, f32[24,128]{1,0:T(8,128)S(1)}, u32[]{:S(2)}, u32[]{:S(2)}) collective-permute-start(f32[24,128]{1,0:T(8,128)S(1)} %share.3), channel_id=1, source_target_pairs={{0,8},{8,0},{1,9},{9,1},{2,10},{10,2},{3,11},{11,3},{4,12},{12,4},... | collective-permute-start | bytes 36872 | tf_op jit(solution)/shard_map/ppermute | solution.py:541
  147.1 20.5 %all-to-all-start.3 = ((f32[32,24,128]{2,1,0:T(8,128)}), f32[32,24,128]{2,1,0:T(8,128)S(1)}, u32[]{:S(2)}, u32[]{:S(2)}) async-start(f32[32,24,128]{2,1,0:T(8,128)} %bitcast.17), calls=%async_computation.3 | async-start | bytes 786432 | tf_op jit(solution)/shard_map/all_to_all | solution.py:633
  158.8 8.7 %collective-permute-start.19 = (f32[256,128]{1,0:T(8,128)}, f32[256,128]{1,0:T(8,128)S(1)}, u32[]{:S(2)}, u32[]{:S(2)}) collective-permute-start(f32[256,128]{1,0:T(8,128)} %get-tuple-element.106), channel_id=1, source_target_pairs={{0,1},{1,0},{2,3},{3,2},{4,5},{5,4},{6,7},{7,6},{8,9},{9,8},{10,11... | collective-permute-start | bytes 393224 | tf_op jit(solution)/shard_map/ppermute | solution.py:533
  160.1 7.4 %collective-permute-start.20 = (f32[256,128]{1,0:T(8,128)}, f32[256,128]{1,0:T(8,128)S(1)}, u32[]{:S(2)}, u32[]{:S(2)}) collective-permute-start(f32[256,128]{1,0:T(8,128)} %get-tuple-element.107), channel_id=1, source_target_pairs={{1,2},{3,4},{5,6},{7,8},{9,10},{11,12},{13,14},{2,1},{4,3},{6,5},{... | collective-permute-start | bytes 393224 | tf_op jit(solution)/shard_map/ppermute | solution.py:535
  167.5 6.1 %copy-start.9 = (f32[256,128]{1,0:T(8,128)}, f32[256,128]{1,0:T(8,128)S(1)}, u32[]{:S(2)}) copy-start(f32[256,128]{1,0:T(8,128)S(1)} %collective-permute-done.19.refs_3_) | copy-start | bytes 393220
  167.5 6.1 %copy-start.10 = (f32[256,128]{1,0:T(8,128)}, f32[256,128]{1,0:T(8,128)S(1)}, u32[]{:S(2)}) copy-start(f32[256,128]{1,0:T(8,128)S(1)} %collective-permute-done.20.refs_4_) | copy-start | bytes 393220
  167.6 6.1 %collective-permute-start.21 = (f32[768,128]{1,0:T(8,128)S(1)}, f32[768,128]{1,0:T(8,128)S(1)}, u32[]{:S(2)}, u32[]{:S(2)}) collective-permute-start(f32[768,128]{1,0:T(8,128)S(1)} %bitcast.25), channel_id=1, source_target_pairs={{0,16},{16,0},{1,17},{17,1},{2,18},{18,2},{3,19},{19,3},{4,20},{20... | collective-permute-start | bytes 1179656 | tf_op jit(solution)/shard_map/ppermute | solution.py:541

commit v4 on v3

--- a/solution.py
+++ b/solution.py
@@ -231,7 +231,7 @@
 
 
 def next_kernel(
-    copies, off_ref, at_ref, obj_ref, top_ref, mid_ref, low_ref, col_a_ref, col_b_ref, light_ref,
+    copies, off_ref, at_ref, obj_ref, own_a_ref, own_b_ref, mid_ref, row_a_ref, row_b_ref, col_a_ref, col_b_ref, light_ref,
     mine_ref, other_ref, probe_ref, meas_ref, fwd_ref, bwd_ref,
     first_ref, second_ref, new_mid_ref, keep_ref, send_ref, new_obj_ref, bright_ref, new_probe_ref,
     canvas, grads,
@@ -245,15 +245,21 @@
     copies.ready(new_probe_ref)
     bright_ref[...] = brightness(new_probe_ref)
     copies.ready(bright_ref)
-    copies.need(obj_ref, top_ref, mid_ref, low_ref, col_a_ref, col_b_ref, light_ref)
-    for j, ref in enumerate((top_ref, mid_ref, low_ref)):
+    copies.need(obj_ref, own_a_ref, own_b_ref, mid_ref, row_a_ref, row_b_ref, col_a_ref, col_b_ref, light_ref)
+    for j in range(3):
         rows = slice(j * n, (j + 1) * n)
         row = lax.broadcasted_iota(jnp.int32, (n, n), 0) + j * n
         row_ok = (row >= at_ref[1]) & (row < at_ref[2])
         for k in range(blocks):
             col = lax.broadcasted_iota(jnp.int32, (n, n), 1) + k * n
             inside = row_ok & (col >= at_ref[3]) & (col < at_ref[4])
-            sums = ref[:, k]
+            if j == 1:
+                sums = mid_ref[:, k]
+            else:
+                ends = ordered(
+                    at_ref[5] == 1, own_a_ref[:, k] + row_a_ref[:, k], own_b_ref[:, k] + row_b_ref[:, k]
+                )
+                sums = ends[j > 0]
             if k in (0, blocks - 1):
                 sides = ordered(at_ref[6] == 1, col_a_ref[:, rows], col_b_ref[:, rows])
                 sums = sums + sides[k > 0]
@@ -299,19 +305,20 @@
     copies.ready(out_ref)
 
 
-def fold_kernel(
-    copies, at_ref, first_ref, second_ref, mid_ref, row_a_ref, row_b_ref, top_ref, low_ref, col_a_ref, col_b_ref
-):
+def fold_kernel(copies, at_ref, first_ref, second_ref, mid_ref, row_a_ref, row_b_ref, col_a_ref, col_b_ref):
     n = col_a_ref.shape[2]
-    last = top_ref.shape[1] - 1
-    copies.need(first_ref, second_ref, mid_ref, row_a_ref, row_b_ref)
-    top_ref[...], low_ref[...] = ordered(
-        at_ref[5] == 1, first_ref[...] + row_a_ref[...], second_ref[...] + row_b_ref[...]
-    )
-    for j, ref in enumerate((top_ref, mid_ref, low_ref)):
+    last = mid_ref.shape[1] - 1
+    copies.need(first_ref, row_a_ref, second_ref, row_b_ref, mid_ref)
+    sides = []
+    for k in (0, last):
+        top, low = ordered(
+            at_ref[5] == 1, first_ref[:, k] + row_a_ref[:, k], second_ref[:, k] + row_b_ref[:, k]
+        )
+        sides.append((top, mid_ref[:, k], low))
+    for j in range(3):
         rows = slice(j * n, (j + 1) * n)
-        col_a_ref[:, rows], col_b_ref[:, rows] = ordered(at_ref[6] == 1, ref[:, 0], ref[:, last])
-    copies.ready(col_a_ref, col_b_ref, top_ref, low_ref)
+        col_a_ref[:, rows], col_b_ref[:, rows] = ordered(at_ref[6] == 1, sides[0][j], sides[1][j])
+    copies.ready(col_a_ref, col_b_ref)
 
 
 def fold_inner_kernel(copies, at_ref, mid_ref, row_a_ref, row_b_ref, sums_ref, col_a_ref, col_b_ref):
@@ -625,11 +632,14 @@
         parts = lax.all_to_all(keep + received, RING, 0, 0, tiled=True)
         light, peak = call(light_kernel, [Far(lights), (8, n)], [canvas, SPOTS], [tags, Far(bright)], 1, "light")
         row_a, row_b = exchange(first, second, ROW)
-        parts, row_a, row_b = lax.optimization_barrier((parts, row_a, row_b))
+        if last:
+            parts, row_a, row_b = lax.optimization_barrier((parts, row_a, row_b))
+        else:
+            parts, row_a = lax.optimization_barrier((parts, row_a))
         share = call(share_kernel, [(CHUNK, n)], [], [parts, peak], 0, "share")[0]
         share = share_over_x(share)
         copies = jnp.broadcast_to(share[None], (PARTS,) + share.shape).reshape(packed)
-        light, copies = lax.optimization_barrier((light, copies))
+        light, copies, row_b = lax.optimization_barrier((light, copies, row_b))
         mine = lax.all_to_all(copies, RING, 0, 0, tiled=True)
         if last:
             outs = [Far((2, blocks, tile, n)), Far((tile, n)), Far((tile, n))]
@@ -638,10 +648,10 @@
             sums = [sums]
         else:
             side = (2, extent, n)
-            outs = [Far(x) for x in (band, band, side, side)]
+            outs = [Far(side), Far(side)]
             args = [info] + [Far(x) for x in (first, second, mid, row_a, row_b)]
-            top, low, col_a, col_b = call(fold_kernel, outs, [], args, 1, "fold_rows")
-            sums = [top, mid, low]
+            col_a, col_b = call(fold_kernel, outs, [], args, 1, "fold_rows")
+            sums = [first, second, mid, row_a, row_b]
             args = [tags, Far(bright), Far(light)]
             light = call(more_light_kernel, [Far(lights)], [canvas, SPOTS], args, 1, "more_light")[0]
         col_a, col_b = exchange(col_a, col_b, COL)

time: 179 us -> 174 us (0.972)
  waiting for transfers between devices: 40.9 us -> 38 us
    ppermute x6, waiting for transfers between devices: 10.8 us -> 5.6 us  [exchange(): second = lax.ppermute(second, axes, pairs + [(j, i) for i, j in pairs])]
where the time goes in v4:
time: 174 us; the launch traced here: 173 us
  starting transfers between devices  79.8 us (46%)
  Pallas kernels  48.5 us (28%)
  waiting for transfers between devices  38 us (22%)
  local copies, waits for them, and re-layouts  3.09 us (2%)
  other arithmetic  2.51 us (1%)
    pallas_call x11, Pallas kernels, call(): pl.pallas_call(whole, out_shape=tuple((pltpu.HBM(x, F32) if is_far else j...  48.5 us
    all_to_all x2, starting transfers between devices, body(): parts = lax.all_to_all(keep + received, RING, 0, 0, tiled=True)  25.9 us
    ppermute x6, waiting for transfers between devices, exchange(): first = lax.ppermute(first, axes, [(i, i ^ 1) for i in range(count)])  18.5 us
    ppermute x6, starting transfers between devices, exchange(): second = lax.ppermute(second, axes, pairs + [(j, i) for i, j in pairs])  17.2 us
    all_to_all x2, starting transfers between devices, body(): mine = lax.all_to_all(copies, RING, 0, 0, tiled=True)  16.5 us
    ppermute x10, starting transfers between devices, swap(): return lax.ppermute(value, axes, [(i, count - 1 - i) for i in range(count)])  14.3 us
    ppermute x10, waiting for transfers between devices, swap(): return lax.ppermute(value, axes, [(i, count - 1 - i) for i in range(count)])  11.6 us
    ppermute x6, starting transfers between devices, exchange(): first = lax.ppermute(first, axes, [(i, i ^ 1) for i in range(count)])  5.93 us
  transfers between devices with their start and end apart: 26, of which 15 were waited for; matrix products, arithmetic and copies ran while one was open for 0% of the time, Pallas kernels for 11%

profile of v4, /device:TPU:1, one launch (start us, length us, event | category | flops | bytes accessed | tf_op | source)
XLA Modules:
  0.0 173.1 jit_solution(17427534479176641565)
XLA Ops:
  0.7 0.7 add_convert_fusion
  1.4 0.1 copy.12
  1.5 0.1 convert_element_type.31
  1.6 1.0 constant_dynamic-slice_fusion
  2.6 6.0 %collective-permute-start.1 = (f32[2,72,256]{2,1,0:T(8,128)S(1)}, f32[2,72,256]{2,1,0:T(8,128)S(1)}, u32[]{:S(2)}, u32[]{:S(2)}) collective-permute-start(f32[2,72,256]{2,1,0:T(8,128)S(1)} %get-tuple-element.116), channel_id=1, source_target_pairs={{16,32},{48,64},{80,96},{112,128},{144,160},{176,192},{208,224},{3... | collective-permute-start | bytes 442376 | tf_op jit(solution)/shard_map/ppermute | solution.py:542
  8.7 0.1 collective-permute-start
  8.8 0.1 convert_element_type.32
  8.9 0.1 stack.31.refs_0_.refs_1_
  9.0 3.1 %collective-permute-done.1.refs_3_ = f32[2,72,256]{2,1,0:T(8,128)S(1)} collective-permute-done((f32[2,72,256]{2,1,0:T(8,128)S(1)}, f32[2,72,256]{2,1,0:T(8,128)S(1)}, u32[]{:S(2)}, u32[]{:S(2)}) %collective-permute-start.1) | collective-permute-done | bytes 147488 | tf_op jit(solution)/shard_map/ppermute | solution.py:542
  12.2 1.8 %join_rows.1 = (f32[2,384,256]{2,1,0:T(8,128)S(1)}, f32[392,128]{1,0:T(8,128)S(1)}, f32[392,128]{1,0:T(8,128)S(1)}, f32[8,128]{1,0:T(8,128)S(1)}) custom-call(s32[7]{0:T(128)S(1)} %stack.31.refs_0_.refs_1_, f32[2,256,256]{2,1,0:T(8,128)} %refs_1_.1, f32[2,72,256]{2,1,0:T(8,128)S(1)} %collective-permute-done.refs_2_, ...), custom_call_target="tpu_custom_call" | custom-call | tf_op jit(solution)/shard_map/join_rows/pallas_call | solution.py:519
  13.9 1.7 collective-permute-start.2
  15.6 0.7 collective-permute-start.3
  16.3 0.1 copy.15.refs_0_
  16.4 2.9 %collective-permute-done.2.refs_3_ = f32[392,128]{1,0:T(8,128)S(1)} collective-permute-done((f32[392,128]{1,0:T(8,128)S(1)}, f32[392,128]{1,0:T(8,128)S(1)}, u32[]{:S(2)}, u32[]{:S(2)}) %collective-permute-start.2) | collective-permute-done | bytes 200736 | tf_op jit(solution)/shard_map/ppermute | solution.py:540
  19.3 11.0 %first_sweep.1 = (f32[2,3,128,128]{3,2,1,0:T(8,128)}, f32[2,3,128,128]{3,2,1,0:T(8,128)}, f32[2,3,128,128]{3,2,1,0:T(8,128)}, f32[768,128]{1,0:T(8,128)S(1)}, f3...) custom-call(s32[16,2]{1,0:T(8,128)S(1)} %copy.15.refs_0_, s32[7]{0:T(128)S(1)} %stack.31.refs_0_.refs_1_, ...), custom_call_target="tpu_custom_call" | custom-call | tf_op jit(solution)/shard_map/first_sweep/pallas_call | solution.py:519
  30.3 0.1 collective-permute-start.4
  30.4 1.7 collective-permute-done.4
  32.1 0.8 add.84
  32.9 17.4 %all-to-all-start = ((f32[32,24,128]{2,1,0:T(8,128)}), f32[32,24,128]{2,1,0:T(8,128)S(1)}, u32[]{:S(2)}, u32[]{:S(2)}) async-start(f32[32,24,128]{2,1,0:T(8,128)} %bitcast.9), calls=%async_computation | async-start | bytes 786432 | tf_op jit(solution)/shard_map/all_to_all | solution.py:632
  50.4 0.7 collective-permute-start.5
  51.1 5.5 %collective-permute-start.9 = (f32[2,3,128,128]{3,2,1,0:T(8,128)S(1)}, f32[2,3,128,128]{3,2,1,0:T(8,128)S(1)}, u32[]{:S(2)}, u32[]{:S(2)}) collective-permute-start(f32[2,3,128,128]{3,2,1,0:T(8,128)S(1)} %copy-done.2), channel_id=1, source_target_pairs={{16,32},{48,64},{80,96},{112,128},{144,160},{176,192},{208,224},{3... | collective-permute-start | bytes 1179656 | tf_op jit(solution)/shard_map/ppermute | solution.py:542
  56.6 4.2 %light.2 = (f32[3,384,128]{2,1,0:T(8,128)}, f32[8,128]{1,0:T(8,128)S(1)}) custom-call(s32[9,32]{1,0:T(8,128)S(1)} %maximum_convert_fusion.refs_0_, f32[128,128]{1,0:T(8,128)} %get-tuple-element.72.refs_1_), custom_call_target="tpu_custom_call" | custom-call | tf_op jit(solution)/shard_map/light/pallas_call | solution.py:519
  60.9 1.4 all-to-all-done
  62.4 3.3 %collective-permute-start.8 = (f32[24,128]{1,0:T(8,128)S(1)}, f32[24,128]{1,0:T(8,128)S(1)}, u32[]{:S(2)}, u32[]{:S(2)}) collective-permute-start(f32[24,128]{1,0:T(8,128)S(1)} %share.2), channel_id=1, source_target_pairs={{0,40},{8,32},{32,8},{40,0},{1,41},{9,33},{33,9},{41,1},{2,42},{10... | collective-permute-start | bytes 36872 | tf_op jit(solution)/shard_map/ppermute | solution.py:548
  65.7 0.4 collective-permute-start.7
  66.0 0.3 collective-permute-start.6
  66.4 0.4 collective-permute-done.8
  66.8 3.0 %collective-permute-done.7 = f32[24,128]{1,0:T(8,128)S(1)} collective-permute-done((f32[24,128]{1,0:T(8,128)S(1)}, f32[24,128]{1,0:T(8,128)S(1)}, u32[]{:S(2)}, u32[]{:S(2)}) %collective-permute-start.7) | collective-permute-done | bytes 12320 | tf_op jit(solution)/shard_map/ppermute | solution.py:548
  69.7 0.1 maximum_select_fusion.1
  69.8 0.8 broadcast_in_dim.4
  70.6 7.7 %all-to-all-start.1 = ((f32[32,24,128]{2,1,0:T(8,128)}), f32[32,24,128]{2,1,0:T(8,128)S(1)}, u32[]{:S(2)}, u32[]{:S(2)}) async-start(f32[32,24,128]{2,1,0:T(8,128)} %bitcast.12), calls=%async_computation.1 | async-start | bytes 786432 | tf_op jit(solution)/shard_map/all_to_all | solution.py:643
  78.4 3.0 %fold_rows.1 = (f32[2,384,128]{2,1,0:T(8,128)}, f32[2,384,128]{2,1,0:T(8,128)}) custom-call(s32[7]{0:T(128)S(1)} %stack.31.refs_0_.refs_1_, f32[2,3,128,128]{3,2,1,0:T(8,128)} %get-tuple-element.65.refs_1_.refs_3_, f32[2,3,128,128]{3,2,1,0:T(8,128)} %get-tuple-element.66.refs_2_.refs_4_, f32[2,3,128,128]{3,2,1,0:T(8,128)} %get-tuple-element.67.refs_3_.refs_5_, ...), custom_call_target="tpu_custom_call" | custom-call | tf_op jit(solution)/shard_map/fold_rows/pallas_call | solution.py:519
  81.5 1.3 collective-permute-start.10
  82.8 0.7 collective-permute-start.11
  83.5 4.3 %more_light.1.refs_10_ = f32[3,384,128]{2,1,0:T(8,128)} custom-call(s32[9,32]{1,0:T(8,128)S(1)} %maximum_convert_fusion.refs_0_, f32[128,128]{1,0:T(8,128)} %get-tuple-element.72.refs_1_, f32[3,384,128]{2,1,0:T(8,128)} %get-tuple-element.80.refs_2_), custom_call_target="tpu_custom_call" | custom-call | tf_op jit(solution)/shard_map/more_light/pallas_call | solution.py:519
  87.7 8.2 %collective-permute-done.10.refs_8_ = f32[2,384,128]{2,1,0:T(8,128)S(1)} collective-permute-done((f32[2,384,128]{2,1,0:T(8,128)}, f32[2,384,128]{2,1,0:T(8,128)S(1)}, u32[]{:S(2)}, u32[]{:S(2)}) %collective-permute-start.10) | collective-permute-done | bytes 393248 | tf_op jit(solution)/shard_map/ppermute | solution.py:540
  95.9 2.6 %collective-permute-start.12 = (f32[768,128]{1,0:T(8,128)S(1)}, f32[768,128]{1,0:T(8,128)S(1)}, u32[]{:S(2)}, u32[]{:S(2)}) collective-permute-start(f32[768,128]{1,0:T(8,128)S(1)} %bitcast.23), channel_id=1, source_target_pairs={{0,16},{16,0},{1,17},{17,1},{2,18},{18,2},{3,19},{19,3},{4,20},{20... | collective-permute-start | bytes 1179656 | tf_op jit(solution)/shard_map/ppermute | solution.py:548
  98.5 1.3 collective-permute-done.12.refs_12_
  99.8 12.9 %next_sweep.1 = (f32[2,3,64,128]{3,2,1,0:T(8,128)}, f32[2,3,64,128]{3,2,1,0:T(8,128)}, f32[2,3,256,128]{3,2,1,0:T(8,128)}, f32[768,128]{1,0:T(8,128)S(1)}, f32[7...) custom-call(s32[16,2]{1,0:T(8,128)S(1)} %copy.15.refs_0_, ...), custom_call_target="tpu_custom_call" | custom-call | tf_op jit(solution)/shard_map/next_sweep/pallas_call | solution.py:519
  112.8 0.5 collective-permute-start.13
  113.3 1.3 collective-permute-done.13
  114.6 0.8 add.88
  115.4 8.5 %all-to-all-start.2 = ((f32[32,24,128]{2,1,0:T(8,128)}), f32[32,24,128]{2,1,0:T(8,128)S(1)}, u32[]{:S(2)}, u32[]{:S(2)}) async-start(f32[32,24,128]{2,1,0:T(8,128)} %bitcast.14), calls=%async_computation.2 | async-start | bytes 786432 | tf_op jit(solution)/shard_map/all_to_all | solution.py:632
  123.9 0.7 collective-permute-start.14
  124.6 3.7 %collective-permute-start.15 = (f32[2,3,64,128]{3,2,1,0:T(8,128)S(1)}, f32[2,3,64,128]{3,2,1,0:T(8,128)S(1)}, u32[]{:S(2)}, u32[]{:S(2)}) collective-permute-start(f32[2,3,64,128]{3,2,1,0:T(8,128)S(1)} %copy-done.12), channel_id=1, source_target_pairs={{16,32},{48,64},{80,96},{112,128},{144,160},{176,192},{208,224},{3... | collective-permute-start | bytes 589832 | tf_op jit(solution)/shard_map/ppermute | solution.py:542
  128.3 4.2 %light.3 = (f32[3,384,128]{2,1,0:T(8,128)}, f32[8,128]{1,0:T(8,128)S(1)}) custom-call(s32[9,32]{1,0:T(8,128)S(1)} %maximum_convert_fusion.refs_0_, f32[128,128]{1,0:T(8,128)} %get-tuple-element.96.refs_1_), custom_call_target="tpu_custom_call" | custom-call | tf_op jit(solution)/shard_map/light/pallas_call | solution.py:519
  132.5 0.0 copy-start.7
  132.5 2.5 %collective-permute-done.15.refs_3_ = f32[2,3,64,128]{3,2,1,0:T(8,128)S(1)} collective-permute-done((f32[2,3,64,128]{3,2,1,0:T(8,128)S(1)}, f32[2,3,64,128]{3,2,1,0:T(8,128)S(1)}, u32[]{:S(2)}, u32[]{:S(2)}) %collective-permute-start.15) | collective-permute-done | bytes 196640 | tf_op jit(solution)/shard_map/ppermute | solution.py:542
  135.0 0.8 all-to-all-done.2
  135.9 1.8 %collective-permute-start.18 = (f32[24,128]{1,0:T(8,128)S(1)}, f32[24,128]{1,0:T(8,128)S(1)}, u32[]{:S(2)}, u32[]{:S(2)}) collective-permute-start(f32[24,128]{1,0:T(8,128)S(1)} %share.3), channel_id=1, source_target_pairs={{0,40},{8,32},{32,8},{40,0},{1,41},{9,33},{33,9},{41,1},{2,42},{10... | collective-permute-start | bytes 36872 | tf_op jit(solution)/shard_map/ppermute | solution.py:548
  137.7 0.5 collective-permute-start.17
  138.2 1.0 collective-permute-start.16
  139.2 0.5 collective-permute-done.18
  139.7 2.0 %collective-permute-done.17 = f32[24,128]{1,0:T(8,128)S(1)} collective-permute-done((f32[24,128]{1,0:T(8,128)S(1)}, f32[24,128]{1,0:T(8,128)S(1)}, u32[]{:S(2)}, u32[]{:S(2)}) %collective-permute-start.17) | collective-permute-done | bytes 12320 | tf_op jit(solution)/shard_map/ppermute | solution.py:548
  141.7 0.1 maximum_select_fusion
  141.8 0.8 broadcast_in_dim.5
  142.6 8.7 %all-to-all-start.3 = ((f32[32,24,128]{2,1,0:T(8,128)}), f32[32,24,128]{2,1,0:T(8,128)S(1)}, u32[]{:S(2)}, u32[]{:S(2)}) async-start(f32[32,24,128]{2,1,0:T(8,128)} %bitcast.17), calls=%async_computation.3 | async-start | bytes 786432 | tf_op jit(solution)/shard_map/all_to_all | solution.py:643
  151.3 2.9 %fold_inner.1 = (f32[2,3,256,128]{3,2,1,0:T(8,128)}, f32[256,128]{1,0:T(8,128)}, f32[256,128]{1,0:T(8,128)}) custom-call(s32[7]{0:T(128)S(1)} %stack.31.refs_0_.refs_1_, f32[2,3,256,128]{3,2,1,0:T(8,128)} %get-tuple-element.86.refs_1_, f32[2,3,64,128]{3,2,1,0:T(8,128)} %copy-done.7, f32[2,3,64,128]{3,2,1,0:T(8,128)} %copy-done.8), custom_call_target="tpu_custom_call" | custom-call | tf_op jit(solution)/shard_map/fold_inner/pallas_call | solution.py:519
  154.3 1.3 collective-permute-start.19
  155.6 0.7 collective-permute-start.20
  156.3 7.4 %collective-permute-done.19.refs_3_ = f32[256,128]{1,0:T(8,128)S(1)} collective-permute-done((f32[256,128]{1,0:T(8,128)}, f32[256,128]{1,0:T(8,128)S(1)}, u32[]{:S(2)}, u32[]{:S(2)}) %collective-permute-start.19) | collective-permute-done | bytes 131104 | tf_op jit(solution)/shard_map/ppermute | solution.py:540
  163.7 3.9 %collective-permute-start.21 = (f32[768,128]{1,0:T(8,128)S(1)}, f32[768,128]{1,0:T(8,128)S(1)}, u32[]{:S(2)}, u32[]{:S(2)}) collective-permute-start(f32[768,128]{1,0:T(8,128)S(1)} %bitcast.25), channel_id=1, source_target_pairs={{0,16},{16,0},{1,17},{17,1},{2,18},{18,2},{3,19},{19,3},{4,20},{20... | collective-permute-start | bytes 1179656 | tf_op jit(solution)/shard_map/ppermute | solution.py:548
  167.5 1.3 collective-permute-done.21.refs_7_
  168.9 4.1 %last_update.1 = (f32[2,256,256]{2,1,0:T(8,128)}, f32[2,4,128,128]{3,2,1,0:T(8,128)}) custom-call(s32[7]{0:T(128)S(1)} %stack.31.refs_0_.refs_1_, f32[2,3,384,128]{3,2,1,0:T(8,128)} %get-tuple-element.85.refs_1_, f32[2,3,256,128]{3,2,1,0:T(8,128)} %get-tuple-element.102.refs_2_, f32[256,128]{1,0:T(8,128)} %copy-done.9, f32[256,128]{1,0:T(8,128)} %copy-done.10, ...), custom_call_target="tpu_custom_call" | custom-call | tf_op jit(solution)/shard_map/last_update/pallas_call | solution.py:519
  (46 shorter events, 0.2 us)
Async XLA Ops:
  0.6 15.7 %copy-start.11 = (s32[1,1,16,2]{2,3,1,0:T(2,128)S(1)}, s32[1,1,16,2]{2,3,1,0:T(2,128)}, u32[]{:S(2)}) copy-start(s32[1,1,16,2]{2,3,1,0:T(2,128)} %param.8) | copy-start | bytes 388
  0.6 18.7 %copy-start = (f32[2,4,128,128]{3,2,1,0:T(8,128)S(1)}, f32[2,4,128,128]{3,2,1,0:T(8,128)}, u32[]{:S(2)}) copy-start(f32[2,4,128,128]{3,2,1,0:T(8,128)} %refs_13_.1) | copy-start | bytes 1572868
  2.6 9.5 %collective-permute-start.1 = (f32[2,72,256]{2,1,0:T(8,128)S(1)}, f32[2,72,256]{2,1,0:T(8,128)S(1)}, u32[]{:S(2)}, u32[]{:S(2)}) collective-permute-start(f32[2,72,256]{2,1,0:T(8,128)S(1)} %get-tuple-element.116), channel_id=1, source_target_pairs={{16,32},{48,64},{80,96},{112,128},{144,160},{176,192},{208,224},{3... | collective-permute-start | bytes 442376 | tf_op jit(solution)/shard_map/ppermute | solution.py:542
  8.7 3.5 %collective-permute-start = (f32[2,72,256]{2,1,0:T(8,128)S(1)}, f32[2,72,256]{2,1,0:T(8,128)S(1)}, u32[]{:S(2)}, u32[]{:S(2)}) collective-permute-start(f32[2,72,256]{2,1,0:T(8,128)S(1)} %get-tuple-element.117), channel_id=1, source_target_pairs={{0,16},{16,0},{32,48},{48,32},{64,80},{80,64},{96,112},{112,96},{1... | collective-permute-start | bytes 442376 | tf_op jit(solution)/shard_map/ppermute | solution.py:540
  13.9 5.4 %collective-permute-start.2 = (f32[392,128]{1,0:T(8,128)S(1)}, f32[392,128]{1,0:T(8,128)S(1)}, u32[]{:S(2)}, u32[]{:S(2)}) collective-permute-start(f32[392,128]{1,0:T(8,128)S(1)} %get-tuple-element.58), channel_id=1, source_target_pairs={{0,1},{1,0},{2,3},{3,2},{4,5},{5,4},{6,7},{7,6},{8,9},{9,8},{10,11... | collective-permute-start | bytes 602120 | tf_op jit(solution)/shard_map/ppermute | solution.py:540
  15.6 3.7 %collective-permute-start.3 = (f32[392,128]{1,0:T(8,128)S(1)}, f32[392,128]{1,0:T(8,128)S(1)}, u32[]{:S(2)}, u32[]{:S(2)}) collective-permute-start(f32[392,128]{1,0:T(8,128)S(1)} %get-tuple-element.59), channel_id=1, source_target_pairs={{1,2},{3,4},{5,6},{7,8},{9,10},{11,12},{13,14},{2,1},{4,3},{6,5},{... | collective-permute-start | bytes 602120 | tf_op jit(solution)/shard_map/ppermute | solution.py:542
  30.3 20.0 %copy-start.1 = (f32[2,3,128,128]{3,2,1,0:T(8,128)S(1)}, f32[2,3,128,128]{3,2,1,0:T(8,128)}, u32[]{:S(2)}) copy-start(f32[2,3,128,128]{3,2,1,0:T(8,128)} %get-tuple-element.65.refs_1_.refs_3_) | copy-start | bytes 1179652
  30.3 20.8 %copy-start.2 = (f32[2,3,128,128]{3,2,1,0:T(8,128)S(1)}, f32[2,3,128,128]{3,2,1,0:T(8,128)}, u32[]{:S(2)}) copy-start(f32[2,3,128,128]{3,2,1,0:T(8,128)} %get-tuple-element.66.refs_2_.refs_4_) | copy-start | bytes 1179652
  30.3 1.8 %collective-permute-start.4 = (f32[768,128]{1,0:T(8,128)S(1)}, f32[768,128]{1,0:T(8,128)S(1)}, u32[]{:S(2)}, u32[]{:S(2)}) collective-permute-start(f32[768,128]{1,0:T(8,128)S(1)} %get-tuple-element.61), channel_id=1, source_target_pairs={{0,16},{16,0},{1,17},{17,1},{2,18},{18,2},{3,19},{19,3},{4,20},{20... | collective-permute-start | bytes 1179656 | tf_op jit(solution)/shard_map/ppermute | solution.py:548
  32.9 29.4 %all-to-all-start = ((f32[32,24,128]{2,1,0:T(8,128)}), f32[32,24,128]{2,1,0:T(8,128)S(1)}, u32[]{:S(2)}, u32[]{:S(2)}) async-start(f32[32,24,128]{2,1,0:T(8,128)} %bitcast.9), calls=%async_computation | async-start | bytes 786432 | tf_op jit(solution)/shard_map/all_to_all | solution.py:632
  50.4 10.5 %collective-permute-start.5 = (f32[2,3,128,128]{3,2,1,0:T(8,128)S(1)}, f32[2,3,128,128]{3,2,1,0:T(8,128)S(1)}, u32[]{:S(2)}, u32[]{:S(2)}) collective-permute-start(f32[2,3,128,128]{3,2,1,0:T(8,128)S(1)} %copy-done.1), channel_id=1, source_target_pairs={{0,16},{16,0},{32,48},{48,32},{64,80},{80,64},{96,112},{112,96},{1... | collective-permute-start | bytes 1179656 | tf_op jit(solution)/shard_map/ppermute | solution.py:540
  51.1 18.7 %collective-permute-start.9 = (f32[2,3,128,128]{3,2,1,0:T(8,128)S(1)}, f32[2,3,128,128]{3,2,1,0:T(8,128)S(1)}, u32[]{:S(2)}, u32[]{:S(2)}) collective-permute-start(f32[2,3,128,128]{3,2,1,0:T(8,128)S(1)} %copy-done.2), channel_id=1, source_target_pairs={{16,32},{48,64},{80,96},{112,128},{144,160},{176,192},{208,224},{3... | collective-permute-start | bytes 1179656 | tf_op jit(solution)/shard_map/ppermute | solution.py:542
  60.9 17.5 %copy-start.3 = (f32[2,3,128,128]{3,2,1,0:T(8,128)}, f32[2,3,128,128]{3,2,1,0:T(8,128)S(1)}, u32[]{:S(2)}) copy-start(f32[2,3,128,128]{3,2,1,0:T(8,128)S(1)} %collective-permute-done.5.refs_4_.refs_6_) | copy-start | bytes 1179652
  62.4 4.4 %collective-permute-start.8 = (f32[24,128]{1,0:T(8,128)S(1)}, f32[24,128]{1,0:T(8,128)S(1)}, u32[]{:S(2)}, u32[]{:S(2)}) collective-permute-start(f32[24,128]{1,0:T(8,128)S(1)} %share.2), channel_id=1, source_target_pairs={{0,40},{8,32},{32,8},{40,0},{1,41},{9,33},{33,9},{41,1},{2,42},{10... | collective-permute-start | bytes 36872 | tf_op jit(solution)/shard_map/ppermute | solution.py:548
  65.7 4.0 %collective-permute-start.7 = (f32[24,128]{1,0:T(8,128)S(1)}, f32[24,128]{1,0:T(8,128)S(1)}, u32[]{:S(2)}, u32[]{:S(2)}) collective-permute-start(f32[24,128]{1,0:T(8,128)S(1)} %share.2), channel_id=1, source_target_pairs={{0,32},{32,0},{1,33},{33,1},{2,34},{34,2},{3,35},{35,3},{4,36},{36... | collective-permute-start | bytes 36872 | tf_op jit(solution)/shard_map/ppermute | solution.py:548
  66.0 3.7 %collective-permute-start.6 = (f32[24,128]{1,0:T(8,128)S(1)}, f32[24,128]{1,0:T(8,128)S(1)}, u32[]{:S(2)}, u32[]{:S(2)}) collective-permute-start(f32[24,128]{1,0:T(8,128)S(1)} %share.2), channel_id=1, source_target_pairs={{0,8},{8,0},{1,9},{9,1},{2,10},{10,2},{3,11},{11,3},{4,12},{12,4},... | collective-permute-start | bytes 36872 | tf_op jit(solution)/shard_map/ppermute | solution.py:548
  69.8 8.6 %copy-start.4 = (f32[2,3,128,128]{3,2,1,0:T(8,128)}, f32[2,3,128,128]{3,2,1,0:T(8,128)S(1)}, u32[]{:S(2)}) copy-start(f32[2,3,128,128]{3,2,1,0:T(8,128)S(1)} %collective-permute-done.9.refs_5_.refs_7_) | copy-start | bytes 1179652
  70.6 25.3 %all-to-all-start.1 = ((f32[32,24,128]{2,1,0:T(8,128)}), f32[32,24,128]{2,1,0:T(8,128)S(1)}, u32[]{:S(2)}, u32[]{:S(2)}) async-start(f32[32,24,128]{2,1,0:T(8,128)} %bitcast.12), calls=%async_computation.1 | async-start | bytes 786432 | tf_op jit(solution)/shard_map/all_to_all | solution.py:643
  81.5 14.5 %collective-permute-start.10 = (f32[2,384,128]{2,1,0:T(8,128)}, f32[2,384,128]{2,1,0:T(8,128)S(1)}, u32[]{:S(2)}, u32[]{:S(2)}) collective-permute-start(f32[2,384,128]{2,1,0:T(8,128)} %get-tuple-element.78), channel_id=1, source_target_pairs={{0,1},{1,0},{2,3},{3,2},{4,5},{5,4},{6,7},{7,6},{8,9},{9,8},{10,11... | collective-permute-start | bytes 1179656 | tf_op jit(solution)/shard_map/ppermute | solution.py:540
  82.8 13.1 %collective-permute-start.11 = (f32[2,384,128]{2,1,0:T(8,128)}, f32[2,384,128]{2,1,0:T(8,128)S(1)}, u32[]{:S(2)}, u32[]{:S(2)}) collective-permute-start(f32[2,384,128]{2,1,0:T(8,128)} %get-tuple-element.79), channel_id=1, source_target_pairs={{1,2},{3,4},{5,6},{7,8},{9,10},{11,12},{13,14},{2,1},{4,3},{6,5},{... | collective-permute-start | bytes 1179656 | tf_op jit(solution)/shard_map/ppermute | solution.py:542
  95.9 3.9 %copy-start.5 = (f32[2,384,128]{2,1,0:T(8,128)}, f32[2,384,128]{2,1,0:T(8,128)S(1)}, u32[]{:S(2)}) copy-start(f32[2,384,128]{2,1,0:T(8,128)S(1)} %collective-permute-done.10.refs_8_) | copy-start | bytes 1179652
  95.9 3.9 %copy-start.6 = (f32[2,384,128]{2,1,0:T(8,128)}, f32[2,384,128]{2,1,0:T(8,128)S(1)}, u32[]{:S(2)}) copy-start(f32[2,384,128]{2,1,0:T(8,128)S(1)} %collective-permute-done.11.refs_9_) | copy-start | bytes 1179652
  95.9 3.9 %collective-permute-start.12 = (f32[768,128]{1,0:T(8,128)S(1)}, f32[768,128]{1,0:T(8,128)S(1)}, u32[]{:S(2)}, u32[]{:S(2)}) collective-permute-start(f32[768,128]{1,0:T(8,128)S(1)} %bitcast.23), channel_id=1, source_target_pairs={{0,16},{16,0},{1,17},{17,1},{2,18},{18,2},{3,19},{19,3},{4,20},{20... | collective-permute-start | bytes 1179656 | tf_op jit(solution)/shard_map/ppermute | solution.py:548
  112.8 11.1 %copy-start.13 = (f32[2,3,64,128]{3,2,1,0:T(8,128)S(1)}, f32[2,3,64,128]{3,2,1,0:T(8,128)}, u32[]{:S(2)}) copy-start(f32[2,3,64,128]{3,2,1,0:T(8,128)} %get-tuple-element.93) | copy-start | bytes 589828
  112.8 11.9 %copy-start.12 = (f32[2,3,64,128]{3,2,1,0:T(8,128)S(1)}, f32[2,3,64,128]{3,2,1,0:T(8,128)}, u32[]{:S(2)}) copy-start(f32[2,3,64,128]{3,2,1,0:T(8,128)} %get-tuple-element.94) | copy-start | bytes 589828
  112.8 1.8 %collective-permute-start.13 = (f32[768,128]{1,0:T(8,128)S(1)}, f32[768,128]{1,0:T(8,128)S(1)}, u32[]{:S(2)}, u32[]{:S(2)}) collective-permute-start(f32[768,128]{1,0:T(8,128)S(1)} %get-tuple-element.88), channel_id=1, source_target_pairs={{0,16},{16,0},{1,17},{17,1},{2,18},{18,2},{3,19},{19,3},{4,20},{20... | collective-permute-start | bytes 1179656 | tf_op jit(solution)/shard_map/ppermute | solution.py:548
  115.4 20.4 %all-to-all-start.2 = ((f32[32,24,128]{2,1,0:T(8,128)}), f32[32,24,128]{2,1,0:T(8,128)S(1)}, u32[]{:S(2)}, u32[]{:S(2)}) async-start(f32[32,24,128]{2,1,0:T(8,128)} %bitcast.14), calls=%async_computation.2 | async-start | bytes 786432 | tf_op jit(solution)/shard_map/all_to_all | solution.py:632
  123.9 8.6 %collective-permute-start.14 = (f32[2,3,64,128]{3,2,1,0:T(8,128)S(1)}, f32[2,3,64,128]{3,2,1,0:T(8,128)S(1)}, u32[]{:S(2)}, u32[]{:S(2)}) collective-permute-start(f32[2,3,64,128]{3,2,1,0:T(8,128)S(1)} %copy-done.13), channel_id=1, source_target_pairs={{0,16},{16,0},{32,48},{48,32},{64,80},{80,64},{96,112},{112,96},{1... | collective-permute-start | bytes 589832 | tf_op jit(solution)/shard_map/ppermute | solution.py:540
  124.6 10.4 %collective-permute-start.15 = (f32[2,3,64,128]{3,2,1,0:T(8,128)S(1)}, f32[2,3,64,128]{3,2,1,0:T(8,128)S(1)}, u32[]{:S(2)}, u32[]{:S(2)}) collective-permute-start(f32[2,3,64,128]{3,2,1,0:T(8,128)S(1)} %copy-done.12), channel_id=1, source_target_pairs={{16,32},{48,64},{80,96},{112,128},{144,160},{176,192},{208,224},{3... | collective-permute-start | bytes 589832 | tf_op jit(solution)/shard_map/ppermute | solution.py:542
  132.5 18.8 %copy-start.7 = (f32[2,3,64,128]{3,2,1,0:T(8,128)}, f32[2,3,64,128]{3,2,1,0:T(8,128)S(1)}, u32[]{:S(2)}) copy-start(f32[2,3,64,128]{3,2,1,0:T(8,128)S(1)} %collective-permute-done.14.refs_2_) | copy-start | bytes 589828
  135.0 16.3 %copy-start.8 = (f32[2,3,64,128]{3,2,1,0:T(8,128)}, f32[2,3,64,128]{3,2,1,0:T(8,128)S(1)}, u32[]{:S(2)}) copy-start(f32[2,3,64,128]{3,2,1,0:T(8,128)S(1)} %collective-permute-done.15.refs_3_) | copy-start | bytes 589828
  135.9 3.8 %collective-permute-start.18 = (f32[24,128]{1,0:T(8,128)S(1)}, f32[24,128]{1,0:T(8,128)S(1)}, u32[]{:S(2)}, u32[]{:S(2)}) collective-permute-start(f32[24,128]{1,0:T(8,128)S(1)} %share.3), channel_id=1, source_target_pairs={{0,40},{8,32},{32,8},{40,0},{1,41},{9,33},{33,9},{41,1},{2,42},{10... | collective-permute-start | bytes 36872 | tf_op jit(solution)/shard_map/ppermute | solution.py:548
  137.7 4.0 %collective-permute-start.17 = (f32[24,128]{1,0:T(8,128)S(1)}, f32[24,128]{1,0:T(8,128)S(1)}, u32[]{:S(2)}, u32[]{:S(2)}) collective-permute-start(f32[24,128]{1,0:T(8,128)S(1)} %share.3), channel_id=1, source_target_pairs={{0,32},{32,0},{1,33},{33,1},{2,34},{34,2},{3,35},{35,3},{4,36},{36... | collective-permute-start | bytes 36872 | tf_op jit(solution)/shard_map/ppermute | solution.py:548
  138.2 3.5 %collective-permute-start.16 = (f32[24,128]{1,0:T(8,128)S(1)}, f32[24,128]{1,0:T(8,128)S(1)}, u32[]{:S(2)}, u32[]{:S(2)}) collective-permute-start(f32[24,128]{1,0:T(8,128)S(1)} %share.3), channel_id=1, source_target_pairs={{0,8},{8,0},{1,9},{9,1},{2,10},{10,2},{3,11},{11,3},{4,12},{12,4},... | collective-permute-start | bytes 36872 | tf_op jit(solution)/shard_map/ppermute | solution.py:548
  142.6 21.1 %all-to-all-start.3 = ((f32[32,24,128]{2,1,0:T(8,128)}), f32[32,24,128]{2,1,0:T(8,128)S(1)}, u32[]{:S(2)}, u32[]{:S(2)}) async-start(f32[32,24,128]{2,1,0:T(8,128)} %bitcast.17), calls=%async_computation.3 | async-start | bytes 786432 | tf_op jit(solution)/shard_map/all_to_all | solution.py:643
  154.3 9.4 %collective-permute-start.19 = (f32[256,128]{1,0:T(8,128)}, f32[256,128]{1,0:T(8,128)S(1)}, u32[]{:S(2)}, u32[]{:S(2)}) collective-permute-start(f32[256,128]{1,0:T(8,128)} %get-tuple-element.104), channel_id=1, source_target_pairs={{0,1},{1,0},{2,3},{3,2},{4,5},{5,4},{6,7},{7,6},{8,9},{9,8},{10,11... | collective-permute-start | bytes 393224 | tf_op jit(solution)/shard_map/ppermute | solution.py:540
  155.6 8.1 %collective-permute-start.20 = (f32[256,128]{1,0:T(8,128)}, f32[256,128]{1,0:T(8,128)S(1)}, u32[]{:S(2)}, u32[]{:S(2)}) collective-permute-start(f32[256,128]{1,0:T(8,128)} %get-tuple-element.105), channel_id=1, source_target_pairs={{1,2},{3,4},{5,6},{7,8},{9,10},{11,12},{13,14},{2,1},{4,3},{6,5},{... | collective-permute-start | bytes 393224 | tf_op jit(solution)/shard_map/ppermute | solution.py:542
  163.7 5.2 %copy-start.9 = (f32[256,128]{1,0:T(8,128)}, f32[256,128]{1,0:T(8,128)S(1)}, u32[]{:S(2)}) copy-start(f32[256,128]{1,0:T(8,128)S(1)} %collective-permute-done.19.refs_3_) | copy-start | bytes 393220
  163.7 5.2 %copy-start.10 = (f32[256,128]{1,0:T(8,128)}, f32[256,128]{1,0:T(8,128)S(1)}, u32[]{:S(2)}) copy-start(f32[256,128]{1,0:T(8,128)S(1)} %collective-permute-done.20.refs_4_) | copy-start | bytes 393220
  163.7 5.2 %collective-permute-start.21 = (f32[768,128]{1,0:T(8,128)S(1)}, f32[768,128]{1,0:T(8,128)S(1)}, u32[]{:S(2)}, u32[]{:S(2)}) collective-permute-start(f32[768,128]{1,0:T(8,128)S(1)} %bitcast.25), channel_id=1, source_target_pairs={{0,16},{16,0},{1,17},{17,1},{2,18},{18,2},{3,19},{19,3},{4,20},{20... | collective-permute-start | bytes 1179656 | tf_op jit(solution)/shard_map/ppermute | solution.py:548

commit v5 on v4

--- a/solution.py
+++ b/solution.py
@@ -152,51 +152,89 @@
     return jnp.sum(probe_ref[0] * probe_ref[0] + probe_ref[1] * probe_ref[1], axis=0)
 
 
-def join_rows_kernel(
-    copies, at_ref, obj_ref, row_a_ref, row_b_ref, tag_ref, tall_ref, col_a_ref, col_b_ref, tags_ref
-):
-    band = row_a_ref.shape[1] - 8
+def side_by_side(cells, lane):
+    n = lane.shape[1]
+    half = n // 2
+    size = cells.shape[2]
+    left = jnp.where(lane < half, cells[0, :, :n], pltpu.roll(cells[1, :, :n], half, 1))
+    right = jnp.where(lane < half, pltpu.roll(cells[0, :, size - n :], half, 1), cells[1, :, size - n :])
+    return left, right
+
+
+def pack_kernel(copies, at_ref, obj_ref, tag_ref, row_a_ref, row_b_ref, col_a_ref, col_b_ref):
     size = obj_ref.shape[1]
     n = col_a_ref.shape[1]
-    extent = tall_ref.shape[1]
-    upper, lower = ordered(at_ref[5] == 1, row_a_ref[...], row_b_ref[...])
-    tall_ref[:, :band] = upper[:, :band]
-    tall_ref[:, band + size :] = lower[:, :band]
-    tags_ref[...] = jnp.zeros_like(tags_ref)
-    tags_ref[:1] = upper[0, band : band + 1, :n]
-    tags_ref[1:2] = tag_ref[:1]
-    tags_ref[2:3] = lower[0, band : band + 1, :n]
+    half = n // 2
     copies.need(obj_ref)
-    tall_ref[:, band : band + size] = obj_ref[...]
-    lane = lax.broadcasted_iota(jnp.int32, (extent, n), 1)
-    left = jnp.where(lane < band, tall_ref[0, :, :n], pltpu.roll(tall_ref[1, :, :n], band, 1))
-    right = jnp.where(lane < band, pltpu.roll(tall_ref[0, :, size - n :], band, 1), tall_ref[1, :, size - n :])
-    col_a_ref[:extent], col_b_ref[:extent] = ordered(at_ref[6] == 1, left, right)
-    col_a_ref[extent:] = tags_ref[...]
-    col_b_ref[extent:] = tags_ref[...]
+    row_a_ref[:, :half], row_b_ref[:, :half] = ordered(at_ref[5] == 1, obj_ref[:, :half], obj_ref[:, size - half :])
+    for ref in (row_a_ref, row_b_ref):
+        ref[:, half:] = jnp.zeros((2, 8, size), F32)
+        ref[0, half:, :n] = tag_ref[...]
+    lane = lax.broadcasted_iota(jnp.int32, (size, n), 1)
+    left, right = side_by_side(obj_ref[...], lane)
+    col_a_ref[:size], col_b_ref[:size] = ordered(at_ref[6] == 1, left, right)
+    col_a_ref[size:] = tag_ref[...]
+    col_b_ref[size:] = tag_ref[...]
+
+
+def corner_kernel(copies, at_ref, row_a_ref, row_b_ref, end_a_ref, end_b_ref):
+    n = end_a_ref.shape[1]
+    half = n // 2
+    lane = lax.broadcasted_iota(jnp.int32, (half, n), 1)
+    rows = ordered(at_ref[5] == 1, row_a_ref[...], row_b_ref[...])
+    for j, strip in enumerate(rows):
+        left, right = side_by_side(strip[:, :half], lane)
+        part = slice(j * half, (j + 1) * half)
+        end_a_ref[part], end_b_ref[part] = ordered(at_ref[6] == 1, left, right)
+    for ref in (end_a_ref, end_b_ref):
+        ref[n:] = jnp.zeros((8, n), F32)
+        for j, strip in enumerate(rows):
+            ref[n + j : n + j + 1] = strip[0, half : half + 1, :n]
 
 
 def first_kernel(
-    copies, off_ref, at_ref, tall_ref, col_a_ref, col_b_ref, probe_ref, meas_ref, fwd_ref, bwd_ref,
-    first_ref, second_ref, mid_ref, keep_ref, send_ref, cells, bright_ref, canvas, grads,
+    copies, off_ref, at_ref, obj_ref, tag_ref,
+    row_a_ref, row_b_ref, col_a_ref, col_b_ref, end_a_ref, end_b_ref,
+    probe_ref, meas_ref, fwd_ref, bwd_ref,
+    first_ref, second_ref, mid_ref, keep_ref, send_ref, cells, bright_ref, tags_ref, canvas, grads,
 ):
     n = probe_ref.shape[2]
     half = n // 2
-    extent = tall_ref.shape[1]
-    lane = lax.broadcasted_iota(jnp.int32, (extent, n), 1)
+    size = obj_ref.shape[1]
+    odd_row = at_ref[5] == 1
+    odd_col = at_ref[6] == 1
     canvas[...] = jnp.zeros_like(canvas)
     bright_ref[...] = brightness(probe_ref)
     copies.ready(bright_ref)
-    before, after = ordered(at_ref[6] == 1, col_a_ref[:extent], col_b_ref[:extent])
-    strips = [
-        (before, pltpu.roll(after, half, 1)),
-        (pltpu.roll(before, half, 1), after),
-    ]
-    for ch in range(2):
-        inner = [pltpu.roll(tall_ref[ch, :, k * n : (k + 1) * n], half, 1) for k in range(2)]
-        row = [strips[ch][0], *inner, strips[ch][1]]
-        for k in range(3):
-            cells[ch, k] = jnp.where(lane < half, row[k], row[k + 1])
+    upper, lower = ordered(odd_row, row_a_ref[...], row_b_ref[...])
+    before, after = ordered(odd_col, col_a_ref[...], col_b_ref[...])
+    ends = ordered(odd_col, end_a_ref[...], end_b_ref[...])
+    over = [x[:half] for x in ends]
+    under = [x[half:n] for x in ends]
+    tags_ref[...] = jnp.zeros_like(tags_ref)
+    tags_ref[:9] = jnp.concatenate(
+        [
+            ends[0][n : n + 1], before[size : size + 1], ends[0][n + 1 : n + 2],
+            upper[0, half : half + 1, :n], tag_ref[:1], lower[0, half : half + 1, :n],
+            ends[1][n : n + 1], after[size : size + 1], ends[1][n + 1 : n + 2],
+        ],
+        0,
+    )
+    copies.need(obj_ref)
+    bands = (
+        (0, half, upper[:, :half], over[0], over[1]),
+        (half, size, obj_ref[...], before[:size], after[:size]),
+        (half + size, half, lower[:, :half], under[0], under[1]),
+    )
+    for start, count, centre, left, right in bands:
+        rows = slice(start, start + count)
+        lane = lax.broadcasted_iota(jnp.int32, (count, n), 1)
+        strips = [(left, pltpu.roll(right, half, 1)), (pltpu.roll(left, half, 1), right)]
+        for ch in range(2):
+            inner = [pltpu.roll(centre[ch, :, k * n : (k + 1) * n], half, 1) for k in range(2)]
+            row = [strips[ch][0], *inner, strips[ch][1]]
+            for k in range(3):
+                cells[ch, k, rows] = jnp.where(lane < half, row[k], row[k + 1])
     copies.ready(cells)
     copies.need(fwd_ref, bwd_ref)
     sweep_positions(copies, off_ref, probe_ref, meas_ref, fwd_ref, bwd_ref, cells, canvas, grads)
@@ -535,12 +573,18 @@
     return functools.reduce(lambda a, b: a * b, [lax.axis_size(axis) for axis in axes])
 
 
+def pairs_first(count):
+    return [(i, i ^ 1) for i in range(count)]
+
+
+def pairs_second(count):
+    pairs = [(i, i + 1) for i in range(1, count - 1, 2)]
+    return pairs + [(j, i) for i, j in pairs]
+
+
 def exchange(first, second, axes):
     count = length(axes)
-    first = lax.ppermute(first, axes, [(i, i ^ 1) for i in range(count)])
-    pairs = [(i, i + 1) for i in range(1, count - 1, 2)]
-    second = lax.ppermute(second, axes, pairs + [(j, i) for i, j in pairs])
-    return first, second
+    return lax.ppermute(first, axes, pairs_first(count)), lax.ppermute(second, axes, pairs_second(count))
 
 
 def swap(value, axes):
@@ -585,25 +629,16 @@
 
     tag = (offsets + 1).astype(F32).reshape(1, 2 * positions)
     tag_rows = jnp.pad(tag, ((0, 7), (0, n - 2 * positions)))
-    tag_block = jnp.pad(tag[None], ((0, 1), (0, 7), (0, tile - 2 * positions)))
-    low = (1 - row % 2) * (tile - half)
-    first = lax.dynamic_slice_in_dim(object_field, low, half, 1)
-    second = lax.dynamic_slice_in_dim(object_field, tile - half - low, half, 1)
-    row_a, row_b = exchange(*(jnp.concatenate([x, tag_block], 1) for x in (first, second)), ROW)
-    strip = (extent + 8, n)
-    tall, col_a, col_b, own = call(
-        join_rows_kernel,
-        [(2, extent, tile), strip, strip, (8, n)],
-        [],
-        [info, Far(object_field), row_a, row_b, tag_rows],
-        1,
-        "join_rows",
+    edge = (2, half + 8, tile)
+    side = (tile + 8, n)
+    ends = (n + 8, n)
+    row_a, row_b, col_a, col_b = call(
+        pack_kernel, [edge, edge, side, side], [], [info, Far(object_field), tag_rows], 1, "pack_edges"
     )
+    row_a, row_b = exchange(row_a, row_b, ROW)
     col_a, col_b = exchange(col_a, col_b, COL)
-    odd = col % 2 == 1
-    before, after = ordered(odd, col_a[extent : extent + 3, :32], col_b[extent : extent + 3, :32])
-    tags = jnp.concatenate([before, own[:3, :32], after], 0)
-    tags = tags.astype(jnp.int32)
+    end_a, end_b = call(corner_kernel, [ends, ends], [], [info, row_a, row_b], 1, "pack_ends")
+    halo = [row_a, row_b, col_a, col_b, *exchange(end_a, end_b, COL)]
 
     cells = (2, blocks, extent, n)
     canvas = (blocks + 2, extent + 2 * n, n)
@@ -619,14 +654,17 @@
         bands = [(2, blocks, x, n) for x in ((half, half, tile) if last else (n, n, n))]
         outs = [Raw(x) for x in bands] + [packed, packed, Far(cells), Far((n, n))]
         if sweep == 0:
-            args = [offsets, info, tall, col_a, col_b, probes, amplitudes, *tables]
-            first, second, mid, keep, send, cells_now, bright = call(first_kernel, outs, [cells, grads], args, 2, "first_sweep")
+            args = [offsets, info, Far(object_field), tag_rows, *halo, probes, amplitudes, *tables]
+            outs = outs + [(16, n)]
+            first, second, mid, keep, send, cells_now, bright, tags = call(first_kernel, outs, [cells, grads], args, 2, "first_sweep")
         else:
             held = [Far(x) for x in (cells_now, *sums, light)]
             args = [offsets, info, *held, mine, other, Far(probes), amplitudes, *tables]
             first, second, mid, keep, send, cells_now, bright, probes = call(
                 next_kernel, outs + [Far(probes.shape)], [cells, grads], args, 2, "next_sweep"
             )
+        if sweep == 0:
+            tags = tags[:9, : 2 * positions].astype(jnp.int32)
         received = swap(send, ("core",))
         received, first, second, bright = lax.optimization_barrier((received, first, second, bright))
         parts = lax.all_to_all(keep + received, RING, 0, 0, tiled=True)

time: 174 us -> 172 us (0.989)
  waiting for transfers between devices: 38 us -> 34.7 us
    ppermute x12 -> x14, waiting for transfers between devices: 24.1 us -> 20.3 us  [the longest x7 15 us: exchange(): lax.ppermute(first, axes, pairs_first(count))]
    pallas_call x11 -> x12, Pallas kernels: 48.5 us -> 49.6 us  [call(): pl.pallas_call(whole, out_shape=tuple((pltpu.HBM(x, F32) if is_far else j...]
    ppermute x12 -> x14, starting transfers between devices: 23.1 us -> 24.1 us  [the longest x7 13.3 us: exchange(): lax.ppermute(second, axes, pairs_second(count))]
  transfers between devices with their start and end apart: 26 -> 28, of which waited for: 15 -> 15; matrix products, arithmetic and copies ran while one was open for 0% -> 0% of each run, Pallas kernels for 11% -> 12%
where the time goes in v5:
time: 172 us; the launch traced here: 171 us
  starting transfers between devices  80.2 us (47%)
  Pallas kernels  49.6 us (29%)
  waiting for transfers between devices  34.7 us (20%)
  local copies, waits for them, and re-layouts  2.68 us (2%)
  other arithmetic  2.49 us (1%)
    pallas_call x12, Pallas kernels, call(): pl.pallas_call(whole, out_shape=tuple((pltpu.HBM(x, F32) if is_far else j...  49.6 us
    all_to_all x2, starting transfers between devices, body(): parts = lax.all_to_all(keep + received, RING, 0, 0, tiled=True)  24.9 us
    all_to_all x2, starting transfers between devices, body(): mine = lax.all_to_all(copies, RING, 0, 0, tiled=True)  16.8 us
    ppermute x7, waiting for transfers between devices, exchange(): lax.ppermute(first, axes, pairs_first(count))  15 us
    ppermute x10, starting transfers between devices, swap(): return lax.ppermute(value, axes, [(i, count - 1 - i) for i in range(count)])  14.3 us
    ppermute x7, starting transfers between devices, exchange(): lax.ppermute(second, axes, pairs_second(count))  13.3 us
    ppermute x7, starting transfers between devices, exchange(): lax.ppermute(first, axes, pairs_first(count))  10.8 us
    ppermute x10, waiting for transfers between devices, swap(): return lax.ppermute(value, axes, [(i, count - 1 - i) for i in range(count)])  10.7 us
  transfers between devices with their start and end apart: 28, of which 15 were waited for; matrix products, arithmetic and copies ran while one was open for 0% of the time, Pallas kernels for 12%

profile of v5, /device:TPU:1, one launch (start us, length us, event | category | flops | bytes accessed | tf_op | source)
XLA Modules:
  0.0 170.8 jit_solution(17260135622118004388)
XLA Ops:
  0.7 0.7 add_convert_fusion
  1.4 0.1 copy.11
  1.5 0.1 convert_element_type.19
  1.6 0.1 stack.31.refs_0_.refs_1_
  1.7 1.7 %pack_edges.1 = (f32[2,72,256]{2,1,0:T(8,128)S(1)}, f32[2,72,256]{2,1,0:T(8,128)S(1)}, f32[264,128]{1,0:T(8,128)S(1)}, f32[264,128]{1,0:T(8,128)S(1)}) custom-call(s32[7]{0:T(128)S(1)} %stack.31.refs_0_.refs_1_, f32[2,256,256]{2,1,0:T(8,128)} %refs_2_.1, f32[8,128]{1,0:T(8,128)S(1)} %pad.4.refs_2_.refs_3_), custom_call_target="tpu_custom_call" | custom-call | tf_op jit(solution)/shard_map/pack_edges/pallas_call | solution.py:557
  3.5 3.3 %collective-permute-start = (f32[2,72,256]{2,1,0:T(8,128)S(1)}, f32[2,72,256]{2,1,0:T(8,128)S(1)}, u32[]{:S(2)}, u32[]{:S(2)}) collective-permute-start(f32[2,72,256]{2,1,0:T(8,128)S(1)} %get-tuple-element.60), channel_id=1, source_target_pairs={{0,16},{16,0},{32,48},{48,32},{64,80},{80,64},{96,112},{112,96},{1... | collective-permute-start | bytes 442376 | tf_op jit(solution)/shard_map/ppermute | solution.py:587
  6.8 2.8 %collective-permute-start.1 = (f32[2,72,256]{2,1,0:T(8,128)S(1)}, f32[2,72,256]{2,1,0:T(8,128)S(1)}, u32[]{:S(2)}, u32[]{:S(2)}) collective-permute-start(f32[2,72,256]{2,1,0:T(8,128)S(1)} %get-tuple-element.61), channel_id=1, source_target_pairs={{16,32},{48,64},{80,96},{112,128},{144,160},{176,192},{208,224},{3... | collective-permute-start | bytes 442376 | tf_op jit(solution)/shard_map/ppermute | solution.py:587
  9.6 1.7 %collective-permute-start.2 = (f32[264,128]{1,0:T(8,128)S(1)}, f32[264,128]{1,0:T(8,128)S(1)}, u32[]{:S(2)}, u32[]{:S(2)}) collective-permute-start(f32[264,128]{1,0:T(8,128)S(1)} %get-tuple-element.62), channel_id=1, source_target_pairs={{0,1},{1,0},{2,3},{3,2},{4,5},{5,4},{6,7},{7,6},{8,9},{9,8},{10,11... | collective-permute-start | bytes 405512 | tf_op jit(solution)/shard_map/ppermute | solution.py:587
  11.3 0.7 collective-permute-start.3
  12.0 2.9 %collective-permute-done.1.refs_2_.refs_5_ = f32[2,72,256]{2,1,0:T(8,128)S(1)} collective-permute-done((f32[2,72,256]{2,1,0:T(8,128)S(1)}, f32[2,72,256]{2,1,0:T(8,128)S(1)}, u32[]{:S(2)}, u32[]{:S(2)}) %collective-permute-start.1) | collective-permute-done | bytes 147488 | tf_op jit(solution)/shard_map/ppermute | solution.py:587
  14.9 0.7 pack_ends.1
  15.6 1.7 collective-permute-start.4
  17.3 0.7 collective-permute-start.5
  17.9 0.8 copy.13.refs_0_
  18.7 0.3 collective-permute-done.4.refs_8_
  19.0 11.2 %first_sweep.1 = (f32[2,3,128,128]{3,2,1,0:T(8,128)}, f32[2,3,128,128]{3,2,1,0:T(8,128)}, f32[2,3,128,128]{3,2,1,0:T(8,128)}, f32[768,128]{1,0:T(8,128)S(1)}, f3...) custom-call(s32[16,2]{1,0:T(8,128)S(1)} %copy.13.refs_0_, ...), custom_call_target="tpu_custom_call" | custom-call | tf_op jit(solution)/shard_map/first_sweep/pallas_call | solution.py:557
  30.2 0.1 collective-permute-start.6
  30.3 1.7 %collective-permute-done.6 = f32[768,128]{1,0:T(8,128)S(1)} collective-permute-done((f32[768,128]{1,0:T(8,128)S(1)}, f32[768,128]{1,0:T(8,128)S(1)}, u32[]{:S(2)}, u32[]{:S(2)}) %collective-permute-start.6) | collective-permute-done | bytes 393248 | tf_op jit(solution)/shard_map/ppermute | solution.py:592
  32.0 0.8 add.63
  32.8 16.3 %all-to-all-start = ((f32[32,24,128]{2,1,0:T(8,128)}), f32[32,24,128]{2,1,0:T(8,128)S(1)}, u32[]{:S(2)}, u32[]{:S(2)}) async-start(f32[32,24,128]{2,1,0:T(8,128)} %bitcast.9), calls=%async_computation | async-start | bytes 786432 | tf_op jit(solution)/shard_map/all_to_all | solution.py:670
  49.1 0.7 collective-permute-start.7
  49.8 3.9 %collective-permute-start.11 = (f32[2,3,128,128]{3,2,1,0:T(8,128)S(1)}, f32[2,3,128,128]{3,2,1,0:T(8,128)S(1)}, u32[]{:S(2)}, u32[]{:S(2)}) collective-permute-start(f32[2,3,128,128]{3,2,1,0:T(8,128)S(1)} %copy-done.2), channel_id=1, source_target_pairs={{16,32},{48,64},{80,96},{112,128},{144,160},{176,192},{208,224},{3... | collective-permute-start | bytes 1179656 | tf_op jit(solution)/shard_map/ppermute | solution.py:587
  53.8 4.3 %light.2 = (f32[3,384,128]{2,1,0:T(8,128)}, f32[8,128]{1,0:T(8,128)S(1)}) custom-call(s32[9,32]{1,0:T(8,128)S(1)} %slice_convert_fusion.refs_0_, f32[128,128]{1,0:T(8,128)} %get-tuple-element.78.refs_1_), custom_call_target="tpu_custom_call" | custom-call | tf_op jit(solution)/shard_map/light/pallas_call | solution.py:557
  58.2 2.9 %all-to-all-done = f32[32,24,128]{2,1,0:T(8,128)S(1)} async-done(((f32[32,24,128]{2,1,0:T(8,128)}), f32[32,24,128]{2,1,0:T(8,128)S(1)}, u32[]{:S(2)}, u32[]{:S(2)}) %all-to-all-start) | async-done | bytes 393248 | tf_op jit(solution)/shard_map/all_to_all | solution.py:670
  61.1 1.7 %collective-permute-start.10 = (f32[24,128]{1,0:T(8,128)S(1)}, f32[24,128]{1,0:T(8,128)S(1)}, u32[]{:S(2)}, u32[]{:S(2)}) collective-permute-start(f32[24,128]{1,0:T(8,128)S(1)} %share.2), channel_id=1, source_target_pairs={{0,40},{8,32},{32,8},{40,0},{1,41},{9,33},{33,9},{41,1},{2,42},{10... | collective-permute-start | bytes 36872 | tf_op jit(solution)/shard_map/ppermute | solution.py:592
  62.8 1.3 collective-permute-start.9
  64.2 0.3 collective-permute-start.8
  64.4 0.5 collective-permute-done.10
  64.9 1.9 %collective-permute-done.9 = f32[24,128]{1,0:T(8,128)S(1)} collective-permute-done((f32[24,128]{1,0:T(8,128)S(1)}, f32[24,128]{1,0:T(8,128)S(1)}, u32[]{:S(2)}, u32[]{:S(2)}) %collective-permute-start.9) | collective-permute-done | bytes 12320 | tf_op jit(solution)/shard_map/ppermute | solution.py:592
  66.9 0.1 maximum_select_fusion.1
  67.0 0.8 broadcast_in_dim.4
  67.8 7.7 %all-to-all-start.1 = ((f32[32,24,128]{2,1,0:T(8,128)}), f32[32,24,128]{2,1,0:T(8,128)S(1)}, u32[]{:S(2)}, u32[]{:S(2)}) async-start(f32[32,24,128]{2,1,0:T(8,128)} %bitcast.12), calls=%async_computation.1 | async-start | bytes 786432 | tf_op jit(solution)/shard_map/all_to_all | solution.py:681
  75.6 3.0 %fold_rows.1 = (f32[2,384,128]{2,1,0:T(8,128)}, f32[2,384,128]{2,1,0:T(8,128)}) custom-call(s32[7]{0:T(128)S(1)} %stack.31.refs_0_.refs_1_, f32[2,3,128,128]{3,2,1,0:T(8,128)} %get-tuple-element.71.refs_1_.refs_3_, f32[2,3,128,128]{3,2,1,0:T(8,128)} %get-tuple-element.72.refs_2_.refs_4_, f32[2,3,128,128]{3,2,1,0:T(8,128)} %get-tuple-element.73.refs_3_.refs_5_, ...), custom_call_target="tpu_custom_call" | custom-call | tf_op jit(solution)/shard_map/fold_rows/pallas_call | solution.py:557
  78.6 1.3 collective-permute-start.12
  79.9 0.9 collective-permute-start.13
  80.8 4.3 %more_light.1.refs_10_ = f32[3,384,128]{2,1,0:T(8,128)} custom-call(s32[9,32]{1,0:T(8,128)S(1)} %slice_convert_fusion.refs_0_, f32[128,128]{1,0:T(8,128)} %get-tuple-element.78.refs_1_, f32[3,384,128]{2,1,0:T(8,128)} %get-tuple-element.86.refs_2_), custom_call_target="tpu_custom_call" | custom-call | tf_op jit(solution)/shard_map/more_light/pallas_call | solution.py:557
  85.1 8.0 %collective-permute-done.12.refs_8_ = f32[2,384,128]{2,1,0:T(8,128)S(1)} collective-permute-done((f32[2,384,128]{2,1,0:T(8,128)}, f32[2,384,128]{2,1,0:T(8,128)S(1)}, u32[]{:S(2)}, u32[]{:S(2)}) %collective-permute-start.12) | collective-permute-done | bytes 393248 | tf_op jit(solution)/shard_map/ppermute | solution.py:587
  93.1 2.4 %collective-permute-start.14 = (f32[768,128]{1,0:T(8,128)S(1)}, f32[768,128]{1,0:T(8,128)S(1)}, u32[]{:S(2)}, u32[]{:S(2)}) collective-permute-start(f32[768,128]{1,0:T(8,128)S(1)} %bitcast.21), channel_id=1, source_target_pairs={{0,16},{16,0},{1,17},{17,1},{2,18},{18,2},{3,19},{19,3},{4,20},{20... | collective-permute-start | bytes 1179656 | tf_op jit(solution)/shard_map/ppermute | solution.py:592
  95.4 1.3 collective-permute-done.14.refs_12_
  96.8 13.0 %next_sweep.1 = (f32[2,3,64,128]{3,2,1,0:T(8,128)}, f32[2,3,64,128]{3,2,1,0:T(8,128)}, f32[2,3,256,128]{3,2,1,0:T(8,128)}, f32[768,128]{1,0:T(8,128)S(1)}, f32[7...) custom-call(s32[16,2]{1,0:T(8,128)S(1)} %copy.13.refs_0_, ...), custom_call_target="tpu_custom_call" | custom-call | tf_op jit(solution)/shard_map/next_sweep/pallas_call | solution.py:557
  109.8 0.4 collective-permute-start.15
  110.2 1.4 collective-permute-done.15
  111.6 0.8 add.67
  112.4 8.6 %all-to-all-start.2 = ((f32[32,24,128]{2,1,0:T(8,128)}), f32[32,24,128]{2,1,0:T(8,128)S(1)}, u32[]{:S(2)}, u32[]{:S(2)}) async-start(f32[32,24,128]{2,1,0:T(8,128)} %bitcast.14), calls=%async_computation.2 | async-start | bytes 786432 | tf_op jit(solution)/shard_map/all_to_all | solution.py:670
  121.1 0.7 collective-permute-start.16
  121.8 3.7 %collective-permute-start.17 = (f32[2,3,64,128]{3,2,1,0:T(8,128)S(1)}, f32[2,3,64,128]{3,2,1,0:T(8,128)S(1)}, u32[]{:S(2)}, u32[]{:S(2)}) collective-permute-start(f32[2,3,64,128]{3,2,1,0:T(8,128)S(1)} %copy-done.11), channel_id=1, source_target_pairs={{16,32},{48,64},{80,96},{112,128},{144,160},{176,192},{208,224},{3... | collective-permute-start | bytes 589832 | tf_op jit(solution)/shard_map/ppermute | solution.py:587
  125.5 4.3 %light.3 = (f32[3,384,128]{2,1,0:T(8,128)}, f32[8,128]{1,0:T(8,128)S(1)}) custom-call(s32[9,32]{1,0:T(8,128)S(1)} %slice_convert_fusion.refs_0_, f32[128,128]{1,0:T(8,128)} %get-tuple-element.102.refs_1_), custom_call_target="tpu_custom_call" | custom-call | tf_op jit(solution)/shard_map/light/pallas_call | solution.py:557
  129.9 2.3 %collective-permute-done.17.refs_3_ = f32[2,3,64,128]{3,2,1,0:T(8,128)S(1)} collective-permute-done((f32[2,3,64,128]{3,2,1,0:T(8,128)S(1)}, f32[2,3,64,128]{3,2,1,0:T(8,128)S(1)}, u32[]{:S(2)}, u32[]{:S(2)}) %collective-permute-start.17) | collective-permute-done | bytes 196640 | tf_op jit(solution)/shard_map/ppermute | solution.py:587
  132.2 0.9 all-to-all-done.2
  133.1 1.7 collective-permute-start.20
  134.8 1.1 collective-permute-start.19
  135.9 0.5 collective-permute-start.18
  136.4 0.5 collective-permute-done.20
  136.9 1.9 %collective-permute-done.19 = f32[24,128]{1,0:T(8,128)S(1)} collective-permute-done((f32[24,128]{1,0:T(8,128)S(1)}, f32[24,128]{1,0:T(8,128)S(1)}, u32[]{:S(2)}, u32[]{:S(2)}) %collective-permute-start.19) | collective-permute-done | bytes 12320 | tf_op jit(solution)/shard_map/ppermute | solution.py:592
  138.8 0.1 maximum_select_fusion
  138.9 0.8 broadcast_in_dim.5
  139.7 9.1 %all-to-all-start.3 = ((f32[32,24,128]{2,1,0:T(8,128)}), f32[32,24,128]{2,1,0:T(8,128)S(1)}, u32[]{:S(2)}, u32[]{:S(2)}) async-start(f32[32,24,128]{2,1,0:T(8,128)} %bitcast.17), calls=%async_computation.3 | async-start | bytes 786432 | tf_op jit(solution)/shard_map/all_to_all | solution.py:681
  148.8 2.9 %fold_inner.1 = (f32[2,3,256,128]{3,2,1,0:T(8,128)}, f32[256,128]{1,0:T(8,128)}, f32[256,128]{1,0:T(8,128)}) custom-call(s32[7]{0:T(128)S(1)} %stack.31.refs_0_.refs_1_, f32[2,3,256,128]{3,2,1,0:T(8,128)} %get-tuple-element.92.refs_1_, f32[2,3,64,128]{3,2,1,0:T(8,128)} %copy-done.7, f32[2,3,64,128]{3,2,1,0:T(8,128)} %copy-done.8), custom_call_target="tpu_custom_call" | custom-call | tf_op jit(solution)/shard_map/fold_inner/pallas_call | solution.py:557
  151.7 1.3 collective-permute-start.21
  153.0 0.7 collective-permute-start.22
  153.7 6.8 %collective-permute-done.21.refs_3_ = f32[256,128]{1,0:T(8,128)S(1)} collective-permute-done((f32[256,128]{1,0:T(8,128)}, f32[256,128]{1,0:T(8,128)S(1)}, u32[]{:S(2)}, u32[]{:S(2)}) %collective-permute-start.21) | collective-permute-done | bytes 131104 | tf_op jit(solution)/shard_map/ppermute | solution.py:587
  160.5 4.8 %collective-permute-start.23 = (f32[768,128]{1,0:T(8,128)S(1)}, f32[768,128]{1,0:T(8,128)S(1)}, u32[]{:S(2)}, u32[]{:S(2)}) collective-permute-start(f32[768,128]{1,0:T(8,128)S(1)} %bitcast.23), channel_id=1, source_target_pairs={{0,16},{16,0},{1,17},{17,1},{2,18},{18,2},{3,19},{19,3},{4,20},{20... | collective-permute-start | bytes 1179656 | tf_op jit(solution)/shard_map/ppermute | solution.py:592
  165.3 1.3 collective-permute-done.23.refs_7_
  166.6 4.1 %last_update.1 = (f32[2,256,256]{2,1,0:T(8,128)}, f32[2,4,128,128]{3,2,1,0:T(8,128)}) custom-call(s32[7]{0:T(128)S(1)} %stack.31.refs_0_.refs_1_, f32[2,3,384,128]{3,2,1,0:T(8,128)} %get-tuple-element.91.refs_1_, f32[2,3,256,128]{3,2,1,0:T(8,128)} %get-tuple-element.108.refs_2_, f32[256,128]{1,0:T(8,128)} %copy-done.9, f32[256,128]{1,0:T(8,128)} %copy-done.10, ...), custom_call_target="tpu_custom_call" | custom-call | tf_op jit(solution)/shard_map/last_update/pallas_call | solution.py:557
  (44 shorter events, 0.2 us)
Async XLA Ops:
  0.6 18.4 %copy-start = (f32[2,4,128,128]{3,2,1,0:T(8,128)S(1)}, f32[2,4,128,128]{3,2,1,0:T(8,128)}, u32[]{:S(2)}) copy-start(f32[2,4,128,128]{3,2,1,0:T(8,128)} %refs_13_.2) | copy-start | bytes 1572868
  3.5 8.5 %collective-permute-start = (f32[2,72,256]{2,1,0:T(8,128)S(1)}, f32[2,72,256]{2,1,0:T(8,128)S(1)}, u32[]{:S(2)}, u32[]{:S(2)}) collective-permute-start(f32[2,72,256]{2,1,0:T(8,128)S(1)} %get-tuple-element.60), channel_id=1, source_target_pairs={{0,16},{16,0},{32,48},{48,32},{64,80},{80,64},{96,112},{112,96},{1... | collective-permute-start | bytes 442376 | tf_op jit(solution)/shard_map/ppermute | solution.py:587
  6.8 8.1 %collective-permute-start.1 = (f32[2,72,256]{2,1,0:T(8,128)S(1)}, f32[2,72,256]{2,1,0:T(8,128)S(1)}, u32[]{:S(2)}, u32[]{:S(2)}) collective-permute-start(f32[2,72,256]{2,1,0:T(8,128)S(1)} %get-tuple-element.61), channel_id=1, source_target_pairs={{16,32},{48,64},{80,96},{112,128},{144,160},{176,192},{208,224},{3... | collective-permute-start | bytes 442376 | tf_op jit(solution)/shard_map/ppermute | solution.py:587
  9.6 9.1 %collective-permute-start.2 = (f32[264,128]{1,0:T(8,128)S(1)}, f32[264,128]{1,0:T(8,128)S(1)}, u32[]{:S(2)}, u32[]{:S(2)}) collective-permute-start(f32[264,128]{1,0:T(8,128)S(1)} %get-tuple-element.62), channel_id=1, source_target_pairs={{0,1},{1,0},{2,3},{3,2},{4,5},{5,4},{6,7},{7,6},{8,9},{9,8},{10,11... | collective-permute-start | bytes 405512 | tf_op jit(solution)/shard_map/ppermute | solution.py:587
  11.3 7.4 %collective-permute-start.3 = (f32[264,128]{1,0:T(8,128)S(1)}, f32[264,128]{1,0:T(8,128)S(1)}, u32[]{:S(2)}, u32[]{:S(2)}) collective-permute-start(f32[264,128]{1,0:T(8,128)S(1)} %get-tuple-element.63), channel_id=1, source_target_pairs={{1,2},{3,4},{5,6},{7,8},{9,10},{11,12},{13,14},{2,1},{4,3},{6,5},{... | collective-permute-start | bytes 405512 | tf_op jit(solution)/shard_map/ppermute | solution.py:587
  15.6 3.4 %collective-permute-start.4 = (f32[136,128]{1,0:T(8,128)S(1)}, f32[136,128]{1,0:T(8,128)S(1)}, u32[]{:S(2)}, u32[]{:S(2)}) collective-permute-start(f32[136,128]{1,0:T(8,128)S(1)} %get-tuple-element.64), channel_id=1, source_target_pairs={{0,1},{1,0},{2,3},{3,2},{4,5},{5,4},{6,7},{7,6},{8,9},{9,8},{10,11... | collective-permute-start | bytes 208904 | tf_op jit(solution)/shard_map/ppermute | solution.py:587
  17.3 1.7 collective-permute-start.5
  30.1 18.9 %copy-start.1 = (f32[2,3,128,128]{3,2,1,0:T(8,128)S(1)}, f32[2,3,128,128]{3,2,1,0:T(8,128)}, u32[]{:S(2)}) copy-start(f32[2,3,128,128]{3,2,1,0:T(8,128)} %get-tuple-element.71.refs_1_.refs_3_) | copy-start | bytes 1179652
  30.2 19.7 %copy-start.2 = (f32[2,3,128,128]{3,2,1,0:T(8,128)S(1)}, f32[2,3,128,128]{3,2,1,0:T(8,128)}, u32[]{:S(2)}) copy-start(f32[2,3,128,128]{3,2,1,0:T(8,128)} %get-tuple-element.72.refs_2_.refs_4_) | copy-start | bytes 1179652
  30.2 1.8 %collective-permute-start.6 = (f32[768,128]{1,0:T(8,128)S(1)}, f32[768,128]{1,0:T(8,128)S(1)}, u32[]{:S(2)}, u32[]{:S(2)}) collective-permute-start(f32[768,128]{1,0:T(8,128)S(1)} %get-tuple-element.67), channel_id=1, source_target_pairs={{0,16},{16,0},{1,17},{17,1},{2,18},{18,2},{3,19},{19,3},{4,20},{20... | collective-permute-start | bytes 1179656 | tf_op jit(solution)/shard_map/ppermute | solution.py:592
  32.8 28.2 %all-to-all-start = ((f32[32,24,128]{2,1,0:T(8,128)}), f32[32,24,128]{2,1,0:T(8,128)S(1)}, u32[]{:S(2)}, u32[]{:S(2)}) async-start(f32[32,24,128]{2,1,0:T(8,128)} %bitcast.9), calls=%async_computation | async-start | bytes 786432 | tf_op jit(solution)/shard_map/all_to_all | solution.py:670
  49.1 9.1 %collective-permute-start.7 = (f32[2,3,128,128]{3,2,1,0:T(8,128)S(1)}, f32[2,3,128,128]{3,2,1,0:T(8,128)S(1)}, u32[]{:S(2)}, u32[]{:S(2)}) collective-permute-start(f32[2,3,128,128]{3,2,1,0:T(8,128)S(1)} %copy-done.1), channel_id=1, source_target_pairs={{0,16},{16,0},{32,48},{48,32},{64,80},{80,64},{96,112},{112,96},{1... | collective-permute-start | bytes 1179656 | tf_op jit(solution)/shard_map/ppermute | solution.py:587
  49.8 17.1 %collective-permute-start.11 = (f32[2,3,128,128]{3,2,1,0:T(8,128)S(1)}, f32[2,3,128,128]{3,2,1,0:T(8,128)S(1)}, u32[]{:S(2)}, u32[]{:S(2)}) collective-permute-start(f32[2,3,128,128]{3,2,1,0:T(8,128)S(1)} %copy-done.2), channel_id=1, source_target_pairs={{16,32},{48,64},{80,96},{112,128},{144,160},{176,192},{208,224},{3... | collective-permute-start | bytes 1179656 | tf_op jit(solution)/shard_map/ppermute | solution.py:587
  58.1 17.4 %copy-start.3 = (f32[2,3,128,128]{3,2,1,0:T(8,128)}, f32[2,3,128,128]{3,2,1,0:T(8,128)S(1)}, u32[]{:S(2)}) copy-start(f32[2,3,128,128]{3,2,1,0:T(8,128)S(1)} %collective-permute-done.7.refs_4_.refs_6_) | copy-start | bytes 1179652
  61.1 3.8 %collective-permute-start.10 = (f32[24,128]{1,0:T(8,128)S(1)}, f32[24,128]{1,0:T(8,128)S(1)}, u32[]{:S(2)}, u32[]{:S(2)}) collective-permute-start(f32[24,128]{1,0:T(8,128)S(1)} %share.2), channel_id=1, source_target_pairs={{0,40},{8,32},{32,8},{40,0},{1,41},{9,33},{33,9},{41,1},{2,42},{10... | collective-permute-start | bytes 36872 | tf_op jit(solution)/shard_map/ppermute | solution.py:592
  62.8 4.0 %collective-permute-start.9 = (f32[24,128]{1,0:T(8,128)S(1)}, f32[24,128]{1,0:T(8,128)S(1)}, u32[]{:S(2)}, u32[]{:S(2)}) collective-permute-start(f32[24,128]{1,0:T(8,128)S(1)} %share.2), channel_id=1, source_target_pairs={{0,32},{32,0},{1,33},{33,1},{2,34},{34,2},{3,35},{35,3},{4,36},{36... | collective-permute-start | bytes 36872 | tf_op jit(solution)/shard_map/ppermute | solution.py:592
  64.2 2.7 %collective-permute-start.8 = (f32[24,128]{1,0:T(8,128)S(1)}, f32[24,128]{1,0:T(8,128)S(1)}, u32[]{:S(2)}, u32[]{:S(2)}) collective-permute-start(f32[24,128]{1,0:T(8,128)S(1)} %share.2), channel_id=1, source_target_pairs={{0,8},{8,0},{1,9},{9,1},{2,10},{10,2},{3,11},{11,3},{4,12},{12,4},... | collective-permute-start | bytes 36872 | tf_op jit(solution)/shard_map/ppermute | solution.py:592
  67.0 8.6 %copy-start.4 = (f32[2,3,128,128]{3,2,1,0:T(8,128)}, f32[2,3,128,128]{3,2,1,0:T(8,128)S(1)}, u32[]{:S(2)}) copy-start(f32[2,3,128,128]{3,2,1,0:T(8,128)S(1)} %collective-permute-done.11.refs_5_.refs_7_) | copy-start | bytes 1179652
  67.8 25.3 %all-to-all-start.1 = ((f32[32,24,128]{2,1,0:T(8,128)}), f32[32,24,128]{2,1,0:T(8,128)S(1)}, u32[]{:S(2)}, u32[]{:S(2)}) async-start(f32[32,24,128]{2,1,0:T(8,128)} %bitcast.12), calls=%async_computation.1 | async-start | bytes 786432 | tf_op jit(solution)/shard_map/all_to_all | solution.py:681
  78.6 14.4 %collective-permute-start.12 = (f32[2,384,128]{2,1,0:T(8,128)}, f32[2,384,128]{2,1,0:T(8,128)S(1)}, u32[]{:S(2)}, u32[]{:S(2)}) collective-permute-start(f32[2,384,128]{2,1,0:T(8,128)} %get-tuple-element.84), channel_id=1, source_target_pairs={{0,1},{1,0},{2,3},{3,2},{4,5},{5,4},{6,7},{7,6},{8,9},{9,8},{10,11... | collective-permute-start | bytes 1179656 | tf_op jit(solution)/shard_map/ppermute | solution.py:587
  79.9 13.1 %collective-permute-start.13 = (f32[2,384,128]{2,1,0:T(8,128)}, f32[2,384,128]{2,1,0:T(8,128)S(1)}, u32[]{:S(2)}, u32[]{:S(2)}) collective-permute-start(f32[2,384,128]{2,1,0:T(8,128)} %get-tuple-element.85), channel_id=1, source_target_pairs={{1,2},{3,4},{5,6},{7,8},{9,10},{11,12},{13,14},{2,1},{4,3},{6,5},{... | collective-permute-start | bytes 1179656 | tf_op jit(solution)/shard_map/ppermute | solution.py:587
  93.1 3.7 %copy-start.5 = (f32[2,384,128]{2,1,0:T(8,128)}, f32[2,384,128]{2,1,0:T(8,128)S(1)}, u32[]{:S(2)}) copy-start(f32[2,384,128]{2,1,0:T(8,128)S(1)} %collective-permute-done.12.refs_8_) | copy-start | bytes 1179652
  93.1 3.7 %copy-start.6 = (f32[2,384,128]{2,1,0:T(8,128)}, f32[2,384,128]{2,1,0:T(8,128)S(1)}, u32[]{:S(2)}) copy-start(f32[2,384,128]{2,1,0:T(8,128)S(1)} %collective-permute-done.13.refs_9_) | copy-start | bytes 1179652
  93.1 3.7 %collective-permute-start.14 = (f32[768,128]{1,0:T(8,128)S(1)}, f32[768,128]{1,0:T(8,128)S(1)}, u32[]{:S(2)}, u32[]{:S(2)}) collective-permute-start(f32[768,128]{1,0:T(8,128)S(1)} %bitcast.21), channel_id=1, source_target_pairs={{0,16},{16,0},{1,17},{17,1},{2,18},{18,2},{3,19},{19,3},{4,20},{20... | collective-permute-start | bytes 1179656 | tf_op jit(solution)/shard_map/ppermute | solution.py:592
  109.8 11.2 %copy-start.12 = (f32[2,3,64,128]{3,2,1,0:T(8,128)S(1)}, f32[2,3,64,128]{3,2,1,0:T(8,128)}, u32[]{:S(2)}) copy-start(f32[2,3,64,128]{3,2,1,0:T(8,128)} %get-tuple-element.99) | copy-start | bytes 589828
  109.8 12.0 %copy-start.11 = (f32[2,3,64,128]{3,2,1,0:T(8,128)S(1)}, f32[2,3,64,128]{3,2,1,0:T(8,128)}, u32[]{:S(2)}) copy-start(f32[2,3,64,128]{3,2,1,0:T(8,128)} %get-tuple-element.100) | copy-start | bytes 589828
  109.8 1.8 %collective-permute-start.15 = (f32[768,128]{1,0:T(8,128)S(1)}, f32[768,128]{1,0:T(8,128)S(1)}, u32[]{:S(2)}, u32[]{:S(2)}) collective-permute-start(f32[768,128]{1,0:T(8,128)S(1)} %get-tuple-element.94), channel_id=1, source_target_pairs={{0,16},{16,0},{1,17},{17,1},{2,18},{18,2},{3,19},{19,3},{4,20},{20... | collective-permute-start | bytes 1179656 | tf_op jit(solution)/shard_map/ppermute | solution.py:592
  112.4 20.6 %all-to-all-start.2 = ((f32[32,24,128]{2,1,0:T(8,128)}), f32[32,24,128]{2,1,0:T(8,128)S(1)}, u32[]{:S(2)}, u32[]{:S(2)}) async-start(f32[32,24,128]{2,1,0:T(8,128)} %bitcast.14), calls=%async_computation.2 | async-start | bytes 786432 | tf_op jit(solution)/shard_map/all_to_all | solution.py:670
  121.1 8.8 %collective-permute-start.16 = (f32[2,3,64,128]{3,2,1,0:T(8,128)S(1)}, f32[2,3,64,128]{3,2,1,0:T(8,128)S(1)}, u32[]{:S(2)}, u32[]{:S(2)}) collective-permute-start(f32[2,3,64,128]{3,2,1,0:T(8,128)S(1)} %copy-done.12), channel_id=1, source_target_pairs={{0,16},{16,0},{32,48},{48,32},{64,80},{80,64},{96,112},{112,96},{1... | collective-permute-start | bytes 589832 | tf_op jit(solution)/shard_map/ppermute | solution.py:587
  121.8 10.4 %collective-permute-start.17 = (f32[2,3,64,128]{3,2,1,0:T(8,128)S(1)}, f32[2,3,64,128]{3,2,1,0:T(8,128)S(1)}, u32[]{:S(2)}, u32[]{:S(2)}) collective-permute-start(f32[2,3,64,128]{3,2,1,0:T(8,128)S(1)} %copy-done.11), channel_id=1, source_target_pairs={{16,32},{48,64},{80,96},{112,128},{144,160},{176,192},{208,224},{3... | collective-permute-start | bytes 589832 | tf_op jit(solution)/shard_map/ppermute | solution.py:587
  129.8 18.9 %copy-start.7 = (f32[2,3,64,128]{3,2,1,0:T(8,128)}, f32[2,3,64,128]{3,2,1,0:T(8,128)S(1)}, u32[]{:S(2)}) copy-start(f32[2,3,64,128]{3,2,1,0:T(8,128)S(1)} %collective-permute-done.16.refs_2_) | copy-start | bytes 589828
  132.2 16.6 %copy-start.8 = (f32[2,3,64,128]{3,2,1,0:T(8,128)}, f32[2,3,64,128]{3,2,1,0:T(8,128)S(1)}, u32[]{:S(2)}) copy-start(f32[2,3,64,128]{3,2,1,0:T(8,128)S(1)} %collective-permute-done.17.refs_3_) | copy-start | bytes 589828
  133.1 3.8 %collective-permute-start.20 = (f32[24,128]{1,0:T(8,128)S(1)}, f32[24,128]{1,0:T(8,128)S(1)}, u32[]{:S(2)}, u32[]{:S(2)}) collective-permute-start(f32[24,128]{1,0:T(8,128)S(1)} %share.3), channel_id=1, source_target_pairs={{0,40},{8,32},{32,8},{40,0},{1,41},{9,33},{33,9},{41,1},{2,42},{10... | collective-permute-start | bytes 36872 | tf_op jit(solution)/shard_map/ppermute | solution.py:592
  134.8 4.0 %collective-permute-start.19 = (f32[24,128]{1,0:T(8,128)S(1)}, f32[24,128]{1,0:T(8,128)S(1)}, u32[]{:S(2)}, u32[]{:S(2)}) collective-permute-start(f32[24,128]{1,0:T(8,128)S(1)} %share.3), channel_id=1, source_target_pairs={{0,32},{32,0},{1,33},{33,1},{2,34},{34,2},{3,35},{35,3},{4,36},{36... | collective-permute-start | bytes 36872 | tf_op jit(solution)/shard_map/ppermute | solution.py:592
  135.9 2.9 %collective-permute-start.18 = (f32[24,128]{1,0:T(8,128)S(1)}, f32[24,128]{1,0:T(8,128)S(1)}, u32[]{:S(2)}, u32[]{:S(2)}) collective-permute-start(f32[24,128]{1,0:T(8,128)S(1)} %share.3), channel_id=1, source_target_pairs={{0,8},{8,0},{1,9},{9,1},{2,10},{10,2},{3,11},{11,3},{4,12},{12,4},... | collective-permute-start | bytes 36872 | tf_op jit(solution)/shard_map/ppermute | solution.py:592
  139.7 20.8 %all-to-all-start.3 = ((f32[32,24,128]{2,1,0:T(8,128)}), f32[32,24,128]{2,1,0:T(8,128)S(1)}, u32[]{:S(2)}, u32[]{:S(2)}) async-start(f32[32,24,128]{2,1,0:T(8,128)} %bitcast.17), calls=%async_computation.3 | async-start | bytes 786432 | tf_op jit(solution)/shard_map/all_to_all | solution.py:681
  151.7 8.7 %collective-permute-start.21 = (f32[256,128]{1,0:T(8,128)}, f32[256,128]{1,0:T(8,128)S(1)}, u32[]{:S(2)}, u32[]{:S(2)}) collective-permute-start(f32[256,128]{1,0:T(8,128)} %get-tuple-element.110), channel_id=1, source_target_pairs={{0,1},{1,0},{2,3},{3,2},{4,5},{5,4},{6,7},{7,6},{8,9},{9,8},{10,11... | collective-permute-start | bytes 393224 | tf_op jit(solution)/shard_map/ppermute | solution.py:587
  153.0 7.4 %collective-permute-start.22 = (f32[256,128]{1,0:T(8,128)}, f32[256,128]{1,0:T(8,128)S(1)}, u32[]{:S(2)}, u32[]{:S(2)}) collective-permute-start(f32[256,128]{1,0:T(8,128)} %get-tuple-element.111), channel_id=1, source_target_pairs={{1,2},{3,4},{5,6},{7,8},{9,10},{11,12},{13,14},{2,1},{4,3},{6,5},{... | collective-permute-start | bytes 393224 | tf_op jit(solution)/shard_map/ppermute | solution.py:587
  160.5 6.1 %copy-start.9 = (f32[256,128]{1,0:T(8,128)}, f32[256,128]{1,0:T(8,128)S(1)}, u32[]{:S(2)}) copy-start(f32[256,128]{1,0:T(8,128)S(1)} %collective-permute-done.21.refs_3_) | copy-start | bytes 393220
  160.5 6.1 %copy-start.10 = (f32[256,128]{1,0:T(8,128)}, f32[256,128]{1,0:T(8,128)S(1)}, u32[]{:S(2)}) copy-start(f32[256,128]{1,0:T(8,128)S(1)} %collective-permute-done.22.refs_4_) | copy-start | bytes 393220
  160.5 6.1 %collective-permute-start.23 = (f32[768,128]{1,0:T(8,128)S(1)}, f32[768,128]{1,0:T(8,128)S(1)}, u32[]{:S(2)}, u32[]{:S(2)}) collective-permute-start(f32[768,128]{1,0:T(8,128)S(1)} %bitcast.23), channel_id=1, source_target_pairs={{0,16},{16,0},{1,17},{17,1},{2,18},{18,2},{3,19},{19,3},{4,20},{20... | collective-permute-start | bytes 1179656 | tf_op jit(solution)/shard_map/ppermute | solution.py:592

commit v6 on v5

--- a/solution.py
+++ b/solution.py
@@ -9,7 +9,7 @@
 from jax.sharding import Mesh, PartitionSpec as P
 
 ITERS = 2
-BATCH = 4
+BATCH = 8
 SPLIT = (("y", 4), ("xh", 2), ("core", 2), ("xl", 2), ("z", 8))
 ROW = ("y", "xh", "core")
 COL = ("xl", "z")
@@ -690,10 +690,14 @@
             args = [info] + [Far(x) for x in (first, second, mid, row_a, row_b)]
             col_a, col_b = call(fold_kernel, outs, [], args, 1, "fold_rows")
             sums = [first, second, mid, row_a, row_b]
+            light, col_a, col_b = lax.optimization_barrier((light, col_a, col_b))
             args = [tags, Far(bright), Far(light)]
             light = call(more_light_kernel, [Far(lights)], [canvas, SPOTS], args, 1, "more_light")[0]
         col_a, col_b = exchange(col_a, col_b, COL)
-        mine, col_a, col_b, light = lax.optimization_barrier((mine, col_a, col_b, light))
+        if last:
+            mine, col_a, col_b, light = lax.optimization_barrier((mine, col_a, col_b, light))
+        else:
+            mine, light = lax.optimization_barrier((mine, light))
         sums += [col_a, col_b]
         other = swap(mine, ("core",))
     held = [Far(x) for x in (cells_now, *sums, light)]

time: 172 us -> 170 us (0.988)
  waiting for transfers between devices: 34.7 us -> 27.2 us
  starting transfers between devices: 80.2 us -> 86.2 us
    ppermute x7, waiting for transfers between devices: 15 us -> 7.76 us  [exchange(): lax.ppermute(first, axes, pairs_first(count))]
    ppermute x10, starting transfers between devices: 14.3 us -> 20.5 us  [swap(): return lax.ppermute(value, axes, [(i, count - 1 - i) for i in range(count)])]
  transfers between devices with their start and end apart: 28 -> 28, of which waited for: 15 -> 16; matrix products, arithmetic and copies ran while one was open for 0% -> 0% of each run, Pallas kernels for 12% -> 12%
where the time goes in v6:
time: 170 us; the launch traced here: 169 us
  starting transfers between devices  86.2 us (51%)
  Pallas kernels  49.2 us (29%)
  waiting for transfers between devices  27.2 us (16%)
  local copies, waits for them, and re-layouts  2.96 us (2%)
  other arithmetic  2.49 us (1%)
    pallas_call x12, Pallas kernels, call(): pl.pallas_call(whole, out_shape=tuple((pltpu.HBM(x, F32) if is_far else j...  49.2 us
    all_to_all x2, starting transfers between devices, body(): parts = lax.all_to_all(keep + received, RING, 0, 0, tiled=True)  24.9 us
    ppermute x10, starting transfers between devices, swap(): return lax.ppermute(value, axes, [(i, count - 1 - i) for i in range(count)])  20.5 us
    all_to_all x2, starting transfers between devices, body(): mine = lax.all_to_all(copies, RING, 0, 0, tiled=True)  16.8 us
    ppermute x7, starting transfers between devices, exchange(): lax.ppermute(second, axes, pairs_second(count))  13.1 us
    ppermute x7, starting transfers between devices, exchange(): lax.ppermute(first, axes, pairs_first(count))  10.9 us
    ppermute x10, waiting for transfers between devices, swap(): return lax.ppermute(value, axes, [(i, count - 1 - i) for i in range(count)])  9.97 us
    ppermute x7, waiting for transfers between devices, exchange(): lax.ppermute(first, axes, pairs_first(count))  7.76 us
  transfers between devices with their start and end apart: 28, of which 16 were waited for; matrix products, arithmetic and copies ran while one was open for 0% of the time, Pallas kernels for 12%

profile of v6, /device:TPU:1, one launch (start us, length us, event | category | flops | bytes accessed | tf_op | source)
XLA Modules:
  0.0 169.3 jit_solution(7940169654677663136)
XLA Ops:
  0.7 0.7 add_convert_fusion
  1.5 0.1 convert_element_type.19
  1.6 0.1 stack.31.refs_0_.refs_1_
  1.7 1.7 %pack_edges.1 = (f32[2,72,256]{2,1,0:T(8,128)S(1)}, f32[2,72,256]{2,1,0:T(8,128)S(1)}, f32[264,128]{1,0:T(8,128)S(1)}, f32[264,128]{1,0:T(8,128)S(1)}) custom-call(s32[7]{0:T(128)S(1)} %stack.31.refs_0_.refs_1_, f32[2,256,256]{2,1,0:T(8,128)} %refs_2_.1, f32[8,128]{1,0:T(8,128)S(1)} %pad.4.refs_2_.refs_3_), custom_call_target="tpu_custom_call" | custom-call | tf_op jit(solution)/shard_map/pack_edges/pallas_call | solution.py:557
  3.5 3.3 %collective-permute-start = (f32[2,72,256]{2,1,0:T(8,128)S(1)}, f32[2,72,256]{2,1,0:T(8,128)S(1)}, u32[]{:S(2)}, u32[]{:S(2)}) collective-permute-start(f32[2,72,256]{2,1,0:T(8,128)S(1)} %get-tuple-element.61), channel_id=1, source_target_pairs={{0,16},{16,0},{32,48},{48,32},{64,80},{80,64},{96,112},{112,96},{1... | collective-permute-start | bytes 442376 | tf_op jit(solution)/shard_map/ppermute | solution.py:587
  6.8 2.8 %collective-permute-start.1 = (f32[2,72,256]{2,1,0:T(8,128)S(1)}, f32[2,72,256]{2,1,0:T(8,128)S(1)}, u32[]{:S(2)}, u32[]{:S(2)}) collective-permute-start(f32[2,72,256]{2,1,0:T(8,128)S(1)} %get-tuple-element.62), channel_id=1, source_target_pairs={{16,32},{48,64},{80,96},{112,128},{144,160},{176,192},{208,224},{3... | collective-permute-start | bytes 442376 | tf_op jit(solution)/shard_map/ppermute | solution.py:587
  9.6 1.7 %collective-permute-start.2 = (f32[264,128]{1,0:T(8,128)S(1)}, f32[264,128]{1,0:T(8,128)S(1)}, u32[]{:S(2)}, u32[]{:S(2)}) collective-permute-start(f32[264,128]{1,0:T(8,128)S(1)} %get-tuple-element.63), channel_id=1, source_target_pairs={{0,1},{1,0},{2,3},{3,2},{4,5},{5,4},{6,7},{7,6},{8,9},{9,8},{10,11... | collective-permute-start | bytes 405512 | tf_op jit(solution)/shard_map/ppermute | solution.py:587
  11.3 0.7 collective-permute-start.3
  12.0 2.9 %collective-permute-done.1.refs_2_.refs_5_ = f32[2,72,256]{2,1,0:T(8,128)S(1)} collective-permute-done((f32[2,72,256]{2,1,0:T(8,128)S(1)}, f32[2,72,256]{2,1,0:T(8,128)S(1)}, u32[]{:S(2)}, u32[]{:S(2)}) %collective-permute-start.1) | collective-permute-done | bytes 147488 | tf_op jit(solution)/shard_map/ppermute | solution.py:587
  14.9 0.7 pack_ends.1
  15.6 1.7 collective-permute-start.4
  17.3 0.7 collective-permute-start.5
  17.9 0.8 copy.13.refs_0_
  18.7 0.3 collective-permute-done.4.refs_8_
  19.0 10.8 %first_sweep.1 = (f32[2,3,128,128]{3,2,1,0:T(8,128)}, f32[2,3,128,128]{3,2,1,0:T(8,128)}, f32[2,3,128,128]{3,2,1,0:T(8,128)}, f32[768,128]{1,0:T(8,128)S(1)}, f3...) custom-call(s32[16,2]{1,0:T(8,128)S(1)} %copy.13.refs_0_, ...), custom_call_target="tpu_custom_call" | custom-call | tf_op jit(solution)/shard_map/first_sweep/pallas_call | solution.py:557
  29.9 0.1 collective-permute-start.6
  30.0 1.7 %collective-permute-done.6 = f32[768,128]{1,0:T(8,128)S(1)} collective-permute-done((f32[768,128]{1,0:T(8,128)S(1)}, f32[768,128]{1,0:T(8,128)S(1)}, u32[]{:S(2)}, u32[]{:S(2)}) %collective-permute-start.6) | collective-permute-done | bytes 393248 | tf_op jit(solution)/shard_map/ppermute | solution.py:592
  31.7 0.8 add.63
  32.5 16.3 %all-to-all-start = ((f32[32,24,128]{2,1,0:T(8,128)}), f32[32,24,128]{2,1,0:T(8,128)S(1)}, u32[]{:S(2)}, u32[]{:S(2)}) async-start(f32[32,24,128]{2,1,0:T(8,128)} %bitcast.9), calls=%async_computation | async-start | bytes 786432 | tf_op jit(solution)/shard_map/all_to_all | solution.py:670
  48.8 0.7 collective-permute-start.7
  49.5 4.0 %collective-permute-start.11 = (f32[2,3,128,128]{3,2,1,0:T(8,128)S(1)}, f32[2,3,128,128]{3,2,1,0:T(8,128)S(1)}, u32[]{:S(2)}, u32[]{:S(2)}) collective-permute-start(f32[2,3,128,128]{3,2,1,0:T(8,128)S(1)} %copy-done.2), channel_id=1, source_target_pairs={{16,32},{48,64},{80,96},{112,128},{144,160},{176,192},{208,224},{3... | collective-permute-start | bytes 1179656 | tf_op jit(solution)/shard_map/ppermute | solution.py:587
  53.5 4.5 %light.2 = (f32[3,384,128]{2,1,0:T(8,128)}, f32[8,128]{1,0:T(8,128)S(1)}) custom-call(s32[9,32]{1,0:T(8,128)S(1)} %slice_convert_fusion.refs_0_, f32[128,128]{1,0:T(8,128)} %get-tuple-element.79.refs_1_), custom_call_target="tpu_custom_call" | custom-call | tf_op jit(solution)/shard_map/light/pallas_call | solution.py:557
  58.0 2.7 %all-to-all-done = f32[32,24,128]{2,1,0:T(8,128)S(1)} async-done(((f32[32,24,128]{2,1,0:T(8,128)}), f32[32,24,128]{2,1,0:T(8,128)S(1)}, u32[]{:S(2)}, u32[]{:S(2)}) %all-to-all-start) | async-done | bytes 393248 | tf_op jit(solution)/shard_map/all_to_all | solution.py:670
  60.8 1.8 %collective-permute-start.10 = (f32[24,128]{1,0:T(8,128)S(1)}, f32[24,128]{1,0:T(8,128)S(1)}, u32[]{:S(2)}, u32[]{:S(2)}) collective-permute-start(f32[24,128]{1,0:T(8,128)S(1)} %share.2), channel_id=1, source_target_pairs={{0,40},{8,32},{32,8},{40,0},{1,41},{9,33},{33,9},{41,1},{2,42},{10... | collective-permute-start | bytes 36872 | tf_op jit(solution)/shard_map/ppermute | solution.py:592
  62.6 1.3 collective-permute-start.9
  63.9 0.2 collective-permute-start.8
  64.1 0.5 collective-permute-done.10
  64.6 2.0 %collective-permute-done.9 = f32[24,128]{1,0:T(8,128)S(1)} collective-permute-done((f32[24,128]{1,0:T(8,128)S(1)}, f32[24,128]{1,0:T(8,128)S(1)}, u32[]{:S(2)}, u32[]{:S(2)}) %collective-permute-start.9) | collective-permute-done | bytes 12320 | tf_op jit(solution)/shard_map/ppermute | solution.py:592
  66.7 0.9 broadcast_in_dim.4
  67.6 7.7 %all-to-all-start.1 = ((f32[32,24,128]{2,1,0:T(8,128)}), f32[32,24,128]{2,1,0:T(8,128)S(1)}, u32[]{:S(2)}, u32[]{:S(2)}) async-start(f32[32,24,128]{2,1,0:T(8,128)} %bitcast.12), calls=%async_computation.1 | async-start | bytes 786432 | tf_op jit(solution)/shard_map/all_to_all | solution.py:681
  75.3 3.0 %fold_rows.1 = (f32[2,384,128]{2,1,0:T(8,128)}, f32[2,384,128]{2,1,0:T(8,128)}) custom-call(s32[7]{0:T(128)S(1)} %stack.31.refs_0_.refs_1_, f32[2,3,128,128]{3,2,1,0:T(8,128)} %get-tuple-element.72.refs_1_.refs_3_, f32[2,3,128,128]{3,2,1,0:T(8,128)} %get-tuple-element.73.refs_2_.refs_4_, f32[2,3,128,128]{3,2,1,0:T(8,128)} %get-tuple-element.74.refs_3_.refs_5_, ...), custom_call_target="tpu_custom_call" | custom-call | tf_op jit(solution)/shard_map/fold_rows/pallas_call | solution.py:557
  78.4 1.3 collective-permute-start.12
  79.7 0.7 collective-permute-start.13
  80.4 4.3 %more_light.1.refs_10_ = f32[3,384,128]{2,1,0:T(8,128)} custom-call(s32[9,32]{1,0:T(8,128)S(1)} %slice_convert_fusion.refs_0_, f32[128,128]{1,0:T(8,128)} %get-tuple-element.79.refs_1_, f32[3,384,128]{2,1,0:T(8,128)} %get-tuple-element.90.refs_2_), custom_call_target="tpu_custom_call" | custom-call | tf_op jit(solution)/shard_map/more_light/pallas_call | solution.py:557
  84.7 0.9 all-to-all-done.1
  85.6 6.6 %collective-permute-start.14 = (f32[768,128]{1,0:T(8,128)S(1)}, f32[768,128]{1,0:T(8,128)S(1)}, u32[]{:S(2)}, u32[]{:S(2)}) collective-permute-start(f32[768,128]{1,0:T(8,128)S(1)} %bitcast.21), channel_id=1, source_target_pairs={{0,16},{16,0},{1,17},{17,1},{2,18},{18,2},{3,19},{19,3},{4,20},{20... | collective-permute-start | bytes 1179656 | tf_op jit(solution)/shard_map/ppermute | solution.py:592
  92.1 0.7 collective-permute-done.12.refs_8_
  92.9 0.6 collective-permute-done.14.refs_12_
  93.5 0.1 copy-done.5
  93.6 0.1 copy-done.6
  93.7 12.6 %next_sweep.1 = (f32[2,3,64,128]{3,2,1,0:T(8,128)}, f32[2,3,64,128]{3,2,1,0:T(8,128)}, f32[2,3,256,128]{3,2,1,0:T(8,128)}, f32[768,128]{1,0:T(8,128)S(1)}, f32[7...) custom-call(s32[16,2]{1,0:T(8,128)S(1)} %copy.13.refs_0_, ...), custom_call_target="tpu_custom_call" | custom-call | tf_op jit(solution)/shard_map/next_sweep/pallas_call | solution.py:557
  106.3 2.4 %collective-permute-start.15 = (f32[768,128]{1,0:T(8,128)S(1)}, f32[768,128]{1,0:T(8,128)S(1)}, u32[]{:S(2)}, u32[]{:S(2)}) collective-permute-start(f32[768,128]{1,0:T(8,128)S(1)} %get-tuple-element.96), channel_id=1, source_target_pairs={{0,16},{16,0},{1,17},{17,1},{2,18},{18,2},{3,19},{19,3},{4,20},{20... | collective-permute-start | bytes 1179656 | tf_op jit(solution)/shard_map/ppermute | solution.py:592
  108.7 1.3 collective-permute-done.15
  110.1 0.8 add.67
  110.9 8.6 %all-to-all-start.2 = ((f32[32,24,128]{2,1,0:T(8,128)}), f32[32,24,128]{2,1,0:T(8,128)S(1)}, u32[]{:S(2)}, u32[]{:S(2)}) async-start(f32[32,24,128]{2,1,0:T(8,128)} %bitcast.14), calls=%async_computation.2 | async-start | bytes 786432 | tf_op jit(solution)/shard_map/all_to_all | solution.py:670
  119.5 0.7 collective-permute-start.16
  120.2 3.7 %collective-permute-start.17 = (f32[2,3,64,128]{3,2,1,0:T(8,128)S(1)}, f32[2,3,64,128]{3,2,1,0:T(8,128)S(1)}, u32[]{:S(2)}, u32[]{:S(2)}) collective-permute-start(f32[2,3,64,128]{3,2,1,0:T(8,128)S(1)} %copy-done.11), channel_id=1, source_target_pairs={{16,32},{48,64},{80,96},{112,128},{144,160},{176,192},{208,224},{3... | collective-permute-start | bytes 589832 | tf_op jit(solution)/shard_map/ppermute | solution.py:587
  123.9 4.5 %light.3 = (f32[3,384,128]{2,1,0:T(8,128)}, f32[8,128]{1,0:T(8,128)S(1)}) custom-call(s32[9,32]{1,0:T(8,128)S(1)} %slice_convert_fusion.refs_0_, f32[128,128]{1,0:T(8,128)} %get-tuple-element.104.refs_1_), custom_call_target="tpu_custom_call" | custom-call | tf_op jit(solution)/shard_map/light/pallas_call | solution.py:557
  128.4 2.1 %collective-permute-done.17.refs_3_ = f32[2,3,64,128]{3,2,1,0:T(8,128)S(1)} collective-permute-done((f32[2,3,64,128]{3,2,1,0:T(8,128)S(1)}, f32[2,3,64,128]{3,2,1,0:T(8,128)S(1)}, u32[]{:S(2)}, u32[]{:S(2)}) %collective-permute-start.17) | collective-permute-done | bytes 196640 | tf_op jit(solution)/shard_map/ppermute | solution.py:587
  130.6 0.8 all-to-all-done.2
  131.5 1.7 %collective-permute-start.20 = (f32[24,128]{1,0:T(8,128)S(1)}, f32[24,128]{1,0:T(8,128)S(1)}, u32[]{:S(2)}, u32[]{:S(2)}) collective-permute-start(f32[24,128]{1,0:T(8,128)S(1)} %share.3), channel_id=1, source_target_pairs={{0,40},{8,32},{32,8},{40,0},{1,41},{9,33},{33,9},{41,1},{2,42},{10... | collective-permute-start | bytes 36872 | tf_op jit(solution)/shard_map/ppermute | solution.py:592
  133.2 1.1 collective-permute-start.19
  134.3 0.5 collective-permute-start.18
  134.8 0.5 collective-permute-done.20
  135.3 1.9 %collective-permute-done.19 = f32[24,128]{1,0:T(8,128)S(1)} collective-permute-done((f32[24,128]{1,0:T(8,128)S(1)}, f32[24,128]{1,0:T(8,128)S(1)}, u32[]{:S(2)}, u32[]{:S(2)}) %collective-permute-start.19) | collective-permute-done | bytes 12320 | tf_op jit(solution)/shard_map/ppermute | solution.py:592
  137.3 0.8 broadcast_in_dim.5
  138.1 9.1 %all-to-all-start.3 = ((f32[32,24,128]{2,1,0:T(8,128)}), f32[32,24,128]{2,1,0:T(8,128)S(1)}, u32[]{:S(2)}, u32[]{:S(2)}) async-start(f32[32,24,128]{2,1,0:T(8,128)} %bitcast.17), calls=%async_computation.3 | async-start | bytes 786432 | tf_op jit(solution)/shard_map/all_to_all | solution.py:681
  147.2 2.9 %fold_inner.1 = (f32[2,3,256,128]{3,2,1,0:T(8,128)}, f32[256,128]{1,0:T(8,128)}, f32[256,128]{1,0:T(8,128)}) custom-call(s32[7]{0:T(128)S(1)} %stack.31.refs_0_.refs_1_, f32[2,3,256,128]{3,2,1,0:T(8,128)} %get-tuple-element.94.refs_1_, f32[2,3,64,128]{3,2,1,0:T(8,128)} %copy-done.7, f32[2,3,64,128]{3,2,1,0:T(8,128)} %copy-done.8), custom_call_target="tpu_custom_call" | custom-call | tf_op jit(solution)/shard_map/fold_inner/pallas_call | solution.py:557
  150.1 1.3 collective-permute-start.21
  151.5 0.7 collective-permute-start.22
  152.1 6.8 %collective-permute-done.21.refs_3_ = f32[256,128]{1,0:T(8,128)S(1)} collective-permute-done((f32[256,128]{1,0:T(8,128)}, f32[256,128]{1,0:T(8,128)S(1)}, u32[]{:S(2)}, u32[]{:S(2)}) %collective-permute-start.21) | collective-permute-done | bytes 131104 | tf_op jit(solution)/shard_map/ppermute | solution.py:587
  158.9 4.8 %collective-permute-start.23 = (f32[768,128]{1,0:T(8,128)S(1)}, f32[768,128]{1,0:T(8,128)S(1)}, u32[]{:S(2)}, u32[]{:S(2)}) collective-permute-start(f32[768,128]{1,0:T(8,128)S(1)} %bitcast.23), channel_id=1, source_target_pairs={{0,16},{16,0},{1,17},{17,1},{2,18},{18,2},{3,19},{19,3},{4,20},{20... | collective-permute-start | bytes 1179656 | tf_op jit(solution)/shard_map/ppermute | solution.py:592
  163.7 1.3 collective-permute-done.23.refs_7_
  165.0 4.1 %last_update.1 = (f32[2,256,256]{2,1,0:T(8,128)}, f32[2,4,128,128]{3,2,1,0:T(8,128)}) custom-call(s32[7]{0:T(128)S(1)} %stack.31.refs_0_.refs_1_, f32[2,3,384,128]{3,2,1,0:T(8,128)} %get-tuple-element.93.refs_1_, f32[2,3,256,128]{3,2,1,0:T(8,128)} %get-tuple-element.110.refs_2_, f32[256,128]{1,0:T(8,128)} %copy-done.9, f32[256,128]{1,0:T(8,128)} %copy-done.10, ...), custom_call_target="tpu_custom_call" | custom-call | tf_op jit(solution)/shard_map/last_update/pallas_call | solution.py:557
  (44 shorter events, 0.4 us)
Async XLA Ops:
  0.6 18.4 %copy-start = (f32[2,4,128,128]{3,2,1,0:T(8,128)S(1)}, f32[2,4,128,128]{3,2,1,0:T(8,128)}, u32[]{:S(2)}) copy-start(f32[2,4,128,128]{3,2,1,0:T(8,128)} %refs_13_.2) | copy-start | bytes 1572868
  3.5 8.5 %collective-permute-start = (f32[2,72,256]{2,1,0:T(8,128)S(1)}, f32[2,72,256]{2,1,0:T(8,128)S(1)}, u32[]{:S(2)}, u32[]{:S(2)}) collective-permute-start(f32[2,72,256]{2,1,0:T(8,128)S(1)} %get-tuple-element.61), channel_id=1, source_target_pairs={{0,16},{16,0},{32,48},{48,32},{64,80},{80,64},{96,112},{112,96},{1... | collective-permute-start | bytes 442376 | tf_op jit(solution)/shard_map/ppermute | solution.py:587
  6.8 8.1 %collective-permute-start.1 = (f32[2,72,256]{2,1,0:T(8,128)S(1)}, f32[2,72,256]{2,1,0:T(8,128)S(1)}, u32[]{:S(2)}, u32[]{:S(2)}) collective-permute-start(f32[2,72,256]{2,1,0:T(8,128)S(1)} %get-tuple-element.62), channel_id=1, source_target_pairs={{16,32},{48,64},{80,96},{112,128},{144,160},{176,192},{208,224},{3... | collective-permute-start | bytes 442376 | tf_op jit(solution)/shard_map/ppermute | solution.py:587
  9.6 9.1 %collective-permute-start.2 = (f32[264,128]{1,0:T(8,128)S(1)}, f32[264,128]{1,0:T(8,128)S(1)}, u32[]{:S(2)}, u32[]{:S(2)}) collective-permute-start(f32[264,128]{1,0:T(8,128)S(1)} %get-tuple-element.63), channel_id=1, source_target_pairs={{0,1},{1,0},{2,3},{3,2},{4,5},{5,4},{6,7},{7,6},{8,9},{9,8},{10,11... | collective-permute-start | bytes 405512 | tf_op jit(solution)/shard_map/ppermute | solution.py:587
  11.3 7.4 %collective-permute-start.3 = (f32[264,128]{1,0:T(8,128)S(1)}, f32[264,128]{1,0:T(8,128)S(1)}, u32[]{:S(2)}, u32[]{:S(2)}) collective-permute-start(f32[264,128]{1,0:T(8,128)S(1)} %get-tuple-element.64), channel_id=1, source_target_pairs={{1,2},{3,4},{5,6},{7,8},{9,10},{11,12},{13,14},{2,1},{4,3},{6,5},{... | collective-permute-start | bytes 405512 | tf_op jit(solution)/shard_map/ppermute | solution.py:587
  15.6 3.4 %collective-permute-start.4 = (f32[136,128]{1,0:T(8,128)S(1)}, f32[136,128]{1,0:T(8,128)S(1)}, u32[]{:S(2)}, u32[]{:S(2)}) collective-permute-start(f32[136,128]{1,0:T(8,128)S(1)} %get-tuple-element.65), channel_id=1, source_target_pairs={{0,1},{1,0},{2,3},{3,2},{4,5},{5,4},{6,7},{7,6},{8,9},{9,8},{10,11... | collective-permute-start | bytes 208904 | tf_op jit(solution)/shard_map/ppermute | solution.py:587
  17.3 1.7 %collective-permute-start.5 = (f32[136,128]{1,0:T(8,128)S(1)}, f32[136,128]{1,0:T(8,128)S(1)}, u32[]{:S(2)}, u32[]{:S(2)}) collective-permute-start(f32[136,128]{1,0:T(8,128)S(1)} %get-tuple-element.66), channel_id=1, source_target_pairs={{1,2},{3,4},{5,6},{7,8},{9,10},{11,12},{13,14},{2,1},{4,3},{6,5},{... | collective-permute-start | bytes 208904 | tf_op jit(solution)/shard_map/ppermute | solution.py:587
  29.8 18.9 %copy-start.1 = (f32[2,3,128,128]{3,2,1,0:T(8,128)S(1)}, f32[2,3,128,128]{3,2,1,0:T(8,128)}, u32[]{:S(2)}) copy-start(f32[2,3,128,128]{3,2,1,0:T(8,128)} %get-tuple-element.72.refs_1_.refs_3_) | copy-start | bytes 1179652
  29.8 19.7 %copy-start.2 = (f32[2,3,128,128]{3,2,1,0:T(8,128)S(1)}, f32[2,3,128,128]{3,2,1,0:T(8,128)}, u32[]{:S(2)}) copy-start(f32[2,3,128,128]{3,2,1,0:T(8,128)} %get-tuple-element.73.refs_2_.refs_4_) | copy-start | bytes 1179652
  29.9 1.8 %collective-permute-start.6 = (f32[768,128]{1,0:T(8,128)S(1)}, f32[768,128]{1,0:T(8,128)S(1)}, u32[]{:S(2)}, u32[]{:S(2)}) collective-permute-start(f32[768,128]{1,0:T(8,128)S(1)} %get-tuple-element.68), channel_id=1, source_target_pairs={{0,16},{16,0},{1,17},{17,1},{2,18},{18,2},{3,19},{19,3},{4,20},{20... | collective-permute-start | bytes 1179656 | tf_op jit(solution)/shard_map/ppermute | solution.py:592
  32.5 28.3 %all-to-all-start = ((f32[32,24,128]{2,1,0:T(8,128)}), f32[32,24,128]{2,1,0:T(8,128)S(1)}, u32[]{:S(2)}, u32[]{:S(2)}) async-start(f32[32,24,128]{2,1,0:T(8,128)} %bitcast.9), calls=%async_computation | async-start | bytes 786432 | tf_op jit(solution)/shard_map/all_to_all | solution.py:670
  48.8 9.2 %collective-permute-start.7 = (f32[2,3,128,128]{3,2,1,0:T(8,128)S(1)}, f32[2,3,128,128]{3,2,1,0:T(8,128)S(1)}, u32[]{:S(2)}, u32[]{:S(2)}) collective-permute-start(f32[2,3,128,128]{3,2,1,0:T(8,128)S(1)} %copy-done.1), channel_id=1, source_target_pairs={{0,16},{16,0},{32,48},{48,32},{64,80},{80,64},{96,112},{112,96},{1... | collective-permute-start | bytes 1179656 | tf_op jit(solution)/shard_map/ppermute | solution.py:587
  49.5 17.2 %collective-permute-start.11 = (f32[2,3,128,128]{3,2,1,0:T(8,128)S(1)}, f32[2,3,128,128]{3,2,1,0:T(8,128)S(1)}, u32[]{:S(2)}, u32[]{:S(2)}) collective-permute-start(f32[2,3,128,128]{3,2,1,0:T(8,128)S(1)} %copy-done.2), channel_id=1, source_target_pairs={{16,32},{48,64},{80,96},{112,128},{144,160},{176,192},{208,224},{3... | collective-permute-start | bytes 1179656 | tf_op jit(solution)/shard_map/ppermute | solution.py:587
  58.0 17.3 %copy-start.3 = (f32[2,3,128,128]{3,2,1,0:T(8,128)}, f32[2,3,128,128]{3,2,1,0:T(8,128)S(1)}, u32[]{:S(2)}) copy-start(f32[2,3,128,128]{3,2,1,0:T(8,128)S(1)} %collective-permute-done.7.refs_4_.refs_6_) | copy-start | bytes 1179652
  60.8 3.8 %collective-permute-start.10 = (f32[24,128]{1,0:T(8,128)S(1)}, f32[24,128]{1,0:T(8,128)S(1)}, u32[]{:S(2)}, u32[]{:S(2)}) collective-permute-start(f32[24,128]{1,0:T(8,128)S(1)} %share.2), channel_id=1, source_target_pairs={{0,40},{8,32},{32,8},{40,0},{1,41},{9,33},{33,9},{41,1},{2,42},{10... | collective-permute-start | bytes 36872 | tf_op jit(solution)/shard_map/ppermute | solution.py:592
  62.6 4.0 %collective-permute-start.9 = (f32[24,128]{1,0:T(8,128)S(1)}, f32[24,128]{1,0:T(8,128)S(1)}, u32[]{:S(2)}, u32[]{:S(2)}) collective-permute-start(f32[24,128]{1,0:T(8,128)S(1)} %share.2), channel_id=1, source_target_pairs={{0,32},{32,0},{1,33},{33,1},{2,34},{34,2},{3,35},{35,3},{4,36},{36... | collective-permute-start | bytes 36872 | tf_op jit(solution)/shard_map/ppermute | solution.py:592
  63.9 2.7 %collective-permute-start.8 = (f32[24,128]{1,0:T(8,128)S(1)}, f32[24,128]{1,0:T(8,128)S(1)}, u32[]{:S(2)}, u32[]{:S(2)}) collective-permute-start(f32[24,128]{1,0:T(8,128)S(1)} %share.2), channel_id=1, source_target_pairs={{0,8},{8,0},{1,9},{9,1},{2,10},{10,2},{3,11},{11,3},{4,12},{12,4},... | collective-permute-start | bytes 36872 | tf_op jit(solution)/shard_map/ppermute | solution.py:592
  66.7 8.6 %copy-start.4 = (f32[2,3,128,128]{3,2,1,0:T(8,128)}, f32[2,3,128,128]{3,2,1,0:T(8,128)S(1)}, u32[]{:S(2)}) copy-start(f32[2,3,128,128]{3,2,1,0:T(8,128)S(1)} %collective-permute-done.11.refs_5_.refs_7_) | copy-start | bytes 1179652
  67.6 18.0 %all-to-all-start.1 = ((f32[32,24,128]{2,1,0:T(8,128)}), f32[32,24,128]{2,1,0:T(8,128)S(1)}, u32[]{:S(2)}, u32[]{:S(2)}) async-start(f32[32,24,128]{2,1,0:T(8,128)} %bitcast.12), calls=%async_computation.1 | async-start | bytes 786432 | tf_op jit(solution)/shard_map/all_to_all | solution.py:681
  78.4 14.5 %collective-permute-start.12 = (f32[2,384,128]{2,1,0:T(8,128)}, f32[2,384,128]{2,1,0:T(8,128)S(1)}, u32[]{:S(2)}, u32[]{:S(2)}) collective-permute-start(f32[2,384,128]{2,1,0:T(8,128)} %get-tuple-element.87), channel_id=1, source_target_pairs={{0,1},{1,0},{2,3},{3,2},{4,5},{5,4},{6,7},{7,6},{8,9},{9,8},{10,11... | collective-permute-start | bytes 1179656 | tf_op jit(solution)/shard_map/ppermute | solution.py:587
  79.7 13.1 %collective-permute-start.13 = (f32[2,384,128]{2,1,0:T(8,128)}, f32[2,384,128]{2,1,0:T(8,128)S(1)}, u32[]{:S(2)}, u32[]{:S(2)}) collective-permute-start(f32[2,384,128]{2,1,0:T(8,128)} %get-tuple-element.88), channel_id=1, source_target_pairs={{1,2},{3,4},{5,6},{7,8},{9,10},{11,12},{13,14},{2,1},{4,3},{6,5},{... | collective-permute-start | bytes 1179656 | tf_op jit(solution)/shard_map/ppermute | solution.py:587
  85.6 7.9 %collective-permute-start.14 = (f32[768,128]{1,0:T(8,128)S(1)}, f32[768,128]{1,0:T(8,128)S(1)}, u32[]{:S(2)}, u32[]{:S(2)}) collective-permute-start(f32[768,128]{1,0:T(8,128)S(1)} %bitcast.21), channel_id=1, source_target_pairs={{0,16},{16,0},{1,17},{17,1},{2,18},{18,2},{3,19},{19,3},{4,20},{20... | collective-permute-start | bytes 1179656 | tf_op jit(solution)/shard_map/ppermute | solution.py:592
  92.8 0.8 copy-start.5
  92.8 0.9 copy-start.6
  106.3 13.2 %copy-start.12 = (f32[2,3,64,128]{3,2,1,0:T(8,128)S(1)}, f32[2,3,64,128]{3,2,1,0:T(8,128)}, u32[]{:S(2)}) copy-start(f32[2,3,64,128]{3,2,1,0:T(8,128)} %get-tuple-element.101) | copy-start | bytes 589828
  106.3 13.9 %copy-start.11 = (f32[2,3,64,128]{3,2,1,0:T(8,128)S(1)}, f32[2,3,64,128]{3,2,1,0:T(8,128)}, u32[]{:S(2)}) copy-start(f32[2,3,64,128]{3,2,1,0:T(8,128)} %get-tuple-element.102) | copy-start | bytes 589828
  106.3 3.8 %collective-permute-start.15 = (f32[768,128]{1,0:T(8,128)S(1)}, f32[768,128]{1,0:T(8,128)S(1)}, u32[]{:S(2)}, u32[]{:S(2)}) collective-permute-start(f32[768,128]{1,0:T(8,128)S(1)} %get-tuple-element.96), channel_id=1, source_target_pairs={{0,16},{16,0},{1,17},{17,1},{2,18},{18,2},{3,19},{19,3},{4,20},{20... | collective-permute-start | bytes 1179656 | tf_op jit(solution)/shard_map/ppermute | solution.py:592
  110.9 20.6 %all-to-all-start.2 = ((f32[32,24,128]{2,1,0:T(8,128)}), f32[32,24,128]{2,1,0:T(8,128)S(1)}, u32[]{:S(2)}, u32[]{:S(2)}) async-start(f32[32,24,128]{2,1,0:T(8,128)} %bitcast.14), calls=%async_computation.2 | async-start | bytes 786432 | tf_op jit(solution)/shard_map/all_to_all | solution.py:670
  119.5 9.0 %collective-permute-start.16 = (f32[2,3,64,128]{3,2,1,0:T(8,128)S(1)}, f32[2,3,64,128]{3,2,1,0:T(8,128)S(1)}, u32[]{:S(2)}, u32[]{:S(2)}) collective-permute-start(f32[2,3,64,128]{3,2,1,0:T(8,128)S(1)} %copy-done.12), channel_id=1, source_target_pairs={{0,16},{16,0},{32,48},{48,32},{64,80},{80,64},{96,112},{112,96},{1... | collective-permute-start | bytes 589832 | tf_op jit(solution)/shard_map/ppermute | solution.py:587
  120.2 10.4 %collective-permute-start.17 = (f32[2,3,64,128]{3,2,1,0:T(8,128)S(1)}, f32[2,3,64,128]{3,2,1,0:T(8,128)S(1)}, u32[]{:S(2)}, u32[]{:S(2)}) collective-permute-start(f32[2,3,64,128]{3,2,1,0:T(8,128)S(1)} %copy-done.11), channel_id=1, source_target_pairs={{16,32},{48,64},{80,96},{112,128},{144,160},{176,192},{208,224},{3... | collective-permute-start | bytes 589832 | tf_op jit(solution)/shard_map/ppermute | solution.py:587
  128.4 18.8 %copy-start.7 = (f32[2,3,64,128]{3,2,1,0:T(8,128)}, f32[2,3,64,128]{3,2,1,0:T(8,128)S(1)}, u32[]{:S(2)}) copy-start(f32[2,3,64,128]{3,2,1,0:T(8,128)S(1)} %collective-permute-done.16.refs_2_) | copy-start | bytes 589828
  130.6 16.6 %copy-start.8 = (f32[2,3,64,128]{3,2,1,0:T(8,128)}, f32[2,3,64,128]{3,2,1,0:T(8,128)S(1)}, u32[]{:S(2)}) copy-start(f32[2,3,64,128]{3,2,1,0:T(8,128)S(1)} %collective-permute-done.17.refs_3_) | copy-start | bytes 589828
  131.5 3.8 %collective-permute-start.20 = (f32[24,128]{1,0:T(8,128)S(1)}, f32[24,128]{1,0:T(8,128)S(1)}, u32[]{:S(2)}, u32[]{:S(2)}) collective-permute-start(f32[24,128]{1,0:T(8,128)S(1)} %share.3), channel_id=1, source_target_pairs={{0,40},{8,32},{32,8},{40,0},{1,41},{9,33},{33,9},{41,1},{2,42},{10... | collective-permute-start | bytes 36872 | tf_op jit(solution)/shard_map/ppermute | solution.py:592
  133.2 4.1 %collective-permute-start.19 = (f32[24,128]{1,0:T(8,128)S(1)}, f32[24,128]{1,0:T(8,128)S(1)}, u32[]{:S(2)}, u32[]{:S(2)}) collective-permute-start(f32[24,128]{1,0:T(8,128)S(1)} %share.3), channel_id=1, source_target_pairs={{0,32},{32,0},{1,33},{33,1},{2,34},{34,2},{3,35},{35,3},{4,36},{36... | collective-permute-start | bytes 36872 | tf_op jit(solution)/shard_map/ppermute | solution.py:592
  134.3 3.0 %collective-permute-start.18 = (f32[24,128]{1,0:T(8,128)S(1)}, f32[24,128]{1,0:T(8,128)S(1)}, u32[]{:S(2)}, u32[]{:S(2)}) collective-permute-start(f32[24,128]{1,0:T(8,128)S(1)} %share.3), channel_id=1, source_target_pairs={{0,8},{8,0},{1,9},{9,1},{2,10},{10,2},{3,11},{11,3},{4,12},{12,4},... | collective-permute-start | bytes 36872 | tf_op jit(solution)/shard_map/ppermute | solution.py:592
  138.1 20.8 %all-to-all-start.3 = ((f32[32,24,128]{2,1,0:T(8,128)}), f32[32,24,128]{2,1,0:T(8,128)S(1)}, u32[]{:S(2)}, u32[]{:S(2)}) async-start(f32[32,24,128]{2,1,0:T(8,128)} %bitcast.17), calls=%async_computation.3 | async-start | bytes 786432 | tf_op jit(solution)/shard_map/all_to_all | solution.py:681
  150.1 8.7 %collective-permute-start.21 = (f32[256,128]{1,0:T(8,128)}, f32[256,128]{1,0:T(8,128)S(1)}, u32[]{:S(2)}, u32[]{:S(2)}) collective-permute-start(f32[256,128]{1,0:T(8,128)} %get-tuple-element.112), channel_id=1, source_target_pairs={{0,1},{1,0},{2,3},{3,2},{4,5},{5,4},{6,7},{7,6},{8,9},{9,8},{10,11... | collective-permute-start | bytes 393224 | tf_op jit(solution)/shard_map/ppermute | solution.py:587
  151.5 7.4 %collective-permute-start.22 = (f32[256,128]{1,0:T(8,128)}, f32[256,128]{1,0:T(8,128)S(1)}, u32[]{:S(2)}, u32[]{:S(2)}) collective-permute-start(f32[256,128]{1,0:T(8,128)} %get-tuple-element.113), channel_id=1, source_target_pairs={{1,2},{3,4},{5,6},{7,8},{9,10},{11,12},{13,14},{2,1},{4,3},{6,5},{... | collective-permute-start | bytes 393224 | tf_op jit(solution)/shard_map/ppermute | solution.py:587
  158.9 6.1 %copy-start.9 = (f32[256,128]{1,0:T(8,128)}, f32[256,128]{1,0:T(8,128)S(1)}, u32[]{:S(2)}) copy-start(f32[256,128]{1,0:T(8,128)S(1)} %collective-permute-done.21.refs_3_) | copy-start | bytes 393220
  158.9 6.1 %copy-start.10 = (f32[256,128]{1,0:T(8,128)}, f32[256,128]{1,0:T(8,128)S(1)}, u32[]{:S(2)}) copy-start(f32[256,128]{1,0:T(8,128)S(1)} %collective-permute-done.22.refs_4_) | copy-start | bytes 393220
  158.9 6.1 %collective-permute-start.23 = (f32[768,128]{1,0:T(8,128)S(1)}, f32[768,128]{1,0:T(8,128)S(1)}, u32[]{:S(2)}, u32[]{:S(2)}) collective-permute-start(f32[768,128]{1,0:T(8,128)S(1)} %bitcast.23), channel_id=1, source_target_pairs={{0,16},{16,0},{1,17},{17,1},{2,18},{18,2},{3,19},{19,3},{4,20},{20... | collective-permute-start | bytes 1179656 | tf_op jit(solution)/shard_map/ppermute | solution.py:592
